TPU v7x, 32 devices: a whole 2x2x4 slice. The times are simulated.
32 devices in a mesh: row: 2 (over x), col: 4 (over z), rep: 4 (over y, core).
Axes of the slice: x: 2, y: 2, z: 4, core: 2. Of those that a mesh axis runs over, the one named last changes fastest.
Arguments:
- features: float32 [16384, 256], P(('row', 'col', 'rep')), may hold values from -6 to 6
- self_weight: float32 [256, 256], replicated, may hold values from -0.375 to 0.375
- neigh_weight: float32 [256, 256], replicated, may hold values from -1.2 to 1.2
- block_source: int32 [256, 8], P(('row', 'col', 'rep')), may hold values from 0 to 95, as said below
- edge_weights: int32 [256, 8, 64, 64], P(('row', 'col', 'rep')), may hold values from 0 to 15, as said below
- labels: int32 [16384], P(('row', 'col', 'rep')), may hold values from 0 to 255
Outputs:
- grad_self: float32 [256, 256], replicated
- grad_neigh: float32 [256, 256], replicated
- grad_features: float32 [16384, 256], P(('row', 'col', 'rep'))
Inputs may be any that keep to these rules, and one draw needn't show every extreme that they name: `block_source`: slot 0 of every block row names the row's own block. `edge_weights`: in each block row the filled slots come first, with entries 1 to 15; later slots are all zero. Every block row has 1 to 8 filled slots, and some block row has all 8.
All inputs are finite; a program needn't handle non-finite values.
Results may differ from a plain program's by a relative error of at most 0.0035.
Values may be sent and summed in bfloat16 or wider, within the bound.
No kernel may reach another device: no remote copies, remote signals or barrier semaphores. Data moves between devices by JAX's collectives and lax.ppermute only.
A program may use at most 64 MiB of HBM per device.

v0:
```python
import jax
import jax.numpy as jnp
from jax import lax
from jax.sharding import PartitionSpec as P

BLOCK = 64


def extended(value, sides, width):
    for axis, dim in sides:
        devices, length = (lax.axis_size(axis), value.shape[dim])
        up = [(i, (i + 1) % devices) for i in range(devices)]
        down = [(j, i) for i, j in up]
        last = lax.slice_in_dim(value, length - width, length, axis=dim)
        first = lax.slice_in_dim(value, 0, width, axis=dim)
        before = lax.ppermute(last, axis, up)
        after = lax.ppermute(first, axis, down)
        value = jnp.concatenate([before, value, after], axis=dim)
    return value


def on_device(features, self_weight, neigh_weight, block_source, edge_weights, labels):
    high = lax.Precision.HIGHEST
    row_count, width_in = features.shape
    block_count = row_count // BLOCK
    lowered = features.astype(jnp.bfloat16)
    gathered_group = lax.all_gather(lowered, "rep", axis=0, tiled=True)
    neighbours = extended(gathered_group[None], (("col", 0),), 1)
    group_blocks = neighbours.shape[1] // BLOCK
    table = neighbours.reshape(3 * group_blocks, BLOCK, width_in)
    source_peer = block_source // group_blocks
    inner_block = block_source % group_blocks
    table_index = jnp.where(
        source_peer == 0,
        group_blocks + inner_block,
        jnp.where(source_peer == 1, inner_block, block_source),
    )
    weights_low = edge_weights.astype(jnp.bfloat16)
    degree = jnp.sum(edge_weights, axis=(1, 3)).astype(jnp.float32)[..., None]
    aggregated = jnp.einsum(
        "bsij,bsjf->bif", weights_low, table[table_index], preferred_element_type=jnp.float32
    )
    neighbour_mean = (aggregated / degree).reshape(row_count, width_in)
    logits = jnp.dot(features, self_weight, precision=high) + jnp.dot(
        neighbour_mean, neigh_weight, precision=high
    )
    class_total = self_weight.shape[1]
    target = (labels[:, None] == jnp.arange(class_total, dtype=jnp.int32)[None, :]).astype(
        jnp.float32
    )
    residual = jax.nn.sigmoid(logits) - target
    contract_rows = (((0,), (0,)), ((), ()))
    self_part = lax.dot_general(features, residual, contract_rows, precision=high)
    neigh_part = lax.dot_general(neighbour_mean, residual, contract_rows, precision=high)
    grad_self, grad_neigh = lax.psum((self_part, neigh_part), ("row", "col", "rep"))
    spread = (
        jnp.dot(residual, neigh_weight.T, precision=high).reshape(block_count, BLOCK, width_in)
        / degree
    ).astype(jnp.bfloat16)
    empty_terms = jnp.zeros((3 * group_blocks, BLOCK, width_in), jnp.float32)
    contrib = jnp.einsum("bsij,bif->bsjf", weights_low, spread, preferred_element_type=jnp.float32)
    partial_sum = empty_terms.at[table_index.reshape(-1)].add(contrib.reshape(-1, BLOCK, width_in))
    terms = partial_sum.astype(jnp.bfloat16).reshape(3, group_blocks * BLOCK, width_in)
    outgoing = terms[0::2]
    incoming = extended(outgoing, (("col", 0),), 1)
    region_terms = (
        terms[1].astype(jnp.float32)
        + incoming[0].astype(jnp.float32)
        + incoming[3].astype(jnp.float32)
    )
    own_terms = lax.psum_scatter(region_terms, "rep", scatter_dimension=0, tiled=True)
    grad_features = jnp.dot(residual, self_weight.T, precision=high) + own_terms
    return (grad_self, grad_neigh, grad_features)


def solution(mesh):
    return jax.shard_map(
        on_device,
        mesh=mesh,
        in_specs=(
            P(("row", "col", "rep"), None),
            P(),
            P(),
            P(("row", "col", "rep"), None),
            P(("row", "col", "rep"), None, None, None),
            P(("row", "col", "rep")),
        ),
        out_specs=(P(), P(), P(("row", "col", "rep"), None)),
        check_vma=False,
    )
```

profile of v0, /device:TPU:0, one launch (start us, length us, event | category | flops | bytes accessed | tf_op | source)
XLA Modules:
  0.0 298.9 jit_solution(13114687228330361843)
XLA Ops:
  7.2 1.8 convert_element_type.40
  9.2 20.5 %all-gather.2.cloned.1.call-done = bf16[2048,256]{1,0:T(8,128)(2,1)} async-done(((bf16[512,256]{1,0:T(8,128)(2,1)}), bf16[2048,256]{1,0:T(8,128)(2,1)}) %all-gather.2.cloned.1.call-update) | async-done | bytes 1048592 | tf_op jit(solution)/shard_map/all_gather | solution.py:27
  29.6 3.3 %collective-permute-start.1 = (bf16[1,2048,256]{2,1,0:T(8,128)(2,1)}, bf16[1,2048,256]{2,1,0:T(8,128)(2,1)S(1)}, u32[]{:S(2)}, u32[]{:S(2)}) collective-permute-start(bf16[1,2048,256]{2,1,0:T(8,128)(2,1)} %bitcast.55), channel_id=1, source_target_pairs={{4,0},{8,4},{12,8},{0,12},{5,1},{9,5},{13,9},{1,13},{6,2},{10,6},{... | collective-permute-start | bytes 3145736 | tf_op jit(solution)/shard_map/ppermute | solution.py:17
  33.8 2.7 fusion.11
  39.3 17.6 %collective-permute-done.1 = bf16[1,2048,256]{2,1,0:T(8,128)(2,1)S(1)} collective-permute-done((bf16[1,2048,256]{2,1,0:T(8,128)(2,1)}, bf16[1,2048,256]{2,1,0:T(8,128)(2,1)S(1)}, u32[]{:S(2)}, u32[]{:S(2)}) %collective-permute-start.1) | collective-permute-done | bytes 1048608 | tf_op jit(solution)/shard_map/ppermute | solution.py:17
  57.8 21.7 %collective-permute-done = bf16[1,2048,256]{2,1,0:T(8,128)(2,1)} collective-permute-done((bf16[1,2048,256]{2,1,0:T(8,128)(2,1)}, bf16[1,2048,256]{2,1,0:T(8,128)(2,1)}, u32[]{:S(2)}, u32[]{:S(2)}) %collective-permute-start) | collective-permute-done | bytes 1048608 | tf_op jit(solution)/shard_map/ppermute | solution.py:16
  79.6 2.2 pad_maximum_fusion
  81.8 2.0 gather_fusion
  83.8 2.5 fusion.5
  87.6 2.8 fusion.6
  90.4 3.4 %broadcast_in_dim.15 = f32[96,64,256]{2,1,0:T(8,128)} broadcast(f32[]{:T(128)} %constant.39.clone.1), dimensions={} | broadcast | bytes 6291460 | tf_op jit(solution)/shard_map/broadcast_in_dim | solution.py:60
  93.8 13.6 %scatter_fusion = f32[96,64,256]{2,1,0:T(8,128)} fusion(f32[96,64,256]{2,1,0:T(8,128)} %broadcast_in_dim.15, s32[64]{0:T(128)S(1)} %fusion.9, f32[64,64,256]{2,1,0:T(8,128)} %bitcast.49), kind=kCustom, calls=%fused_computation.1 | custom fusion | flops 1048576 | bytes 12583168 | tf_op jit(solution)/shard_map/scatter-add | solution.py:62
  107.4 3.3 %convert_element_type.45 = bf16[96,64,256]{2,1,0:T(8,128)(2,1)S(1)} convert(f32[96,64,256]{2,1,0:T(8,128)} %scatter_fusion) | non-fusion elementwise | flops 1572864 | bytes 9437184 | tf_op jit(solution)/shard_map/convert_element_type | solution.py:63
  112.3 1.7 collective-permute-start.2
  114.0 2.2 collective-permute-start.3
  116.2 1.7 fusion.13
  117.9 1.7 convolution_bitcast_fusion.1
  119.7 22.1 %collective-permute-done.2 = bf16[1,2048,256]{2,1,0:T(8,128)(2,1)S(1)} collective-permute-done((bf16[1,2048,256]{2,1,0:T(8,128)(2,1)}, bf16[1,2048,256]{2,1,0:T(8,128)(2,1)S(1)}, u32[]{:S(2)}, u32[]{:S(2)}) %collective-permute-start.2) | collective-permute-done | bytes 1048608 | tf_op jit(solution)/shard_map/ppermute | solution.py:16
  141.8 21.6 %collective-permute-done.3 = bf16[1,2048,256]{2,1,0:T(8,128)(2,1)} collective-permute-done((bf16[1,2048,256]{2,1,0:T(8,128)(2,1)}, bf16[1,2048,256]{2,1,0:T(8,128)(2,1)}, u32[]{:S(2)}, u32[]{:S(2)}) %collective-permute-start.3) | collective-permute-done | bytes 1048608 | tf_op jit(solution)/shard_map/ppermute | solution.py:17
  163.4 2.9 convert_add_fusion
  167.0 88.7 %all-reduce.3.cloned.1.call-done = (f32[256,256]{0,1:T(8,128)}, f32[256,256]{1,0:T(8,128)}) async-done(((f32[256,256]{0,1:T(8,128)}, f32[256,256]{1,0:T(8,128)}), (f32[256,256]{0,1:T(8,128)}, f32[256,256]{1,0:T(8,128)})) %all-reduce.3.cloned.1.call-update) | async-done | bytes 524304 | tf_op jit(solution)/shard_map/psum | solution.py:55
  255.7 1.8 copy.10
  257.5 31.3 %reduce-scatter.2.cloned.1.call-done = f32[512,256]{1,0:T(8,128)} async-done(((f32[2048,256]{1,0:T(8,128)}), f32[512,256]{1,0:T(8,128)}) %reduce-scatter.2.cloned.1.call-update) | async-done | bytes 524304 | tf_op jit(solution)/shard_map/reduce_scatter | solution.py:71
  288.8 1.9 add.63
  (42 shorter events, 10.0 us)
Async XLA Ops:
  7.2 79.1 %copy-start = (f32[256,256]{1,0:T(8,128)S(1)}, f32[256,256]{1,0:T(8,128)}, u32[]{:S(2)}) copy-start(f32[256,256]{1,0:T(8,128)} %param.8) | copy-start | bytes 786436
  7.2 30.7 %copy-start.1 = (f32[512,256]{1,0:T(8,128)S(1)}, f32[512,256]{1,0:T(8,128)}, u32[]{:S(2)}) copy-start(f32[512,256]{1,0:T(8,128)} %param.6) | copy-start | bytes 1572868
  7.2 30.7 %copy-start.5 = (f32[256,256]{1,0:T(8,128)S(1)}, f32[256,256]{1,0:T(8,128)}, u32[]{:S(2)}) copy-start(f32[256,256]{1,0:T(8,128)} %param.7) | copy-start | bytes 786436
  7.2 22.4 %all-gather.2.cloned.1.call-start = ((), (), s32[]{:S(2)}) async-start(), calls=%async_computation.1 | async-start | bytes 1310720 | tf_op jit(solution)/shard_map/all_gather | solution.py:27
  9.1 246.6 %all-reduce.3.cloned.1.call-start = ((), (), s32[]{:S(2)}) async-start(), calls=%async_computation.3 | async-start | bytes 1048576 | tf_op jit(solution)/shard_map/psum | solution.py:55
  29.6 27.2 %collective-permute-start.1 = (bf16[1,2048,256]{2,1,0:T(8,128)(2,1)}, bf16[1,2048,256]{2,1,0:T(8,128)(2,1)S(1)}, u32[]{:S(2)}, u32[]{:S(2)}) collective-permute-start(bf16[1,2048,256]{2,1,0:T(8,128)(2,1)} %bitcast.55), channel_id=1, source_target_pairs={{4,0},{8,4},{12,8},{0,12},{5,1},{9,5},{13,9},{1,13},{6,2},{10,6},{... | collective-permute-start | bytes 3145736 | tf_op jit(solution)/shard_map/ppermute | solution.py:17
  33.0 46.6 %collective-permute-start = (bf16[1,2048,256]{2,1,0:T(8,128)(2,1)}, bf16[1,2048,256]{2,1,0:T(8,128)(2,1)}, u32[]{:S(2)}, u32[]{:S(2)}) collective-permute-start(bf16[1,2048,256]{2,1,0:T(8,128)(2,1)} %bitcast.56), channel_id=1, source_target_pairs={{0,4},{4,8},{8,12},{12,0},{1,5},{5,9},{9,13},{13,1},{2,6},{6,10},{... | collective-permute-start | bytes 3145736 | tf_op jit(solution)/shard_map/ppermute | solution.py:16
  36.5 20.3 %copy-start.4 = (bf16[8,8,64,64]{3,2,1,0:T(8,128)(2,1)}, bf16[8,8,64,64]{3,2,1,0:T(8,128)(2,1)S(1)}, u32[]{:S(2)}) copy-start(bf16[8,8,64,64]{3,2,1,0:T(8,128)(2,1)S(1)} %get-tuple-element.13) | copy-start | bytes 1572868
  56.8 1.0 copy-start.7
  83.8 2.5 copy-start.8
  83.8 2.5 copy-start.9
  86.2 1.3 copy-start.3
  110.8 7.1 %copy-start.2 = (f32[512,256]{1,0:T(8,128)S(1)}, f32[512,256]{1,0:T(8,128)}, u32[]{:S(2)}) copy-start(f32[512,256]{1,0:T(8,128)} %param.6) | copy-start | bytes 1572868
  112.3 29.5 %collective-permute-start.2 = (bf16[1,2048,256]{2,1,0:T(8,128)(2,1)}, bf16[1,2048,256]{2,1,0:T(8,128)(2,1)S(1)}, u32[]{:S(2)}, u32[]{:S(2)}) collective-permute-start(bf16[1,2048,256]{2,1,0:T(8,128)(2,1)} %get-tuple-element.10), channel_id=1, source_target_pairs={{0,4},{4,8},{8,12},{12,0},{1,5},{5,9},{9,13},{13,1},{2,6},{6,10},{... | collective-permute-start | bytes 3145736 | tf_op jit(solution)/shard_map/ppermute | solution.py:16
  114.0 49.5 %collective-permute-start.3 = (bf16[1,2048,256]{2,1,0:T(8,128)(2,1)}, bf16[1,2048,256]{2,1,0:T(8,128)(2,1)}, u32[]{:S(2)}, u32[]{:S(2)}) collective-permute-start(bf16[1,2048,256]{2,1,0:T(8,128)(2,1)} %get-tuple-element.11), channel_id=1, source_target_pairs={{4,0},{8,4},{12,8},{0,12},{5,1},{9,5},{13,9},{1,13},{6,2},{10,6},{... | collective-permute-start | bytes 3145736 | tf_op jit(solution)/shard_map/ppermute | solution.py:17
  119.6 46.7 %copy-start.6 = (f32[256,256]{1,0:T(8,128)S(1)}, f32[256,256]{1,0:T(8,128)}, u32[]{:S(2)}) copy-start(f32[256,256]{1,0:T(8,128)} %param.7) | copy-start | bytes 786436
  119.6 169.2 %reduce-scatter.2.cloned.1.call-start = ((), (), s32[]{:S(2)}) async-start(), calls=%async_computation.2 | async-start | bytes 2621440 | tf_op jit(solution)/shard_map/reduce_scatter | solution.py:71
Sparse Core Ops, SparseCore 0:
  10.2 19.4 all-gather.1
  119.8 135.8 all-reduce.2
  258.4 30.3 reduce-scatter.1
where the time goes:
time: 299 us
  waiting for transfers between devices  224 us (75%)
  other arithmetic  29.1 us (10%)
  between operations  13.9 us (5%)
  local copies, waits for them, and re-layouts  13.1 us (4%)
  matrix products  11.9 us (4%)
  starting transfers between devices  7.28 us (2%)
    psum x1, waiting for transfers between devices, on_device(): lax.psum((self_part, neigh_part), ('row', 'col', 'rep'))  88.7 us
    ppermute x2, waiting for transfers between devices, extended(): before = lax.ppermute(last, axis, up)  43.8 us
    ppermute x2, waiting for transfers between devices, extended(): after = lax.ppermute(first, axis, down)  39.2 us
    reduce_scatter x1, waiting for transfers between devices, on_device(): lax.psum_scatter(region_terms, 'rep', scatter_dimension=0, tiled=True)  31.3 us
    all_gather x1, waiting for transfers between devices, on_device(): gathered_group = lax.all_gather(lowered, 'rep', axis=0, tiled=True)  20.5 us
    scatter-add x1, other arithmetic, on_device(): empty_terms.at[table_index.reshape(-1)]  13.6 us
  transfers between devices with their start and end apart: 7, of which 7 were waited for; matrix products, arithmetic and copies ran while one was open for 5% of the time, Pallas kernels for 0%

commit v1 on v0

v1 whole, which is shorter than its diff:
```python
import functools

import jax
import jax.numpy as jnp
from jax import lax
from jax.experimental import pallas as pl
from jax.experimental.pallas import tpu as pltpu
from jax.sharding import PartitionSpec as P

BLOCK = 64
F32 = jnp.float32
BF16 = jnp.bfloat16
HIGH = lax.Precision.HIGHEST
VMEM = pl.BlockSpec(memory_space=pltpu.VMEM)
SMEM = pl.BlockSpec(memory_space=pltpu.SMEM)
ANY = pl.BlockSpec(memory_space=pl.ANY)


def shape(dims, dtype):
    return jax.ShapeDtypeStruct(dims, dtype)


def call(body, out_shape, operands, in_specs, out_specs, scratch=(), flops=0):
    moved = sum(x.size * x.dtype.itemsize for x in list(operands) + list(out_shape))
    return pl.pallas_call(
        body,
        out_shape=out_shape,
        in_specs=in_specs,
        out_specs=out_specs,
        scratch_shapes=scratch,
        compiler_params=pltpu.CompilerParams(vmem_limit_bytes=40 << 20),
        cost_estimate=pl.CostEstimate(flops=flops, bytes_accessed=moved, transcendentals=0),
    )(*operands)


def dot(a, b, contract=((1,), (0,)), precision=HIGH):
    return lax.dot_general(a, b, (contract, ((), ())), precision=precision, preferred_element_type=F32)


def prepare_body(edge_ref, feat_ref, self_ref, wide_ref, tall_ref, inverse_ref, logit_ref):
    blocks, slots = edge_ref.shape[:2]

    @pl.loop(0, blocks)
    def _(b):
        wide = jnp.concatenate([edge_ref[b, s].astype(F32) for s in range(slots)], axis=1)
        wide_ref[b] = wide.astype(BF16)
        tall_ref[b] = wide.T.astype(BF16)
        degree = jnp.sum(wide, axis=1, keepdims=True)
        inverse_ref[b] = jnp.broadcast_to(1.0 / degree, inverse_ref.shape[1:])

    logit_ref[...] = dot(feat_ref[...], self_ref[...])


def forward_body(*refs):
    pieces, refs = refs[:12], refs[12:]
    index_ref, wide_ref, inverse_ref, logit_ref, label_ref, feat_ref, neigh_ref = refs[:7]
    residual_ref, spread_ref, self_part_ref, neigh_part_ref, table, mean, sems = refs[7:]
    per = pieces[0].shape[0]
    copies = [
        pltpu.make_async_copy(piece, table.at[pl.ds(i * per, per)], sems.at[i])
        for i, piece in enumerate(pieces)
    ]
    for c in copies:
        c.start()
    for c in copies:
        c.wait()
    blocks, rows, wide_cols = wide_ref.shape
    slots = wide_cols // BLOCK
    width = mean.shape[1]

    @pl.loop(0, blocks)
    def _(b):
        gathered = jnp.concatenate([table[index_ref[b, s]] for s in range(slots)], axis=0)
        total = dot(wide_ref[b], gathered, precision=None)
        scale = jnp.concatenate([inverse_ref[b]] * (width // 128), axis=1)
        mean[pl.ds(pl.multiple_of(b * rows, rows), rows)] = total * scale

    logits = logit_ref[...] + dot(mean[...], neigh_ref[...])
    classes = lax.broadcasted_iota(jnp.int32, logits.shape, 1)
    target = jnp.where(classes == label_ref[...], 1.0, 0.0)
    residual = 1.0 / (1.0 + jnp.exp(-logits)) - target
    residual_ref[...] = residual
    spread = dot(residual, neigh_ref[...], ((1,), (1,)))
    inverse = inverse_ref[...].reshape(blocks * rows, 128)
    scale = jnp.concatenate([inverse] * (width // 128), axis=1)
    spread_ref[...] = (spread * scale).astype(BF16).reshape(spread_ref.shape)
    self_part_ref[...] = dot(feat_ref[...], residual, ((0,), (0,)))
    neigh_part_ref[...] = dot(mean[...], residual, ((0,), (0,)))


def backward_body(index_ref, spread_ref, tall_ref, send_ref, keep_ref, terms):
    blocks, tall_rows, _ = tall_ref.shape
    slots = tall_rows // BLOCK
    per = send_ref.shape[1]
    terms[...] = jnp.zeros_like(terms)

    @pl.loop(0, blocks)
    def _(b):
        contrib = dot(tall_ref[b], spread_ref[b], precision=None)
        for s in range(slots):
            at = index_ref[b, s]
            terms[at] = terms[at] + contrib[s * BLOCK : (s + 1) * BLOCK]

    for out_ref, core in ((keep_ref, 0), (send_ref, 1)):
        place = 0
        for rel in (2 + core, core):
            for region in (1, 2, 0):
                out_ref[place] = terms[pl.ds((region * 4 + rel) * per, per)].astype(BF16)
                place += 1


def chunk_body(groups, place_ref, mine_ref, got_ref, *outs):
    rows = mine_ref.shape[0] // groups
    for d, out in enumerate(outs):
        at = pl.ds(pl.multiple_of((place_ref[0] ^ d) * rows, rows), rows)
        out[...] = mine_ref[at] + got_ref[at]


def assemble_body(groups, place_ref, *refs):
    out = refs[-1]
    rows = out.shape[0] // groups
    for d, chunk in enumerate(refs[:-1]):
        at = pl.ds(pl.multiple_of((place_ref[0] ^ d) * rows, rows), rows)
        out[at] = chunk[...]


def tree_sum(values):
    values = list(values)
    while len(values) > 1:
        values = [a + b for a, b in zip(values[0::2], values[1::2])]
    return values[0]


def on_device(features, self_weight, neigh_weight, block_source, edge_weights, labels):
    rows, width = features.shape
    blocks, slots = block_source.shape
    classes = self_weight.shape[1]
    cols, reps, lines = lax.axis_size("col"), lax.axis_size("rep"), lax.axis_size("row")
    assert reps == 4
    me = lax.axis_index("rep")

    def core_swap(x):
        return lax.ppermute(x, "rep", [(i, i ^ 1) for i in range(reps)])

    def half_swap(x):
        return lax.ppermute(x, "rep", [(i, i ^ 2) for i in range(reps)])

    def up(x):
        return lax.ppermute(x, "col", [(i, (i + 1) % cols) for i in range(cols)])

    def down(x):
        return lax.ppermute(x, "col", [((i + 1) % cols, i) for i in range(cols)])

    own = features.astype(BF16).reshape(blocks, BLOCK, width)
    half, lower, upper, core = half_swap(own), up(own), down(own), core_swap(own)
    lower_half, upper_half = half_swap(lower), half_swap(upper)
    pieces = [
        own, core, half, core_swap(half),
        lower, core_swap(lower), lower_half, core_swap(lower_half),
        upper, core_swap(upper), upper_half, core_swap(upper_half),
    ]

    group_blocks = reps * blocks
    region, inner = block_source // group_blocks, block_source % group_blocks
    index = (region * reps + ((inner // blocks) ^ me)) * blocks + inner % blocks

    wide_cols = slots * BLOCK
    wide, tall, inverse, self_logits = call(
        prepare_body,
        (
            shape((blocks, BLOCK, wide_cols), BF16),
            shape((blocks, wide_cols, BLOCK), BF16),
            shape((blocks, BLOCK, 128), F32),
            shape((rows, classes), F32),
        ),
        (edge_weights, features, self_weight),
        [VMEM] * 3,
        [VMEM] * 4,
        flops=12 * rows * width * classes,
    )
    residual, spread, self_part, neigh_part = call(
        forward_body,
        (
            shape((rows, classes), F32),
            shape((blocks, BLOCK, width), BF16),
            shape((width, classes), F32),
            shape((width, classes), F32),
        ),
        (*pieces, index, wide, inverse, self_logits, labels.reshape(rows, 1), features, neigh_weight),
        [ANY] * 12 + [SMEM] + [VMEM] * 6,
        [VMEM] * 4,
        scratch=[
            pltpu.VMEM((12 * blocks, BLOCK, width), BF16),
            pltpu.VMEM((rows, width), F32),
            pltpu.SemaphoreType.DMA((12,)),
        ],
        flops=60 * rows * width * classes,
    )

    first = me % 2 == 0
    kept = jnp.where(first, self_part, neigh_part)
    got = core_swap(jnp.where(first, neigh_part, self_part))

    send, keep = call(
        backward_body,
        (shape((6, blocks, BLOCK, width), BF16), shape((6, blocks, BLOCK, width), BF16)),
        (index, spread, tall),
        [SMEM] + [VMEM] * 2,
        [VMEM] * 2,
        scratch=[pltpu.VMEM((12 * blocks, BLOCK, width), F32)],
        flops=2 * rows * wide_cols * width,
    )
    arrived = core_swap(send)

    groups = lines * reps // 2
    place = (lax.axis_index("row") * (reps // 2) + me // 2).astype(jnp.int32)

    def to_group(x, d):
        pairs = []
        for g in range(groups):
            for c in range(2):
                h = g ^ d
                pairs.append((g * 2 + c, h * 2 + c))
        return lax.ppermute(x, ("row", "rep"), pairs)

    chunk = shape((width // groups, classes), F32)
    chunks = call(
        functools.partial(chunk_body, groups),
        (chunk,) * groups,
        (place.reshape(1), kept, got),
        [SMEM, VMEM, VMEM],
        [VMEM] * groups,
    )
    mine = tree_sum([chunks[0]] + [to_group(chunks[d], d) for d in range(1, groups)])

    def both(a, b):
        return a.astype(F32) + b.astype(F32)

    half_near = half_swap(both(keep[0:2], arrived[0:2]).astype(BF16))
    half_own = half_swap(both(keep[2], arrived[2]).astype(BF16))

    def to_col(x, d):
        return lax.ppermute(x, "col", [(i, i ^ d) for i in range(cols)])

    mine = tree_sum([mine] + [to_col(mine, d) for d in range(1, cols)])

    near = both(keep[3:5], arrived[3:5]) + half_near.astype(F32)
    from_upper = down(near[0].astype(BF16))
    from_lower = up(near[1].astype(BF16))

    parts = [mine] + [to_group(mine, d) for d in range(1, groups)]
    (whole,) = call(
        functools.partial(assemble_body, groups),
        (shape((width, classes), F32),),
        (place.reshape(1), *parts),
        [SMEM] + [VMEM] * groups,
        [VMEM],
    )
    other = core_swap(whole)
    grad_self = jnp.where(first, whole, other)
    grad_neigh = jnp.where(first, other, whole)

    direct = jnp.dot(residual, self_weight.T, precision=HIGH)
    own_terms = both(keep[5], arrived[5]) + half_own.astype(F32)
    own_terms = own_terms + from_upper.astype(F32) + from_lower.astype(F32)
    grad_features = direct + own_terms.reshape(rows, width)
    return grad_self, grad_neigh, grad_features


def solution(mesh):
    split = ("row", "col", "rep")
    return jax.shard_map(
        on_device,
        mesh=mesh,
        in_specs=(P(split, None), P(), P(), P(split, None), P(split, None, None, None), P(split)),
        out_specs=(P(), P(), P(split, None)),
        check_vma=False,
    )
```

time: 299 us -> 102 us (0.34)
  waiting for transfers between devices: 224 us -> 42.7 us
  other arithmetic: 29.1 us -> 6.6 us
  starting transfers between devices: 7.28 us -> 28 us
  between operations: 13.9 us -> 0.9 us
  Pallas kernels: 0 us -> 11.9 us
  matrix products: 11.9 us -> 1.42 us
  local copies, waits for them, and re-layouts: 13.1 us -> 9.36 us
    psum x1 -> x0, waiting for transfers between devices: 88.7 us -> none  [on_device(): lax.psum((self_part, neigh_part), ('row', 'col', 'rep'))]
    ppermute x4 -> x27, waiting for transfers between devices: 83 us -> 42.7 us  [the longest x6 12.6 us: to_group(): return lax.ppermute(x, ('row', 'rep'), pairs)]
    reduce_scatter x1 -> x0, waiting for transfers between devices: 31.3 us -> none  [on_device(): lax.psum_scatter(region_terms, 'rep', scatter_dimension=0, tiled=True)]
    ppermute x4 -> x27, starting transfers between devices: 7.16 us -> 28 us  [the longest x2 8.62 us: down(): return lax.ppermute(x, 'col', [((i + 1) % cols, i) for i in range(cols)])]
    all_gather x1 -> x0, waiting for transfers between devices: 20.5 us -> none  [on_device(): gathered_group = lax.all_gather(lowered, 'rep', axis=0, tiled=True)]
    scatter-add x1 -> x0, other arithmetic: 13.6 us -> none  [on_device(): empty_terms.at[table_index.reshape(-1)]]
    pallas_call x0 -> x5, Pallas kernels: none -> 11.9 us  [call(): pl.pallas_call(body, out_shape=out_shape, in_specs=in_specs, out_specs=ou...]
    dot_general x7 -> x1, matrix products: 9.14 us -> 1.42 us  [on_device(): direct = jnp.dot(residual, self_weight.T, precision=HIGH)]
  transfers between devices with their start and end apart: 7 -> 27, of which waited for: 7 -> 14; matrix products, arithmetic and copies ran while one was open for 5% -> 5% of each run, Pallas kernels for 0% -> 2%
where the time goes in v1:
time: 102 us; the launch traced here: 101 us
  waiting for transfers between devices  42.7 us (42%)
  starting transfers between devices  28 us (27%)
  Pallas kernels  11.9 us (12%)
  local copies, waits for them, and re-layouts  9.36 us (9%)
  other arithmetic  6.6 us (6%)
  matrix products  1.42 us (1%)
    ppermute x6, waiting for transfers between devices, to_group(): return lax.ppermute(x, ('row', 'rep'), pairs)  12.6 us
    pallas_call x5, Pallas kernels, call(): pl.pallas_call(body, out_shape=out_shape, in_specs=in_specs, out_specs=ou...  11.9 us
    ppermute x2, waiting for transfers between devices, up(): return lax.ppermute(x, 'col', [(i, (i + 1) % cols) for i in range(cols)])  9.45 us
    ppermute x2, waiting for transfers between devices, down(): return lax.ppermute(x, 'col', [((i + 1) % cols, i) for i in range(cols)])  8.99 us
    ppermute x2, starting transfers between devices, down(): return lax.ppermute(x, 'col', [((i + 1) % cols, i) for i in range(cols)])  8.62 us
    unnamed x34, local copies, waits for them, and re-layouts  8.46 us
    ppermute x6, starting transfers between devices, to_group(): return lax.ppermute(x, ('row', 'rep'), pairs)  7.12 us
    ppermute x5, starting transfers between devices, half_swap(): return lax.ppermute(x, 'rep', [(i, i ^ 2) for i in range(reps)])  6.13 us
  transfers between devices with their start and end apart: 27, of which 14 were waited for; matrix products, arithmetic and copies ran while one was open for 5% of the time, Pallas kernels for 2%

profile of v1, /device:TPU:0, one launch (start us, length us, event | category | flops | bytes accessed | tf_op | source)
XLA Modules:
  0.0 100.9 jit_solution(1489011321214029768)
XLA Ops:
  1.7 5.1 %collective-permute-start.7 = (bf16[8,64,256]{2,1,0:T(8,128)(2,1)S(1)}, bf16[8,64,256]{2,1,0:T(8,128)(2,1)S(1)}, u32[]{:S(2)}, u32[]{:S(2)}) collective-permute-start(bf16[8,64,256]{2,1,0:T(8,128)(2,1)S(1)} %bitcast.18), channel_id=1, source_target_pairs={{4,0},{8,4},{12,8},{0,12},{5,1},{9,5},{13,9},{1,13},{6,2},{10,6},{... | collective-permute-start | bytes 786440 | tf_op jit(solution)/shard_map/ppermute | solution.py:152
  6.8 1.5 %collective-permute-start.1 = (bf16[8,64,256]{2,1,0:T(8,128)(2,1)S(1)}, bf16[8,64,256]{2,1,0:T(8,128)(2,1)S(1)}, u32[]{:S(2)}, u32[]{:S(2)}) collective-permute-start(bf16[8,64,256]{2,1,0:T(8,128)(2,1)S(1)} %bitcast.20), channel_id=1, source_target_pairs={{0,2},{1,3},{2,0},{3,1},{4,6},{5,7},{6,4},{7,5},{8,10},{9,11},{10,... | collective-permute-start | bytes 786440 | tf_op jit(solution)/shard_map/ppermute | solution.py:146
  8.3 5.2 %collective-permute-done.7.refs_8_ = bf16[8,64,256]{2,1,0:T(8,128)(2,1)S(1)} collective-permute-done((bf16[8,64,256]{2,1,0:T(8,128)(2,1)S(1)}, bf16[8,64,256]{2,1,0:T(8,128)(2,1)S(1)}, u32[]{:S(2)}, u32[]{:S(2)}) %collective-permute-start.7) | collective-permute-done | bytes 262176 | tf_op jit(solution)/shard_map/ppermute | solution.py:152
  13.5 1.5 %collective-permute-start.9 = (bf16[8,64,256]{2,1,0:T(8,128)(2,1)S(1)}, bf16[8,64,256]{2,1,0:T(8,128)(2,1)S(1)}, u32[]{:S(2)}, u32[]{:S(2)}) collective-permute-start(bf16[8,64,256]{2,1,0:T(8,128)(2,1)S(1)} %collective-permute-done.7.refs_8_), channel_id=1, source_target_pairs={{0,2},{1,3},{2,0},{3,1},{4,6},{5,7},{6,4},{7,5},{8,10},{9,11},{10,... | collective-permute-start | bytes 786440 | tf_op jit(solution)/shard_map/ppermute | solution.py:146
  15.0 3.9 %collective-permute-done.3.refs_4_ = bf16[8,64,256]{2,1,0:T(8,128)(2,1)S(1)} collective-permute-done((bf16[8,64,256]{2,1,0:T(8,128)(2,1)S(1)}, bf16[8,64,256]{2,1,0:T(8,128)(2,1)S(1)}, u32[]{:S(2)}, u32[]{:S(2)}) %collective-permute-start.3) | collective-permute-done | bytes 262176 | tf_op jit(solution)/shard_map/ppermute | solution.py:149
  18.9 1.5 %collective-permute-start.5 = (bf16[8,64,256]{2,1,0:T(8,128)(2,1)S(1)}, bf16[8,64,256]{2,1,0:T(8,128)(2,1)S(1)}, u32[]{:S(2)}, u32[]{:S(2)}) collective-permute-start(bf16[8,64,256]{2,1,0:T(8,128)(2,1)S(1)} %collective-permute-done.3.refs_4_), channel_id=1, source_target_pairs={{0,2},{1,3},{2,0},{3,1},{4,6},{5,7},{6,4},{7,5},{8,10},{9,11},{10,... | collective-permute-start | bytes 786440 | tf_op jit(solution)/shard_map/ppermute | solution.py:146
  22.4 3.7 %collective-permute-done.5.refs_6_ = bf16[8,64,256]{2,1,0:T(8,128)(2,1)S(1)} collective-permute-done((bf16[8,64,256]{2,1,0:T(8,128)(2,1)S(1)}, bf16[8,64,256]{2,1,0:T(8,128)(2,1)S(1)}, u32[]{:S(2)}, u32[]{:S(2)}) %collective-permute-start.5) | collective-permute-done | bytes 262176 | tf_op jit(solution)/shard_map/ppermute | solution.py:146
  26.1 1.7 %copy-done = s32[8,8,64,64]{3,2,1,0:T(8,128)S(1)} copy-done((s32[8,8,64,64]{3,2,1,0:T(8,128)S(1)}, s32[8,8,64,64]{3,2,1,0:T(8,128)}, u32[]{:S(2)}) %copy-start) | copy-done | bytes 1048600
  29.8 2.4 %shard_map.85 = (bf16[8,64,512]{2,1,0:T(8,128)(2,1)S(1)}, bf16[8,512,64]{2,1,0:T(8,128)(2,1)S(1)}, f32[8,64,128]{2,1,0:T(8,128)S(1)}, f32[512,256]{1,0:T(8,128)S(1)}) custom-call(s32[8,8,64,64]{3,2,1,0:T(8,128)S(1)} %copy-done, f32[512,256]{1,0:T(8,128)S(1)} %copy-done.1, f32[256,256]{1,0:T(8,128)S(1)} %copy-done.3), custom_call_target="tpu_custom_call" | custom-call | flops 402653184 | bytes 3670016 | tf_op jit(solution)/shard_map/pallas_call | solution.py:25
  37.1 5.1 %shard_map.86 = (f32[512,256]{1,0:T(8,128)S(1)}, bf16[8,64,256]{2,1,0:T(8,128)(2,1)S(1)}, f32[256,256]{1,0:T(8,128)S(1)}, f32[256,256]{1,0:T(8,128)S(1)}) custom-call(bf16[8,64,256]{2,1,0:T(8,128)(2,1)S(1)} %bitcast.22, bf16[8,64,256]{2,1,0:T(8,128)(2,1)S(1)} %copy-done.11, bf16[8,64,256]{2,1,0:T(8,128)(2,1)S(1)} %copy-done.9, ...), custom_call_target="tpu_custom_call" | custom-call | flops 2013265920 | bytes 6555904 | tf_op jit(solution)/shard_map/pallas_call | solution.py:25
  42.2 4.3 %shard_map.89 = (bf16[6,8,64,256]{3,2,1,0:T(8,128)(2,1)}, bf16[6,8,64,256]{3,2,1,0:T(8,128)(2,1)S(1)}) custom-call(s32[8,8]{1,0:T(8,128)S(1)} %fusion.6.refs_12_.index_ref, bf16[8,64,256]{2,1,0:T(8,128)(2,1)S(1)} %get-tuple-element.27.spread_ref, bf16[8,512,64]{2,1,0:T(8,128)(2,1)S(1)} %get-tuple-element.28.tall_ref), custom_call_target="tpu_custom_call" | custom-call | flops 134217728 | bytes 3932416 | tf_op jit(solution)/shard_map/pallas_call | solution.py:25
  47.1 3.2 %collective-permute-done.11.got_ref = f32[256,256]{1,0:T(8,128)S(1)} collective-permute-done((f32[256,256]{1,0:T(8,128)S(1)}, f32[256,256]{1,0:T(8,128)S(1)}, u32[]{:S(2)}, u32[]{:S(2)}) %collective-permute-start.11) | collective-permute-done | bytes 262176 | tf_op jit(solution)/shard_map/ppermute | solution.py:143
  50.4 1.6 %collective-permute-start.12 = (f32[64,256]{1,0:T(8,128)S(1)}, f32[64,256]{1,0:T(8,128)S(1)}, u32[]{:S(2)}, u32[]{:S(2)}) collective-permute-start(f32[64,256]{1,0:T(8,128)S(1)} %get-tuple-element.23), channel_id=1, source_target_pairs={{0,2},{1,3},{2,0},{3,1},{16,18},{17,19},{18,16},{19,17},{4,6},{5,7... | collective-permute-start | bytes 196616 | tf_op jit(solution)/shard_map/ppermute | solution.py:224
  54.8 1.9 %collective-permute-done.13 = f32[64,256]{1,0:T(8,128)S(1)} collective-permute-done((f32[64,256]{1,0:T(8,128)S(1)}, f32[64,256]{1,0:T(8,128)S(1)}, u32[]{:S(2)}, u32[]{:S(2)}) %collective-permute-start.13) | collective-permute-done | bytes 65568 | tf_op jit(solution)/shard_map/ppermute | solution.py:224
  56.7 1.9 %collective-permute-done.14 = f32[64,256]{1,0:T(8,128)S(1)} collective-permute-done((f32[64,256]{1,0:T(8,128)S(1)}, f32[64,256]{1,0:T(8,128)S(1)}, u32[]{:S(2)}, u32[]{:S(2)}) %collective-permute-start.14) | collective-permute-done | bytes 65568 | tf_op jit(solution)/shard_map/ppermute | solution.py:224
  58.6 3.8 %collective-permute-start.17 = (f32[64,256]{1,0:T(8,128)S(1)}, f32[64,256]{1,0:T(8,128)S(1)}, u32[]{:S(2)}, u32[]{:S(2)}) collective-permute-start(f32[64,256]{1,0:T(8,128)S(1)} %add_add_fusion.1), channel_id=1, source_target_pairs={{0,12},{4,8},{8,4},{12,0},{1,13},{5,9},{9,5},{13,1},{2,14},{6,10},... | collective-permute-start | bytes 196616 | tf_op jit(solution)/shard_map/ppermute | solution.py:243
  64.9 2.7 %collective-permute-done.16 = f32[64,256]{1,0:T(8,128)S(1)} collective-permute-done((f32[64,256]{1,0:T(8,128)S(1)}, f32[64,256]{1,0:T(8,128)S(1)}, u32[]{:S(2)}, u32[]{:S(2)}) %collective-permute-start.16) | collective-permute-done | bytes 65568 | tf_op jit(solution)/shard_map/ppermute | solution.py:243
  67.6 1.5 %collective-permute-start.20 = (f32[64,256]{1,0:T(8,128)S(1)}, f32[64,256]{1,0:T(8,128)S(1)}, u32[]{:S(2)}, u32[]{:S(2)}) collective-permute-start(f32[64,256]{1,0:T(8,128)S(1)} %add_add_fusion.refs_0_), channel_id=1, source_target_pairs={{0,18},{1,19},{2,16},{3,17},{16,2},{17,3},{18,0},{19,1},{4,22},{5,... | collective-permute-start | bytes 196616 | tf_op jit(solution)/shard_map/ppermute | solution.py:224
  71.2 1.8 %collective-permute-done.20.refs_3_ = f32[64,256]{1,0:T(8,128)S(1)} collective-permute-done((f32[64,256]{1,0:T(8,128)S(1)}, f32[64,256]{1,0:T(8,128)S(1)}, u32[]{:S(2)}, u32[]{:S(2)}) %collective-permute-start.20) | collective-permute-done | bytes 65568 | tf_op jit(solution)/shard_map/ppermute | solution.py:224
  73.4 5.7 %collective-permute-done.18.refs_1_ = f32[64,256]{1,0:T(8,128)S(1)} collective-permute-done((f32[64,256]{1,0:T(8,128)S(1)}, f32[64,256]{1,0:T(8,128)S(1)}, u32[]{:S(2)}, u32[]{:S(2)}) %collective-permute-start.18) | collective-permute-done | bytes 65568 | tf_op jit(solution)/shard_map/ppermute | solution.py:224
  82.5 3.5 %collective-permute-start.25 = (bf16[8,64,256]{2,1,0:T(8,128)(2,1)S(1)}, bf16[8,64,256]{2,1,0:T(8,128)(2,1)S(1)}, u32[]{:S(2)}, u32[]{:S(2)}) collective-permute-start(bf16[8,64,256]{2,1,0:T(8,128)(2,1)S(1)} %get-tuple-element.31), channel_id=1, source_target_pairs={{4,0},{8,4},{12,8},{0,12},{5,1},{9,5},{13,9},{1,13},{6,2},{10,6},{... | collective-permute-start | bytes 786440 | tf_op jit(solution)/shard_map/ppermute | solution.py:152
  86.9 2.1 %collective-permute-done.23 = bf16[8,64,256]{2,1,0:T(8,128)(2,1)S(1)} collective-permute-done((bf16[8,64,256]{2,1,0:T(8,128)(2,1)S(1)}, bf16[8,64,256]{2,1,0:T(8,128)(2,1)S(1)}, u32[]{:S(2)}, u32[]{:S(2)}) %collective-permute-start.23) | collective-permute-done | bytes 262176 | tf_op jit(solution)/shard_map/ppermute | solution.py:146
  89.0 3.8 %collective-permute-done.25 = bf16[8,64,256]{2,1,0:T(8,128)(2,1)S(1)} collective-permute-done((bf16[8,64,256]{2,1,0:T(8,128)(2,1)S(1)}, bf16[8,64,256]{2,1,0:T(8,128)(2,1)S(1)}, u32[]{:S(2)}, u32[]{:S(2)}) %collective-permute-start.25) | collective-permute-done | bytes 262176 | tf_op jit(solution)/shard_map/ppermute | solution.py:152
  92.8 5.6 %collective-permute-done.26 = bf16[8,64,256]{2,1,0:T(8,128)(2,1)S(1)} collective-permute-done((bf16[8,64,256]{2,1,0:T(8,128)(2,1)S(1)}, bf16[8,64,256]{2,1,0:T(8,128)(2,1)S(1)}, u32[]{:S(2)}, u32[]{:S(2)}) %collective-permute-start.26) | collective-permute-done | bytes 262176 | tf_op jit(solution)/shard_map/ppermute | solution.py:149
  (82 shorter events, 25.1 us)
Async XLA Ops:
  1.7 11.8 %collective-permute-start.7 = (bf16[8,64,256]{2,1,0:T(8,128)(2,1)S(1)}, bf16[8,64,256]{2,1,0:T(8,128)(2,1)S(1)}, u32[]{:S(2)}, u32[]{:S(2)}) collective-permute-start(bf16[8,64,256]{2,1,0:T(8,128)(2,1)S(1)} %bitcast.18), channel_id=1, source_target_pairs={{4,0},{8,4},{12,8},{0,12},{5,1},{9,5},{13,9},{1,13},{6,2},{10,6},{... | collective-permute-start | bytes 786440 | tf_op jit(solution)/shard_map/ppermute | solution.py:152
  6.8 12.1 %collective-permute-start.3 = (bf16[8,64,256]{2,1,0:T(8,128)(2,1)S(1)}, bf16[8,64,256]{2,1,0:T(8,128)(2,1)S(1)}, u32[]{:S(2)}, u32[]{:S(2)}) collective-permute-start(bf16[8,64,256]{2,1,0:T(8,128)(2,1)S(1)} %bitcast.19), channel_id=1, source_target_pairs={{0,4},{4,8},{8,12},{12,0},{1,5},{5,9},{9,13},{13,1},{2,6},{6,10},{... | collective-permute-start | bytes 786440 | tf_op jit(solution)/shard_map/ppermute | solution.py:149
  6.8 14.6 %collective-permute-start.1 = (bf16[8,64,256]{2,1,0:T(8,128)(2,1)S(1)}, bf16[8,64,256]{2,1,0:T(8,128)(2,1)S(1)}, u32[]{:S(2)}, u32[]{:S(2)}) collective-permute-start(bf16[8,64,256]{2,1,0:T(8,128)(2,1)S(1)} %bitcast.20), channel_id=1, source_target_pairs={{0,2},{1,3},{2,0},{3,1},{4,6},{5,7},{6,4},{7,5},{8,10},{9,11},{10,... | collective-permute-start | bytes 786440 | tf_op jit(solution)/shard_map/ppermute | solution.py:146
  8.3 13.5 %collective-permute-start = (bf16[8,64,256]{2,1,0:T(8,128)(2,1)S(1)}, bf16[8,64,256]{2,1,0:T(8,128)(2,1)S(1)}, u32[]{:S(2)}, u32[]{:S(2)}) collective-permute-start(bf16[8,64,256]{2,1,0:T(8,128)(2,1)S(1)} %bitcast.21), channel_id=1, source_target_pairs={{0,1},{1,0},{2,3},{3,2},{4,5},{5,4},{6,7},{7,6},{8,9},{9,8},{10,11... | collective-permute-start | bytes 786440 | tf_op jit(solution)/shard_map/ppermute | solution.py:143
  13.5 8.5 %collective-permute-start.9 = (bf16[8,64,256]{2,1,0:T(8,128)(2,1)S(1)}, bf16[8,64,256]{2,1,0:T(8,128)(2,1)S(1)}, u32[]{:S(2)}, u32[]{:S(2)}) collective-permute-start(bf16[8,64,256]{2,1,0:T(8,128)(2,1)S(1)} %collective-permute-done.7.refs_8_), channel_id=1, source_target_pairs={{0,2},{1,3},{2,0},{3,1},{4,6},{5,7},{6,4},{7,5},{8,10},{9,11},{10,... | collective-permute-start | bytes 786440 | tf_op jit(solution)/shard_map/ppermute | solution.py:146
  18.9 7.2 %collective-permute-start.5 = (bf16[8,64,256]{2,1,0:T(8,128)(2,1)S(1)}, bf16[8,64,256]{2,1,0:T(8,128)(2,1)S(1)}, u32[]{:S(2)}, u32[]{:S(2)}) collective-permute-start(bf16[8,64,256]{2,1,0:T(8,128)(2,1)S(1)} %collective-permute-done.3.refs_4_), channel_id=1, source_target_pairs={{0,2},{1,3},{2,0},{3,1},{4,6},{5,7},{6,4},{7,5},{8,10},{9,11},{10,... | collective-permute-start | bytes 786440 | tf_op jit(solution)/shard_map/ppermute | solution.py:146
  21.3 11.0 %collective-permute-start.8 = (bf16[8,64,256]{2,1,0:T(8,128)(2,1)S(1)}, bf16[8,64,256]{2,1,0:T(8,128)(2,1)S(1)}, u32[]{:S(2)}, u32[]{:S(2)}) collective-permute-start(bf16[8,64,256]{2,1,0:T(8,128)(2,1)S(1)} %collective-permute-done.7.refs_8_), channel_id=1, source_target_pairs={{0,1},{1,0},{2,3},{3,2},{4,5},{5,4},{6,7},{7,6},{8,9},{9,8},{10,11... | collective-permute-start | bytes 786440 | tf_op jit(solution)/shard_map/ppermute | solution.py:143
  21.4 10.9 %collective-permute-start.4 = (bf16[8,64,256]{2,1,0:T(8,128)(2,1)S(1)}, bf16[8,64,256]{2,1,0:T(8,128)(2,1)S(1)}, u32[]{:S(2)}, u32[]{:S(2)}) collective-permute-start(bf16[8,64,256]{2,1,0:T(8,128)(2,1)S(1)} %collective-permute-done.3.refs_4_), channel_id=1, source_target_pairs={{0,1},{1,0},{2,3},{3,2},{4,5},{5,4},{6,7},{7,6},{8,9},{9,8},{10,11... | collective-permute-start | bytes 786440 | tf_op jit(solution)/shard_map/ppermute | solution.py:143
  21.9 10.4 %collective-permute-start.2 = (bf16[8,64,256]{2,1,0:T(8,128)(2,1)S(1)}, bf16[8,64,256]{2,1,0:T(8,128)(2,1)S(1)}, u32[]{:S(2)}, u32[]{:S(2)}) collective-permute-start(bf16[8,64,256]{2,1,0:T(8,128)(2,1)S(1)} %collective-permute-done.1.refs_2_), channel_id=1, source_target_pairs={{0,1},{1,0},{2,3},{3,2},{4,5},{5,4},{6,7},{7,6},{8,9},{9,8},{10,11... | collective-permute-start | bytes 786440 | tf_op jit(solution)/shard_map/ppermute | solution.py:143
  22.0 10.3 %collective-permute-start.10 = (bf16[8,64,256]{2,1,0:T(8,128)(2,1)S(1)}, bf16[8,64,256]{2,1,0:T(8,128)(2,1)S(1)}, u32[]{:S(2)}, u32[]{:S(2)}) collective-permute-start(bf16[8,64,256]{2,1,0:T(8,128)(2,1)S(1)} %collective-permute-done.9.refs_10_), channel_id=1, source_target_pairs={{0,1},{1,0},{2,3},{3,2},{4,5},{5,4},{6,7},{7,6},{8,9},{9,8},{10,11... | collective-permute-start | bytes 786440 | tf_op jit(solution)/shard_map/ppermute | solution.py:143
  26.1 6.2 %collective-permute-start.6 = (bf16[8,64,256]{2,1,0:T(8,128)(2,1)S(1)}, bf16[8,64,256]{2,1,0:T(8,128)(2,1)S(1)}, u32[]{:S(2)}, u32[]{:S(2)}) collective-permute-start(bf16[8,64,256]{2,1,0:T(8,128)(2,1)S(1)} %collective-permute-done.5.refs_6_), channel_id=1, source_target_pairs={{0,1},{1,0},{2,3},{3,2},{4,5},{5,4},{6,7},{7,6},{8,9},{9,8},{10,11... | collective-permute-start | bytes 786440 | tf_op jit(solution)/shard_map/ppermute | solution.py:143
  46.5 16.6 %collective-permute-start.22 = (bf16[6,8,64,256]{3,2,1,0:T(8,128)(2,1)}, bf16[6,8,64,256]{3,2,1,0:T(8,128)(2,1)}, u32[]{:S(2)}, u32[]{:S(2)}) collective-permute-start(bf16[6,8,64,256]{3,2,1,0:T(8,128)(2,1)} %get-tuple-element.30), channel_id=1, source_target_pairs={{0,1},{1,0},{2,3},{3,2},{4,5},{5,4},{6,7},{7,6},{8,9},{9,8},{10,11... | collective-permute-start | bytes 4718600 | tf_op jit(solution)/shard_map/ppermute | solution.py:143
  52.0 4.7 %collective-permute-start.13 = (f32[64,256]{1,0:T(8,128)S(1)}, f32[64,256]{1,0:T(8,128)S(1)}, u32[]{:S(2)}, u32[]{:S(2)}) collective-permute-start(f32[64,256]{1,0:T(8,128)S(1)} %get-tuple-element.24), channel_id=1, source_target_pairs={{0,16},{1,17},{2,18},{3,19},{16,0},{17,1},{18,2},{19,3},{4,20},{5,... | collective-permute-start | bytes 196616 | tf_op jit(solution)/shard_map/ppermute | solution.py:224
  53.4 5.2 %collective-permute-start.14 = (f32[64,256]{1,0:T(8,128)S(1)}, f32[64,256]{1,0:T(8,128)S(1)}, u32[]{:S(2)}, u32[]{:S(2)}) collective-permute-start(f32[64,256]{1,0:T(8,128)S(1)} %get-tuple-element.25), channel_id=1, source_target_pairs={{0,18},{1,19},{2,16},{3,17},{16,2},{17,3},{18,0},{19,1},{4,22},{5,... | collective-permute-start | bytes 196616 | tf_op jit(solution)/shard_map/ppermute | solution.py:224
  58.6 6.2 %collective-permute-start.17 = (f32[64,256]{1,0:T(8,128)S(1)}, f32[64,256]{1,0:T(8,128)S(1)}, u32[]{:S(2)}, u32[]{:S(2)}) collective-permute-start(f32[64,256]{1,0:T(8,128)S(1)} %add_add_fusion.1), channel_id=1, source_target_pairs={{0,12},{4,8},{8,4},{12,0},{1,13},{5,9},{9,5},{13,1},{2,14},{6,10},... | collective-permute-start | bytes 196616 | tf_op jit(solution)/shard_map/ppermute | solution.py:243
  62.4 5.2 %collective-permute-start.16 = (f32[64,256]{1,0:T(8,128)S(1)}, f32[64,256]{1,0:T(8,128)S(1)}, u32[]{:S(2)}, u32[]{:S(2)}) collective-permute-start(f32[64,256]{1,0:T(8,128)S(1)} %add_add_fusion.1), channel_id=1, source_target_pairs={{0,8},{4,12},{8,0},{12,4},{1,9},{5,13},{9,1},{13,5},{2,10},{6,14},... | collective-permute-start | bytes 196616 | tf_op jit(solution)/shard_map/ppermute | solution.py:243
  62.4 5.2 %collective-permute-start.15 = (f32[64,256]{1,0:T(8,128)S(1)}, f32[64,256]{1,0:T(8,128)S(1)}, u32[]{:S(2)}, u32[]{:S(2)}) collective-permute-start(f32[64,256]{1,0:T(8,128)S(1)} %add_add_fusion.1), channel_id=1, source_target_pairs={{0,4},{4,0},{8,12},{12,8},{1,5},{5,1},{9,13},{13,9},{2,6},{6,2},{1... | collective-permute-start | bytes 196616 | tf_op jit(solution)/shard_map/ppermute | solution.py:243
  64.3 16.9 %collective-permute-start.24 = (bf16[2,8,64,256]{3,2,1,0:T(8,128)(2,1)S(1)}, bf16[2,8,64,256]{3,2,1,0:T(8,128)(2,1)S(1)}, u32[]{:S(2)}, u32[]{:S(2)}) collective-permute-start(bf16[2,8,64,256]{3,2,1,0:T(8,128)(2,1)S(1)} %add_convert_fusion.1), channel_id=1, source_target_pairs={{0,2},{1,3},{2,0},{3,1},{4,6},{5,7},{6,4},{7,5},{8,10},{9,11},{10,... | collective-permute-start | bytes 1572872 | tf_op jit(solution)/shard_map/ppermute | solution.py:146
  67.6 5.3 %collective-permute-start.20 = (f32[64,256]{1,0:T(8,128)S(1)}, f32[64,256]{1,0:T(8,128)S(1)}, u32[]{:S(2)}, u32[]{:S(2)}) collective-permute-start(f32[64,256]{1,0:T(8,128)S(1)} %add_add_fusion.refs_0_), channel_id=1, source_target_pairs={{0,18},{1,19},{2,16},{3,17},{16,2},{17,3},{18,0},{19,1},{4,22},{5,... | collective-permute-start | bytes 196616 | tf_op jit(solution)/shard_map/ppermute | solution.py:224
  69.9 9.2 %collective-permute-start.18 = (f32[64,256]{1,0:T(8,128)S(1)}, f32[64,256]{1,0:T(8,128)S(1)}, u32[]{:S(2)}, u32[]{:S(2)}) collective-permute-start(f32[64,256]{1,0:T(8,128)S(1)} %add_add_fusion.refs_0_), channel_id=1, source_target_pairs={{0,2},{1,3},{2,0},{3,1},{16,18},{17,19},{18,16},{19,17},{4,6},{5,7... | collective-permute-start | bytes 196616 | tf_op jit(solution)/shard_map/ppermute | solution.py:224
  79.1 7.0 %collective-permute-start.21 = (f32[256,256]{1,0:T(8,128)S(1)}, f32[256,256]{1,0:T(8,128)S(1)}, u32[]{:S(2)}, u32[]{:S(2)}) collective-permute-start(f32[256,256]{1,0:T(8,128)S(1)} %shard_map.88), channel_id=1, source_target_pairs={{0,1},{1,0},{2,3},{3,2},{4,5},{5,4},{6,7},{7,6},{8,9},{9,8},{10,11... | collective-permute-start | bytes 786440 | tf_op jit(solution)/shard_map/ppermute | solution.py:143
  80.2 8.8 %collective-permute-start.23 = (bf16[8,64,256]{2,1,0:T(8,128)(2,1)S(1)}, bf16[8,64,256]{2,1,0:T(8,128)(2,1)S(1)}, u32[]{:S(2)}, u32[]{:S(2)}) collective-permute-start(bf16[8,64,256]{2,1,0:T(8,128)(2,1)S(1)} %fusion.2), channel_id=1, source_target_pairs={{0,2},{1,3},{2,0},{3,1},{4,6},{5,7},{6,4},{7,5},{8,10},{9,11},{10,... | collective-permute-start | bytes 786440 | tf_op jit(solution)/shard_map/ppermute | solution.py:146
  82.5 10.2 %collective-permute-start.25 = (bf16[8,64,256]{2,1,0:T(8,128)(2,1)S(1)}, bf16[8,64,256]{2,1,0:T(8,128)(2,1)S(1)}, u32[]{:S(2)}, u32[]{:S(2)}) collective-permute-start(bf16[8,64,256]{2,1,0:T(8,128)(2,1)S(1)} %get-tuple-element.31), channel_id=1, source_target_pairs={{4,0},{8,4},{12,8},{0,12},{5,1},{9,5},{13,9},{1,13},{6,2},{10,6},{... | collective-permute-start | bytes 786440 | tf_op jit(solution)/shard_map/ppermute | solution.py:152
  86.1 12.3 %collective-permute-start.26 = (bf16[8,64,256]{2,1,0:T(8,128)(2,1)S(1)}, bf16[8,64,256]{2,1,0:T(8,128)(2,1)S(1)}, u32[]{:S(2)}, u32[]{:S(2)}) collective-permute-start(bf16[8,64,256]{2,1,0:T(8,128)(2,1)S(1)} %get-tuple-element.32), channel_id=1, source_target_pairs={{0,4},{4,8},{8,12},{12,0},{1,5},{5,9},{9,13},{13,1},{2,6},{6,10},{... | collective-permute-start | bytes 786440 | tf_op jit(solution)/shard_map/ppermute | solution.py:149
  (20 other events, 115.1 us)

commit v2 on v1

v2 whole, which is shorter than its diff:
```python
import functools

import jax
import jax.numpy as jnp
from jax import lax
from jax.experimental import pallas as pl
from jax.experimental.pallas import tpu as pltpu
from jax.sharding import PartitionSpec as P

BLOCK = 64
F32 = jnp.float32
BF16 = jnp.bfloat16
VMEM = pl.BlockSpec(memory_space=pltpu.VMEM)
SMEM = pl.BlockSpec(memory_space=pltpu.SMEM)
ANY = pl.BlockSpec(memory_space=pl.ANY)
ROWS_BOTH = ((0,), (0,))


def shape(dims, dtype):
    return jax.ShapeDtypeStruct(dims, dtype)


def call(body, out_shape, operands, in_specs, out_specs, scratch=(), flops=0, vmem=60):
    moved = sum(x.size * x.dtype.itemsize for x in list(operands) + list(out_shape))
    return pl.pallas_call(
        body,
        out_shape=out_shape,
        in_specs=in_specs,
        out_specs=out_specs,
        scratch_shapes=scratch,
        compiler_params=pltpu.CompilerParams(vmem_limit_bytes=vmem << 20),
        cost_estimate=pl.CostEstimate(flops=flops, bytes_accessed=moved, transcendentals=0),
    )(*operands)


def dot(a, b, contract=((1,), (0,))):
    return lax.dot_general(a, b, (contract, ((), ())), preferred_element_type=F32)


def halves(x):
    high = x.astype(BF16)
    return high, (x - high.astype(F32)).astype(BF16)


def dot3(a, b, contract=((1,), (0,))):
    return dot(a[0], b[0], contract) + (dot(a[0], b[1], contract) + dot(a[1], b[0], contract))


def wider(x):
    return jnp.concatenate([x, x], axis=-1)


def prepare_body(
    edge_hbm, feat_hbm, self_hbm, neigh_hbm, label_ref,
    wide_ref, tall_ref, inverse_ref, logit_ref, label_out, feat_out, weight_out,
    edge_ref, feat_ref, self_ref, neigh_ref, sems,
):
    blocks, slots = edge_ref.shape[:2]
    tiles = [pltpu.make_async_copy(edge_hbm.at[b], edge_ref.at[b], sems.at[b]) for b in range(blocks)]
    dense = [
        pltpu.make_async_copy(source, target, sems.at[blocks + i])
        for i, (source, target) in enumerate(
            ((feat_hbm, feat_ref), (self_hbm, self_ref), (neigh_hbm, neigh_ref))
        )
    ]
    for c in tiles + dense:
        c.start()
    lines = label_ref.shape[0]
    columns = jnp.concatenate([label_ref[...].astype(F32), jnp.zeros((8 - lines % 8, 128), F32)], axis=0).T
    for r in range(lines):
        label_out[r * 128 : (r + 1) * 128] = jnp.broadcast_to(columns[:, r : r + 1], (128, 128))
    for b in range(blocks):
        tiles[b].wait()
        wide = jnp.concatenate([edge_ref[b, s].astype(F32) for s in range(slots)], axis=1)
        wide_ref[b] = wide.astype(BF16)
        tall_ref[b] = wide.T.astype(BF16)
        degree = jnp.sum(wide, axis=1, keepdims=True)
        inverse_ref[b] = jnp.broadcast_to(1.0 / degree, inverse_ref.shape[1:])
    for c in dense:
        c.wait()
    feat, own, neigh = feat_ref[...], self_ref[...], neigh_ref[...]
    logit_ref[...] = dot3(halves(feat), halves(own))
    for k, x in enumerate(halves(feat.T)):
        feat_out[k] = x
    for k, x in enumerate(halves(neigh) + halves(neigh.T) + halves(own.T)):
        weight_out[k] = x


def layer_body(*refs):
    pieces, refs = refs[:12], refs[12:]
    place_ref, source_ref, refs = refs[0], refs[1], refs[2:]
    inputs, outputs, refs = refs[:7], refs[7:14], refs[14:]
    table, held, made, refs = refs[0], refs[1:8], refs[8:15], refs[15:]
    mean, terms, index, piece_sems, in_sems, out_sems = refs
    wide_ref, inverse_ref, logit_ref, label_ref, weight_ref, tall_ref, feat_ref = held
    direct_ref, mine_ref, passed_ref = made[4:]
    per = pieces[0].shape[0]
    copies = [
        pltpu.make_async_copy(piece, table.at[pl.ds(i * per, per)], piece_sems.at[i])
        for i, piece in enumerate(pieces)
    ]
    loads = [pltpu.make_async_copy(x, y, in_sems.at[i]) for i, (x, y) in enumerate(zip(inputs, held))]
    for c in loads[:1] + copies + loads[1:]:
        c.start()

    def store(i, source, target):
        c = pltpu.make_async_copy(source, target, out_sems.at[i])
        c.start()
        return c

    blocks, rows, wide_cols = wide_ref.shape
    slots = wide_cols // BLOCK
    me = place_ref[0]

    for b in range(blocks):
        for s in range(slots):
            index[b, s] = source_ref[b, s] ^ (me * blocks)
    terms[...] = jnp.zeros_like(terms)
    for c in loads[:1] + copies + loads[1:2]:
        c.wait()

    for b in range(blocks):
        gathered = jnp.concatenate([table[index[b, s]] for s in range(slots)], axis=0)
        total = dot(wide_ref[b], gathered)
        mean[b * rows : (b + 1) * rows] = total * wider(inverse_ref[b])

    for c in loads[2:5]:
        c.wait()
    neigh, neigh_t, own_t = [(weight_ref[2 * k], weight_ref[2 * k + 1]) for k in range(3)]
    mean_parts = halves(mean[...])
    logits = logit_ref[...] + dot3(mean_parts, neigh)
    classes = lax.broadcasted_iota(jnp.int32, logits.shape, 1).astype(F32)
    target = jnp.where(classes == wider(label_ref[...]), 1.0, 0.0)
    residual = halves(1.0 / (1.0 + jnp.exp(-logits)) - target)
    inverse = inverse_ref[...].reshape(blocks * rows, 128)
    spread = (dot3(residual, neigh_t) * wider(inverse)).astype(BF16)
    direct_ref[...] = dot3(residual, own_t)
    stores = [store(0, direct_ref, outputs[4])]

    for c in loads[5:]:
        c.wait()
    for b in range(blocks):
        contrib = dot(tall_ref[b], spread[b * rows : (b + 1) * rows])
        for s in range(slots):
            at = index[b, s]
            terms[at] = terms[at] + contrib[s * BLOCK : (s + 1) * BLOCK]

    count = 1
    for core in (1, 0):
        for place in range(6):
            rel = 2 + core if place < 3 else core
            region = (1, 2, 0)[place % 3]
            which, at = (2 * core, place) if place < 2 else (2 * core + 1, place - 2)
            made[which][at] = terms[pl.ds((region * 4 + rel) * per, per)].astype(BF16)
            stores.append(store(count, made[which].at[at], outputs[which].at[at]))
            count += 1

    self_part = dot3((feat_ref[0], feat_ref[1]), residual)
    neigh_part = dot3(mean_parts, residual, ROWS_BOTH)
    first = me % 2 == 0
    mine_ref[...] = jnp.where(first, self_part, neigh_part)
    passed_ref[...] = jnp.where(first, neigh_part, self_part)
    stores.append(store(count, mine_ref, outputs[5]))
    stores.append(store(count + 1, passed_ref, outputs[6]))
    for c in stores:
        c.wait()


def split_body(place_ref, *refs):
    outs = [r for r in refs if r.shape != refs[0].shape]
    total = tree_sum(r[...] for r in refs[: len(refs) - len(outs)])
    chunks = total.reshape(len(outs), *outs[0].shape)
    if len(outs) == 1:
        outs[0][...] = chunks[0]
        return
    for d, out in enumerate(outs):
        for c in range(len(outs)):

            @pl.when(place_ref[0] ^ d == c)
            def _():
                out[...] = chunks[c]


def join_body(place_ref, *refs):
    out = refs[-1]
    rows = refs[0].shape[0]
    for d, chunk in enumerate(refs[:-1]):
        for c in range(len(refs) - 1):

            @pl.when(place_ref[0] ^ d == c)
            def _():
                out[c * rows : (c + 1) * rows] = chunk[...]


def tree_sum(values):
    values = list(values)
    while len(values) > 1:
        values = [sum(values[i + 1 : i + 2], values[i]) for i in range(0, len(values), 2)]
    return values[0]


def on_device(features, self_weight, neigh_weight, block_source, edge_weights, labels):
    rows, width = features.shape
    blocks, slots = block_source.shape
    classes = self_weight.shape[1]
    reps = lax.axis_size("rep")
    assert reps == 4
    me = lax.axis_index("rep").astype(jnp.int32)

    def swap(x, axis, d):
        return lax.ppermute(x, axis, [(i, i ^ d) for i in range(lax.axis_size(axis))])

    def core_swap(x):
        return swap(x, "rep", 1)

    def half_swap(x):
        return swap(x, "rep", 2)

    def up(x):
        cols = lax.axis_size("col")
        return lax.ppermute(x, "col", [(i, (i + 1) % cols) for i in range(cols)])

    def down(x):
        cols = lax.axis_size("col")
        return lax.ppermute(x, "col", [((i + 1) % cols, i) for i in range(cols)])

    own = features.astype(BF16).reshape(blocks, BLOCK, width)
    half, lower, upper, core = half_swap(own), up(own), down(own), core_swap(own)

    wide_cols = slots * BLOCK
    prepared = call(
        prepare_body,
        (
            shape((blocks, BLOCK, wide_cols), BF16),
            shape((blocks, wide_cols, BLOCK), BF16),
            shape((blocks, BLOCK, 128), F32),
            shape((rows, classes), F32),
            shape((rows, 128), F32),
            shape((2, width, rows), BF16),
            shape((6, width, classes), BF16),
        ),
        (edge_weights, features, self_weight, neigh_weight, labels.reshape(rows // 128, 128)),
        [ANY] * 4 + [VMEM],
        [VMEM] * 7,
        scratch=[
            pltpu.VMEM(edge_weights.shape, jnp.int32),
            pltpu.VMEM(features.shape, F32),
            pltpu.VMEM(self_weight.shape, F32),
            pltpu.VMEM(neigh_weight.shape, F32),
            pltpu.SemaphoreType.DMA((blocks + 3,)),
        ],
        flops=6 * rows * width * classes,
    )
    wide, tall, inverse, self_logits, label_cols, feat_parts, weight_parts = prepared
    half, lower, upper, core = (lax.optimization_barrier((x, inverse))[0] for x in (half, lower, upper, core))
    lower_half, upper_half = half_swap(lower), half_swap(upper)
    pieces = [
        own, core, half, core_swap(half),
        lower, core_swap(lower), lower_half, core_swap(lower_half),
        upper, core_swap(upper), upper_half, core_swap(upper_half),
    ]

    def piece_shape(*lead):
        return shape((*lead, blocks, BLOCK, width), BF16)

    inputs = (wide, inverse, self_logits, label_cols, weight_parts, tall, feat_parts)
    outputs = (
        piece_shape(2), piece_shape(4), piece_shape(2), piece_shape(4),
        shape((rows, width), F32), shape((width, classes), F32), shape((width, classes), F32),
    )
    keep_near, keep_rest, send_near, send_rest, direct, mine, passed = call(
        layer_body,
        outputs,
        (*pieces, me.reshape(1), block_source, *inputs),
        [ANY] * 12 + [SMEM] * 2 + [ANY] * 7,
        [ANY] * 7,
        scratch=[
            pltpu.VMEM((12 * blocks, BLOCK, width), BF16),
            *[pltpu.VMEM(x.shape, x.dtype) for x in inputs + outputs],
            pltpu.VMEM((rows, width), F32),
            pltpu.VMEM((12 * blocks, BLOCK, width), F32),
            pltpu.SMEM((blocks, slots), jnp.int32),
            pltpu.SemaphoreType.DMA((12,)),
            pltpu.SemaphoreType.DMA((7,)),
            pltpu.SemaphoreType.DMA((15,)),
        ],
        flops=40 * rows * width * classes,
    )
    got_near, got_rest, got = core_swap(send_near), core_swap(send_rest), core_swap(passed)

    def both(a, b):
        return a.astype(F32) + b.astype(F32)

    lines, cols = lax.axis_size("row"), lax.axis_size("col")
    group = lines * reps // 2
    place = lax.axis_index("row").astype(jnp.int32) * (reps // 2) + me // 2

    def to_group(x, d):
        pairs = [(g * 2 + c, (g ^ d) * 2 + c) for g in range(group) for c in range(2)]
        return lax.ppermute(x, ("row", "rep"), pairs)

    def split(parts):
        chunk = shape((parts[0].shape[0] // group, classes), F32)
        return call(
            split_body,
            (chunk,) * group,
            (place.reshape(1), *parts),
            [SMEM] + [VMEM] * len(parts),
            [VMEM] * group,
            vmem=4,
        )

    def join(chunk):
        parts = [chunk] + [to_group(chunk, d) for d in range(1, group)]
        (out,) = call(
            join_body,
            (shape((chunk.shape[0] * group, classes), F32),),
            (place.reshape(1), *parts),
            [SMEM] + [VMEM] * group,
            [VMEM],
            vmem=4,
        )
        return out

    near = [both(keep_near[k], got_near[k]).astype(BF16) for k in range(2)]
    near, got = lax.optimization_barrier((near, got))
    half_near = [half_swap(x) for x in near]
    chunks = split((mine, got))
    part = tree_sum([chunks[0]] + [to_group(c, d) for d, c in enumerate(chunks) if d])
    step = 1
    while step < cols:
        part = part + swap(part, "col", step)
        step *= 2
    half_near, part, got_rest = lax.optimization_barrier((half_near, part, got_rest))

    near = [both(keep_rest[1 + k], got_rest[1 + k]) + half_near[k].astype(F32) for k in range(2)]
    from_upper = down(near[0].astype(BF16))
    from_lower = up(near[1].astype(BF16))
    half_own = half_swap(both(keep_rest[0], got_rest[0]).astype(BF16))
    whole = join(part)
    other = core_swap(whole)
    first = me % 2 == 0
    grad_self = jnp.where(first, whole, other)
    grad_neigh = jnp.where(first, other, whole)

    own_terms = both(keep_rest[3], got_rest[3]) + half_own.astype(F32)
    own_terms = own_terms + from_upper.astype(F32) + from_lower.astype(F32)
    grad_features = direct + own_terms.reshape(rows, width)
    return grad_self, grad_neigh, grad_features


def solution(mesh):
    split = ("row", "col", "rep")
    return jax.shard_map(
        on_device,
        mesh=mesh,
        in_specs=(P(split, None), P(), P(), P(split, None), P(split, None, None, None), P(split)),
        out_specs=(P(), P(), P(split, None)),
        check_vma=False,
    )
```

time: 102 us -> 82.4 us (0.81)
  waiting for transfers between devices: 42.7 us -> 31.1 us
  local copies, waits for them, and re-layouts: 9.36 us -> 1.62 us
  Pallas kernels: 11.9 us -> 13.9 us
  matrix products: 1.42 us -> 0 us
    ppermute x2, waiting for transfers between devices: 8.99 us -> 0.01 us  [down(): return lax.ppermute(x, 'col', [((i + 1) % cols, i) for i in range(cols)])]
    unnamed x34 -> x30, local copies, waits for them, and re-layouts: 8.46 us -> 1.62 us
    ppermute x17 -> x18, waiting for transfers between devices: 11.7 us -> 18.5 us  [swap(): lax.ppermute(x, axis, [(i, i ^ d) for i in range(lax.axis_size(axis))])]
    ppermute x6, waiting for transfers between devices: 12.6 us -> 7.25 us  [to_group(): return lax.ppermute(x, ('row', 'rep'), pairs)]
    ppermute x2, waiting for transfers between devices: 9.45 us -> 5.36 us  [up(): return lax.ppermute(x, 'col', [(i, (i + 1) % cols) for i in range(cols)])]
    pallas_call x5 -> x4, Pallas kernels: 11.9 us -> 13.9 us  [call(): pl.pallas_call(body, out_shape=out_shape, in_specs=in_specs, out_specs=ou...]
    dot_general x1 -> x0, matrix products: 1.42 us -> none  [on_device(): direct = jnp.dot(residual, self_weight.T, precision=HIGH)]
    ppermute x17 -> x18, starting transfers between devices: 12.3 us -> 11 us  [swap(): lax.ppermute(x, axis, [(i, i ^ d) for i in range(lax.axis_size(axis))])]
  transfers between devices with their start and end apart: 27 -> 28, of which waited for: 14 -> 14; matrix products, arithmetic and copies ran while one was open for 5% -> 5% of each run, Pallas kernels for 2% -> 7%
where the time goes in v2:
time: 82.4 us; the launch traced here: 82.1 us
  waiting for transfers between devices  31.1 us (38%)
  starting transfers between devices  27.7 us (34%)
  Pallas kernels  13.9 us (17%)
  other arithmetic  6.88 us (8%)
  local copies, waits for them, and re-layouts  1.62 us (2%)
  between operations  0.91 us (1%)
    ppermute x18, waiting for transfers between devices, swap(): lax.ppermute(x, axis, [(i, i ^ d) for i in range(lax.axis_size(axis))])  18.5 us
    pallas_call x4, Pallas kernels, call(): pl.pallas_call(body, out_shape=out_shape, in_specs=in_specs, out_specs=ou...  13.9 us
    ppermute x18, starting transfers between devices, swap(): lax.ppermute(x, axis, [(i, i ^ d) for i in range(lax.axis_size(axis))])  11 us
    ppermute x2, starting transfers between devices, down(): return lax.ppermute(x, 'col', [((i + 1) % cols, i) for i in range(cols)])  8.98 us
    ppermute x6, starting transfers between devices, to_group(): return lax.ppermute(x, ('row', 'rep'), pairs)  7.71 us
    ppermute x6, waiting for transfers between devices, to_group(): return lax.ppermute(x, ('row', 'rep'), pairs)  7.25 us
    ppermute x2, waiting for transfers between devices, up(): return lax.ppermute(x, 'col', [(i, (i + 1) % cols) for i in range(cols)])  5.36 us
  transfers between devices with their start and end apart: 28, of which 14 were waited for; matrix products, arithmetic and copies ran while one was open for 5% of the time, Pallas kernels for 7%

profile of v2, /device:TPU:0, one launch (start us, length us, event | category | flops | bytes accessed | tf_op | source)
XLA Modules:
  0.0 82.1 jit_solution(6246455682243432492)
XLA Ops:
  1.7 5.1 %collective-permute-start.7 = (bf16[8,64,256]{2,1,0:T(8,128)(2,1)S(1)}, bf16[8,64,256]{2,1,0:T(8,128)(2,1)S(1)}, u32[]{:S(2)}, u32[]{:S(2)}) collective-permute-start(bf16[8,64,256]{2,1,0:T(8,128)(2,1)S(1)} %bitcast.26), channel_id=1, source_target_pairs={{4,0},{8,4},{12,8},{0,12},{5,1},{9,5},{13,9},{1,13},{6,2},{10,6},{... | collective-permute-start | bytes 786440 | tf_op jit(solution)/shard_map/ppermute | solution.py:225
  6.8 1.5 %collective-permute-start.1 = (bf16[8,64,256]{2,1,0:T(8,128)(2,1)S(1)}, bf16[8,64,256]{2,1,0:T(8,128)(2,1)S(1)}, u32[]{:S(2)}, u32[]{:S(2)}) collective-permute-start(bf16[8,64,256]{2,1,0:T(8,128)(2,1)S(1)} %bitcast.28), channel_id=1, source_target_pairs={{0,2},{1,3},{2,0},{3,1},{4,6},{5,7},{6,4},{7,5},{8,10},{9,11},{10,... | collective-permute-start | bytes 786440 | tf_op jit(solution)/shard_map/ppermute | solution.py:211
  8.3 5.5 %shard_map.85 = (bf16[8,64,512]{2,1,0:T(8,128)(2,1)}, bf16[8,512,64]{2,1,0:T(8,128)(2,1)}, f32[8,64,128]{2,1,0:T(8,128)}, f32[512,256]{1,0:T(8,128)}, f32[512,12...) custom-call(s32[8,8,64,64]{3,2,1,0:T(8,128)} %edge_hbm.1, f32[512,256]{1,0:T(8,128)} %feat_hbm.1, ...), custom_call_target="tpu_custom_call" | custom-call | flops 201326592 | bytes 5507072 | tf_op jit(solution)/shard_map/pallas_call | solution.py:25
  15.1 3.9 %collective-permute-done.3.refs_4_ = bf16[8,64,256]{2,1,0:T(8,128)(2,1)S(1)} collective-permute-done((bf16[8,64,256]{2,1,0:T(8,128)(2,1)S(1)}, bf16[8,64,256]{2,1,0:T(8,128)(2,1)S(1)}, u32[]{:S(2)}, u32[]{:S(2)}) %collective-permute-start.3) | collective-permute-done | bytes 262176 | tf_op jit(solution)/shard_map/ppermute | solution.py:221
  18.9 1.5 %collective-permute-start.5 = (bf16[8,64,256]{2,1,0:T(8,128)(2,1)S(1)}, bf16[8,64,256]{2,1,0:T(8,128)(2,1)S(1)}, u32[]{:S(2)}, u32[]{:S(2)}) collective-permute-start(bf16[8,64,256]{2,1,0:T(8,128)(2,1)S(1)} %collective-permute-done.3.refs_4_), channel_id=1, source_target_pairs={{0,2},{1,3},{2,0},{3,1},{4,6},{5,7},{6,4},{7,5},{8,10},{9,11},{10,... | collective-permute-start | bytes 786440 | tf_op jit(solution)/shard_map/ppermute | solution.py:211
  21.0 2.0 %collective-permute-done.9.refs_10_ = bf16[8,64,256]{2,1,0:T(8,128)(2,1)S(1)} collective-permute-done((bf16[8,64,256]{2,1,0:T(8,128)(2,1)S(1)}, bf16[8,64,256]{2,1,0:T(8,128)(2,1)S(1)}, u32[]{:S(2)}, u32[]{:S(2)}) %collective-permute-start.9) | collective-permute-done | bytes 262176 | tf_op jit(solution)/shard_map/ppermute | solution.py:211
  23.1 5.2 %collective-permute-done.5.refs_6_ = bf16[8,64,256]{2,1,0:T(8,128)(2,1)S(1)} collective-permute-done((bf16[8,64,256]{2,1,0:T(8,128)(2,1)S(1)}, bf16[8,64,256]{2,1,0:T(8,128)(2,1)S(1)}, u32[]{:S(2)}, u32[]{:S(2)}) %collective-permute-start.5) | collective-permute-done | bytes 262176 | tf_op jit(solution)/shard_map/ppermute | solution.py:211
  28.4 1.5 %collective-permute-done.6.refs_7_ = bf16[8,64,256]{2,1,0:T(8,128)(2,1)S(1)} collective-permute-done((bf16[8,64,256]{2,1,0:T(8,128)(2,1)S(1)}, bf16[8,64,256]{2,1,0:T(8,128)(2,1)S(1)}, u32[]{:S(2)}, u32[]{:S(2)}) %collective-permute-start.6) | collective-permute-done | bytes 262176 | tf_op jit(solution)/shard_map/ppermute | solution.py:211
  30.5 8.1 %shard_map.86 = (bf16[2,8,64,256]{3,2,1,0:T(8,128)(2,1)}, bf16[4,8,64,256]{3,2,1,0:T(8,128)(2,1)}, bf16[2,8,64,256]{3,2,1,0:T(8,128)(2,1)}, bf16[4,8,64,256]{3,2...) custom-call(bf16[8,64,256]{2,1,0:T(8,128)(2,1)} %bitcast.30, ...), custom_call_target="tpu_custom_call" | custom-call | flops 1342177280 | bytes 10748164 | tf_op jit(solution)/shard_map/pallas_call | solution.py:25
  39.4 1.5 %collective-permute-done.11 = bf16[2,8,64,256]{3,2,1,0:T(8,128)(2,1)S(1)} collective-permute-done((bf16[2,8,64,256]{3,2,1,0:T(8,128)(2,1)}, bf16[2,8,64,256]{3,2,1,0:T(8,128)(2,1)S(1)}, u32[]{:S(2)}, u32[]{:S(2)}) %collective-permute-start.11) | collective-permute-done | bytes 524320 | tf_op jit(solution)/shard_map/ppermute | solution.py:211
  40.9 1.2 %fusion.5 = (bf16[8,64,256]{2,1,0:T(8,128)(2,1)S(1)}, bf16[8,64,256]{2,1,0:T(8,128)(2,1)S(1)}) fusion(bf16[2,8,64,256]{3,2,1,0:T(8,128)(2,1)S(1)} %collective-permute-done.11, bf16[2,8,64,256]{3,2,1,0:T(8,128)(2,1)} %get-tuple-element.43), kind=kLoop, calls=%fused_computation.12 | loop fusion | flops 1048576 | bytes 1572864 | tf_op jit(solution)/shard_map/convert_element_type | solution.py:325
  44.4 1.5 %collective-permute-start.16 = (f32[64,256]{1,0:T(8,128)S(1)}, f32[64,256]{1,0:T(8,128)S(1)}, u32[]{:S(2)}, u32[]{:S(2)}) collective-permute-start(f32[64,256]{1,0:T(8,128)S(1)} %get-tuple-element.52), channel_id=1, source_target_pairs={{0,16},{1,17},{2,18},{3,19},{16,0},{17,1},{18,2},{19,3},{4,20},{5,... | collective-permute-start | bytes 196616 | tf_op jit(solution)/shard_map/ppermute | solution.py:300
  45.9 1.5 %collective-permute-start.17 = (f32[64,256]{1,0:T(8,128)S(1)}, f32[64,256]{1,0:T(8,128)S(1)}, u32[]{:S(2)}, u32[]{:S(2)}) collective-permute-start(f32[64,256]{1,0:T(8,128)S(1)} %get-tuple-element.53), channel_id=1, source_target_pairs={{0,18},{1,19},{2,16},{3,17},{16,2},{17,3},{18,0},{19,1},{4,22},{5,... | collective-permute-start | bytes 196616 | tf_op jit(solution)/shard_map/ppermute | solution.py:300
  48.2 1.3 %collective-permute-start.14 = (bf16[8,64,256]{2,1,0:T(8,128)(2,1)S(1)}, bf16[8,64,256]{2,1,0:T(8,128)(2,1)S(1)}, u32[]{:S(2)}, u32[]{:S(2)}) collective-permute-start(bf16[8,64,256]{2,1,0:T(8,128)(2,1)S(1)} %get-tuple-element.47), channel_id=1, source_target_pairs={{0,2},{1,3},{2,0},{3,1},{4,6},{5,7},{6,4},{7,5},{8,10},{9,11},{10,... | collective-permute-start | bytes 786440 | tf_op jit(solution)/shard_map/ppermute | solution.py:211
  49.4 1.7 %collective-permute-done.17 = f32[64,256]{1,0:T(8,128)S(1)} collective-permute-done((f32[64,256]{1,0:T(8,128)S(1)}, f32[64,256]{1,0:T(8,128)S(1)}, u32[]{:S(2)}, u32[]{:S(2)}) %collective-permute-start.17) | collective-permute-done | bytes 65568 | tf_op jit(solution)/shard_map/ppermute | solution.py:300
  51.7 3.8 %collective-permute-done.18 = f32[64,256]{1,0:T(8,128)S(1)} collective-permute-done((f32[64,256]{1,0:T(8,128)S(1)}, f32[64,256]{1,0:T(8,128)S(1)}, u32[]{:S(2)}, u32[]{:S(2)}) %collective-permute-start.18) | collective-permute-done | bytes 65568 | tf_op jit(solution)/shard_map/ppermute | solution.py:211
  55.5 2.4 %collective-permute-start.19 = (f32[64,256]{1,0:T(8,128)S(1)}, f32[64,256]{1,0:T(8,128)S(1)}, u32[]{:S(2)}, u32[]{:S(2)}) collective-permute-start(f32[64,256]{1,0:T(8,128)S(1)} %add.78), channel_id=1, source_target_pairs={{0,8},{4,12},{8,0},{12,4},{1,9},{5,13},{9,1},{13,5},{2,10},{6,14},... | collective-permute-start | bytes 196616 | tf_op jit(solution)/shard_map/ppermute | solution.py:211
  58.0 2.8 %collective-permute-done.19 = f32[64,256]{1,0:T(8,128)S(1)} collective-permute-done((f32[64,256]{1,0:T(8,128)S(1)}, f32[64,256]{1,0:T(8,128)S(1)}, u32[]{:S(2)}, u32[]{:S(2)}) %collective-permute-start.19) | collective-permute-done | bytes 65568 | tf_op jit(solution)/shard_map/ppermute | solution.py:211
  64.3 3.9 %collective-permute-start.26 = (bf16[8,64,256]{2,1,0:T(8,128)(2,1)}, bf16[8,64,256]{2,1,0:T(8,128)(2,1)S(1)}, u32[]{:S(2)}, u32[]{:S(2)}) collective-permute-start(bf16[8,64,256]{2,1,0:T(8,128)(2,1)} %get-tuple-element.61), channel_id=1, source_target_pairs={{4,0},{8,4},{12,8},{0,12},{5,1},{9,5},{13,9},{1,13},{6,2},{10,6},{... | collective-permute-start | bytes 786440 | tf_op jit(solution)/shard_map/ppermute | solution.py:225
  68.1 1.3 %collective-permute-start.21 = (f32[64,256]{1,0:T(8,128)S(1)}, f32[64,256]{1,0:T(8,128)S(1)}, u32[]{:S(2)}, u32[]{:S(2)}) collective-permute-start(f32[64,256]{1,0:T(8,128)S(1)} %add.79.refs_0_), channel_id=1, source_target_pairs={{0,2},{1,3},{2,0},{3,1},{16,18},{17,19},{18,16},{19,17},{4,6},{5,7... | collective-permute-start | bytes 196616 | tf_op jit(solution)/shard_map/ppermute | solution.py:300
  70.5 1.9 %collective-permute-done.21.refs_1_ = f32[64,256]{1,0:T(8,128)S(1)} collective-permute-done((f32[64,256]{1,0:T(8,128)S(1)}, f32[64,256]{1,0:T(8,128)S(1)}, u32[]{:S(2)}, u32[]{:S(2)}) %collective-permute-start.21) | collective-permute-done | bytes 65568 | tf_op jit(solution)/shard_map/ppermute | solution.py:300
  72.4 1.8 %collective-permute-start.23 = (f32[64,256]{1,0:T(8,128)S(1)}, f32[64,256]{1,0:T(8,128)S(1)}, u32[]{:S(2)}, u32[]{:S(2)}) collective-permute-start(f32[64,256]{1,0:T(8,128)S(1)} %add.79.refs_0_), channel_id=1, source_target_pairs={{0,18},{1,19},{2,16},{3,17},{16,2},{17,3},{18,0},{19,1},{4,22},{5,... | collective-permute-start | bytes 196616 | tf_op jit(solution)/shard_map/ppermute | solution.py:300
  74.2 3.4 %collective-permute-done.23.refs_3_ = f32[64,256]{1,0:T(8,128)S(1)} collective-permute-done((f32[64,256]{1,0:T(8,128)S(1)}, f32[64,256]{1,0:T(8,128)S(1)}, u32[]{:S(2)}, u32[]{:S(2)}) %collective-permute-start.23) | collective-permute-done | bytes 65568 | tf_op jit(solution)/shard_map/ppermute | solution.py:300
  77.8 1.5 %collective-permute-done.27 = bf16[8,64,256]{2,1,0:T(8,128)(2,1)} collective-permute-done((bf16[8,64,256]{2,1,0:T(8,128)(2,1)}, bf16[8,64,256]{2,1,0:T(8,128)(2,1)}, u32[]{:S(2)}, u32[]{:S(2)}) %collective-permute-start.27) | collective-permute-done | bytes 262176 | tf_op jit(solution)/shard_map/ppermute | solution.py:221
  (76 shorter events, 15.5 us)
Async XLA Ops:
  1.7 12.2 %collective-permute-start.7 = (bf16[8,64,256]{2,1,0:T(8,128)(2,1)S(1)}, bf16[8,64,256]{2,1,0:T(8,128)(2,1)S(1)}, u32[]{:S(2)}, u32[]{:S(2)}) collective-permute-start(bf16[8,64,256]{2,1,0:T(8,128)(2,1)S(1)} %bitcast.26), channel_id=1, source_target_pairs={{4,0},{8,4},{12,8},{0,12},{5,1},{9,5},{13,9},{1,13},{6,2},{10,6},{... | collective-permute-start | bytes 786440 | tf_op jit(solution)/shard_map/ppermute | solution.py:225
  6.8 12.1 %collective-permute-start.3 = (bf16[8,64,256]{2,1,0:T(8,128)(2,1)S(1)}, bf16[8,64,256]{2,1,0:T(8,128)(2,1)S(1)}, u32[]{:S(2)}, u32[]{:S(2)}) collective-permute-start(bf16[8,64,256]{2,1,0:T(8,128)(2,1)S(1)} %bitcast.27), channel_id=1, source_target_pairs={{0,4},{4,8},{8,12},{12,0},{1,5},{5,9},{9,13},{13,1},{2,6},{6,10},{... | collective-permute-start | bytes 786440 | tf_op jit(solution)/shard_map/ppermute | solution.py:221
  6.8 13.6 %collective-permute-start.1 = (bf16[8,64,256]{2,1,0:T(8,128)(2,1)S(1)}, bf16[8,64,256]{2,1,0:T(8,128)(2,1)S(1)}, u32[]{:S(2)}, u32[]{:S(2)}) collective-permute-start(bf16[8,64,256]{2,1,0:T(8,128)(2,1)S(1)} %bitcast.28), channel_id=1, source_target_pairs={{0,2},{1,3},{2,0},{3,1},{4,6},{5,7},{6,4},{7,5},{8,10},{9,11},{10,... | collective-permute-start | bytes 786440 | tf_op jit(solution)/shard_map/ppermute | solution.py:211
  8.3 12.6 %collective-permute-start = (bf16[8,64,256]{2,1,0:T(8,128)(2,1)S(1)}, bf16[8,64,256]{2,1,0:T(8,128)(2,1)S(1)}, u32[]{:S(2)}, u32[]{:S(2)}) collective-permute-start(bf16[8,64,256]{2,1,0:T(8,128)(2,1)S(1)} %bitcast.29), channel_id=1, source_target_pairs={{0,1},{1,0},{2,3},{3,2},{4,5},{5,4},{6,7},{7,6},{8,9},{9,8},{10,11... | collective-permute-start | bytes 786440 | tf_op jit(solution)/shard_map/ppermute | solution.py:211
  13.9 9.2 %collective-permute-start.9 = (bf16[8,64,256]{2,1,0:T(8,128)(2,1)S(1)}, bf16[8,64,256]{2,1,0:T(8,128)(2,1)S(1)}, u32[]{:S(2)}, u32[]{:S(2)}) collective-permute-start(bf16[8,64,256]{2,1,0:T(8,128)(2,1)S(1)} %collective-permute-done.7.refs_8_), channel_id=1, source_target_pairs={{0,2},{1,3},{2,0},{3,1},{4,6},{5,7},{6,4},{7,5},{8,10},{9,11},{10,... | collective-permute-start | bytes 786440 | tf_op jit(solution)/shard_map/ppermute | solution.py:211
  18.9 9.4 %collective-permute-start.5 = (bf16[8,64,256]{2,1,0:T(8,128)(2,1)S(1)}, bf16[8,64,256]{2,1,0:T(8,128)(2,1)S(1)}, u32[]{:S(2)}, u32[]{:S(2)}) collective-permute-start(bf16[8,64,256]{2,1,0:T(8,128)(2,1)S(1)} %collective-permute-done.3.refs_4_), channel_id=1, source_target_pairs={{0,2},{1,3},{2,0},{3,1},{4,6},{5,7},{6,4},{7,5},{8,10},{9,11},{10,... | collective-permute-start | bytes 786440 | tf_op jit(solution)/shard_map/ppermute | solution.py:211
  20.4 7.9 %collective-permute-start.4 = (bf16[8,64,256]{2,1,0:T(8,128)(2,1)S(1)}, bf16[8,64,256]{2,1,0:T(8,128)(2,1)S(1)}, u32[]{:S(2)}, u32[]{:S(2)}) collective-permute-start(bf16[8,64,256]{2,1,0:T(8,128)(2,1)S(1)} %collective-permute-done.3.refs_4_), channel_id=1, source_target_pairs={{0,1},{1,0},{2,3},{3,2},{4,5},{5,4},{6,7},{7,6},{8,9},{9,8},{10,11... | collective-permute-start | bytes 786440 | tf_op jit(solution)/shard_map/ppermute | solution.py:211
  20.4 7.9 %collective-permute-start.8 = (bf16[8,64,256]{2,1,0:T(8,128)(2,1)S(1)}, bf16[8,64,256]{2,1,0:T(8,128)(2,1)S(1)}, u32[]{:S(2)}, u32[]{:S(2)}) collective-permute-start(bf16[8,64,256]{2,1,0:T(8,128)(2,1)S(1)} %collective-permute-done.7.refs_8_), channel_id=1, source_target_pairs={{0,1},{1,0},{2,3},{3,2},{4,5},{5,4},{6,7},{7,6},{8,9},{9,8},{10,11... | collective-permute-start | bytes 786440 | tf_op jit(solution)/shard_map/ppermute | solution.py:211
  20.9 7.4 %collective-permute-start.2 = (bf16[8,64,256]{2,1,0:T(8,128)(2,1)S(1)}, bf16[8,64,256]{2,1,0:T(8,128)(2,1)S(1)}, u32[]{:S(2)}, u32[]{:S(2)}) collective-permute-start(bf16[8,64,256]{2,1,0:T(8,128)(2,1)S(1)} %collective-permute-done.1.refs_2_), channel_id=1, source_target_pairs={{0,1},{1,0},{2,3},{3,2},{4,5},{5,4},{6,7},{7,6},{8,9},{9,8},{10,11... | collective-permute-start | bytes 786440 | tf_op jit(solution)/shard_map/ppermute | solution.py:211
  23.1 5.3 %collective-permute-start.10 = (bf16[8,64,256]{2,1,0:T(8,128)(2,1)S(1)}, bf16[8,64,256]{2,1,0:T(8,128)(2,1)S(1)}, u32[]{:S(2)}, u32[]{:S(2)}) collective-permute-start(bf16[8,64,256]{2,1,0:T(8,128)(2,1)S(1)} %collective-permute-done.9.refs_10_), channel_id=1, source_target_pairs={{0,1},{1,0},{2,3},{3,2},{4,5},{5,4},{6,7},{7,6},{8,9},{9,8},{10,11... | collective-permute-start | bytes 786440 | tf_op jit(solution)/shard_map/ppermute | solution.py:211
  38.9 22.9 %collective-permute-start.20 = (bf16[4,8,64,256]{3,2,1,0:T(8,128)(2,1)}, bf16[4,8,64,256]{3,2,1,0:T(8,128)(2,1)S(1)}, u32[]{:S(2)}, u32[]{:S(2)}) collective-permute-start(bf16[4,8,64,256]{3,2,1,0:T(8,128)(2,1)} %get-tuple-element.54), channel_id=1, source_target_pairs={{0,1},{1,0},{2,3},{3,2},{4,5},{5,4},{6,7},{7,6},{8,9},{9,8},{10,11... | collective-permute-start | bytes 3145736 | tf_op jit(solution)/shard_map/ppermute | solution.py:211
  43.9 4.3 %collective-permute-start.15 = (f32[64,256]{1,0:T(8,128)S(1)}, f32[64,256]{1,0:T(8,128)S(1)}, u32[]{:S(2)}, u32[]{:S(2)}) collective-permute-start(f32[64,256]{1,0:T(8,128)S(1)} %get-tuple-element.51), channel_id=1, source_target_pairs={{0,2},{1,3},{2,0},{3,1},{16,18},{17,19},{18,16},{19,17},{4,6},{5,7... | collective-permute-start | bytes 196616 | tf_op jit(solution)/shard_map/ppermute | solution.py:300
  44.4 5.0 %collective-permute-start.16 = (f32[64,256]{1,0:T(8,128)S(1)}, f32[64,256]{1,0:T(8,128)S(1)}, u32[]{:S(2)}, u32[]{:S(2)}) collective-permute-start(f32[64,256]{1,0:T(8,128)S(1)} %get-tuple-element.52), channel_id=1, source_target_pairs={{0,16},{1,17},{2,18},{3,19},{16,0},{17,1},{18,2},{19,3},{4,20},{5,... | collective-permute-start | bytes 196616 | tf_op jit(solution)/shard_map/ppermute | solution.py:300
  45.9 5.2 %collective-permute-start.17 = (f32[64,256]{1,0:T(8,128)S(1)}, f32[64,256]{1,0:T(8,128)S(1)}, u32[]{:S(2)}, u32[]{:S(2)}) collective-permute-start(f32[64,256]{1,0:T(8,128)S(1)} %get-tuple-element.53), channel_id=1, source_target_pairs={{0,18},{1,19},{2,16},{3,17},{16,2},{17,3},{18,0},{19,1},{4,22},{5,... | collective-permute-start | bytes 196616 | tf_op jit(solution)/shard_map/ppermute | solution.py:300
  47.4 13.4 %collective-permute-start.13 = (bf16[8,64,256]{2,1,0:T(8,128)(2,1)S(1)}, bf16[8,64,256]{2,1,0:T(8,128)(2,1)S(1)}, u32[]{:S(2)}, u32[]{:S(2)}) collective-permute-start(bf16[8,64,256]{2,1,0:T(8,128)(2,1)S(1)} %get-tuple-element.46), channel_id=1, source_target_pairs={{0,2},{1,3},{2,0},{3,1},{4,6},{5,7},{6,4},{7,5},{8,10},{9,11},{10,... | collective-permute-start | bytes 786440 | tf_op jit(solution)/shard_map/ppermute | solution.py:211
  48.2 13.6 %collective-permute-start.14 = (bf16[8,64,256]{2,1,0:T(8,128)(2,1)S(1)}, bf16[8,64,256]{2,1,0:T(8,128)(2,1)S(1)}, u32[]{:S(2)}, u32[]{:S(2)}) collective-permute-start(bf16[8,64,256]{2,1,0:T(8,128)(2,1)S(1)} %get-tuple-element.47), channel_id=1, source_target_pairs={{0,2},{1,3},{2,0},{3,1},{4,6},{5,7},{6,4},{7,5},{8,10},{9,11},{10,... | collective-permute-start | bytes 786440 | tf_op jit(solution)/shard_map/ppermute | solution.py:211
  51.2 4.3 %collective-permute-start.18 = (f32[64,256]{1,0:T(8,128)S(1)}, f32[64,256]{1,0:T(8,128)S(1)}, u32[]{:S(2)}, u32[]{:S(2)}) collective-permute-start(f32[64,256]{1,0:T(8,128)S(1)} %add_add_fusion), channel_id=1, source_target_pairs={{0,4},{4,0},{8,12},{12,8},{1,5},{5,1},{9,13},{13,9},{2,6},{6,2},{1... | collective-permute-start | bytes 196616 | tf_op jit(solution)/shard_map/ppermute | solution.py:211
  55.5 5.2 %collective-permute-start.19 = (f32[64,256]{1,0:T(8,128)S(1)}, f32[64,256]{1,0:T(8,128)S(1)}, u32[]{:S(2)}, u32[]{:S(2)}) collective-permute-start(f32[64,256]{1,0:T(8,128)S(1)} %add.78), channel_id=1, source_target_pairs={{0,8},{4,12},{8,0},{12,4},{1,9},{5,13},{9,1},{13,5},{2,10},{6,14},... | collective-permute-start | bytes 196616 | tf_op jit(solution)/shard_map/ppermute | solution.py:211
  62.6 15.2 %collective-permute-start.25 = (bf16[8,64,256]{2,1,0:T(8,128)(2,1)}, bf16[8,64,256]{2,1,0:T(8,128)(2,1)S(1)}, u32[]{:S(2)}, u32[]{:S(2)}) collective-permute-start(bf16[8,64,256]{2,1,0:T(8,128)(2,1)} %fusion.6), channel_id=1, source_target_pairs={{0,2},{1,3},{2,0},{3,1},{4,6},{5,7},{6,4},{7,5},{8,10},{9,11},{10,... | collective-permute-start | bytes 786440 | tf_op jit(solution)/shard_map/ppermute | solution.py:211
  64.3 13.5 %collective-permute-start.26 = (bf16[8,64,256]{2,1,0:T(8,128)(2,1)}, bf16[8,64,256]{2,1,0:T(8,128)(2,1)S(1)}, u32[]{:S(2)}, u32[]{:S(2)}) collective-permute-start(bf16[8,64,256]{2,1,0:T(8,128)(2,1)} %get-tuple-element.61), channel_id=1, source_target_pairs={{4,0},{8,4},{12,8},{0,12},{5,1},{9,5},{13,9},{1,13},{6,2},{10,6},{... | collective-permute-start | bytes 786440 | tf_op jit(solution)/shard_map/ppermute | solution.py:225
  68.1 11.1 %collective-permute-start.27 = (bf16[8,64,256]{2,1,0:T(8,128)(2,1)}, bf16[8,64,256]{2,1,0:T(8,128)(2,1)}, u32[]{:S(2)}, u32[]{:S(2)}) collective-permute-start(bf16[8,64,256]{2,1,0:T(8,128)(2,1)} %get-tuple-element.62), channel_id=1, source_target_pairs={{0,4},{4,8},{8,12},{12,0},{1,5},{5,9},{9,13},{13,1},{2,6},{6,10},{... | collective-permute-start | bytes 786440 | tf_op jit(solution)/shard_map/ppermute | solution.py:221
  68.1 4.3 %collective-permute-start.21 = (f32[64,256]{1,0:T(8,128)S(1)}, f32[64,256]{1,0:T(8,128)S(1)}, u32[]{:S(2)}, u32[]{:S(2)}) collective-permute-start(f32[64,256]{1,0:T(8,128)S(1)} %add.79.refs_0_), channel_id=1, source_target_pairs={{0,2},{1,3},{2,0},{3,1},{16,18},{17,19},{18,16},{19,17},{4,6},{5,7... | collective-permute-start | bytes 196616 | tf_op jit(solution)/shard_map/ppermute | solution.py:300
  69.4 4.8 %collective-permute-start.22 = (f32[64,256]{1,0:T(8,128)S(1)}, f32[64,256]{1,0:T(8,128)S(1)}, u32[]{:S(2)}, u32[]{:S(2)}) collective-permute-start(f32[64,256]{1,0:T(8,128)S(1)} %add.79.refs_0_), channel_id=1, source_target_pairs={{0,16},{1,17},{2,18},{3,19},{16,0},{17,1},{18,2},{19,3},{4,20},{5,... | collective-permute-start | bytes 196616 | tf_op jit(solution)/shard_map/ppermute | solution.py:300
  72.4 5.2 %collective-permute-start.23 = (f32[64,256]{1,0:T(8,128)S(1)}, f32[64,256]{1,0:T(8,128)S(1)}, u32[]{:S(2)}, u32[]{:S(2)}) collective-permute-start(f32[64,256]{1,0:T(8,128)S(1)} %add.79.refs_0_), channel_id=1, source_target_pairs={{0,18},{1,19},{2,16},{3,17},{16,2},{17,3},{18,0},{19,1},{4,22},{5,... | collective-permute-start | bytes 196616 | tf_op jit(solution)/shard_map/ppermute | solution.py:300
  (19 other events, 141.4 us)

commit v3 on v2

--- a/solution.py
+++ b/solution.py
@@ -52,7 +52,7 @@
 
 def prepare_body(
     edge_hbm, feat_hbm, self_hbm, neigh_hbm, label_ref,
-    wide_ref, tall_ref, inverse_ref, logit_ref, label_out, feat_out, weight_out,
+    wide_ref, inverse_ref, logit_ref, label_out, feat_out, weight_out,
     edge_ref, feat_ref, self_ref, neigh_ref, sems,
 ):
     blocks, slots = edge_ref.shape[:2]
@@ -68,12 +68,11 @@
     lines = label_ref.shape[0]
     columns = jnp.concatenate([label_ref[...].astype(F32), jnp.zeros((8 - lines % 8, 128), F32)], axis=0).T
     for r in range(lines):
-        label_out[r * 128 : (r + 1) * 128] = jnp.broadcast_to(columns[:, r : r + 1], (128, 128))
+        label_out[r * 128 : (r + 1) * 128] = jnp.broadcast_to(columns[:, r : r + 1], (128, 128)).astype(BF16)
     for b in range(blocks):
         tiles[b].wait()
         wide = jnp.concatenate([edge_ref[b, s].astype(F32) for s in range(slots)], axis=1)
         wide_ref[b] = wide.astype(BF16)
-        tall_ref[b] = wide.T.astype(BF16)
         degree = jnp.sum(wide, axis=1, keepdims=True)
         inverse_ref[b] = jnp.broadcast_to(1.0 / degree, inverse_ref.shape[1:])
     for c in dense:
@@ -88,11 +87,13 @@
 
 def layer_body(*refs):
     pieces, refs = refs[:12], refs[12:]
-    place_ref, source_ref, refs = refs[0], refs[1], refs[2:]
-    inputs, outputs, refs = refs[:7], refs[7:14], refs[14:]
-    table, held, made, refs = refs[0], refs[1:8], refs[8:15], refs[15:]
-    mean, terms, index, piece_sems, in_sems, out_sems = refs
-    wide_ref, inverse_ref, logit_ref, label_ref, weight_ref, tall_ref, feat_ref = held
+    source_hbm, refs = refs[0], refs[1:]
+    inputs, outputs, refs = refs[:6], refs[6:13], refs[13:]
+    table, held, made, refs = refs[0], refs[1:7], refs[7:14], refs[14:]
+    mean, terms, source_ref, source_sem, piece_sems, in_sems, out_sems = refs
+    sources = pltpu.make_async_copy(source_hbm, source_ref, source_sem)
+    sources.start()
+    wide_ref, inverse_ref, logit_ref, label_ref, weight_ref, feat_ref = held
     direct_ref, mine_ref, passed_ref = made[4:]
     per = pieces[0].shape[0]
     copies = [
@@ -110,17 +111,17 @@
 
     blocks, rows, wide_cols = wide_ref.shape
     slots = wide_cols // BLOCK
-    me = place_ref[0]
+    me = lax.axis_index("rep")
+
+    def named(b, s):
+        return source_ref[b, s] ^ (me * blocks)
+
+    terms[...] = jnp.zeros_like(terms)
+    for c in [sources] + loads[:1] + copies + loads[1:2]:
+        c.wait()
 
     for b in range(blocks):
-        for s in range(slots):
-            index[b, s] = source_ref[b, s] ^ (me * blocks)
-    terms[...] = jnp.zeros_like(terms)
-    for c in loads[:1] + copies + loads[1:2]:
-        c.wait()
-
-    for b in range(blocks):
-        gathered = jnp.concatenate([table[index[b, s]] for s in range(slots)], axis=0)
+        gathered = jnp.concatenate([table[named(b, s)] for s in range(slots)], axis=0)
         total = dot(wide_ref[b], gathered)
         mean[b * rows : (b + 1) * rows] = total * wider(inverse_ref[b])
 
@@ -130,7 +131,7 @@
     mean_parts = halves(mean[...])
     logits = logit_ref[...] + dot3(mean_parts, neigh)
     classes = lax.broadcasted_iota(jnp.int32, logits.shape, 1).astype(F32)
-    target = jnp.where(classes == wider(label_ref[...]), 1.0, 0.0)
+    target = jnp.where(classes == wider(label_ref[...].astype(F32)), 1.0, 0.0)
     residual = halves(1.0 / (1.0 + jnp.exp(-logits)) - target)
     inverse = inverse_ref[...].reshape(blocks * rows, 128)
     spread = (dot3(residual, neigh_t) * wider(inverse)).astype(BF16)
@@ -140,9 +141,9 @@
     for c in loads[5:]:
         c.wait()
     for b in range(blocks):
-        contrib = dot(tall_ref[b], spread[b * rows : (b + 1) * rows])
+        contrib = dot(wide_ref[b], spread[b * rows : (b + 1) * rows], ROWS_BOTH)
         for s in range(slots):
-            at = index[b, s]
+            at = named(b, s)
             terms[at] = terms[at] + contrib[s * BLOCK : (s + 1) * BLOCK]
 
     count = 1
@@ -166,6 +167,10 @@
         c.wait()
 
 
+def own_body(direct_ref, keep_ref, got_ref, out_ref):
+    out_ref[...] = direct_ref[...] + (keep_ref[3].astype(F32) + got_ref[3].astype(F32))
+
+
 def split_body(place_ref, *refs):
     outs = [r for r in refs if r.shape != refs[0].shape]
     total = tree_sum(r[...] for r in refs[: len(refs) - len(outs)])
@@ -232,16 +237,15 @@
         prepare_body,
         (
             shape((blocks, BLOCK, wide_cols), BF16),
-            shape((blocks, wide_cols, BLOCK), BF16),
             shape((blocks, BLOCK, 128), F32),
             shape((rows, classes), F32),
-            shape((rows, 128), F32),
+            shape((rows, 128), BF16),
             shape((2, width, rows), BF16),
             shape((6, width, classes), BF16),
         ),
         (edge_weights, features, self_weight, neigh_weight, labels.reshape(rows // 128, 128)),
         [ANY] * 4 + [VMEM],
-        [VMEM] * 7,
+        [VMEM] * 6,
         scratch=[
             pltpu.VMEM(edge_weights.shape, jnp.int32),
             pltpu.VMEM(features.shape, F32),
@@ -251,7 +255,7 @@
         ],
         flops=6 * rows * width * classes,
     )
-    wide, tall, inverse, self_logits, label_cols, feat_parts, weight_parts = prepared
+    wide, inverse, self_logits, label_cols, feat_parts, weight_parts = prepared
     half, lower, upper, core = (lax.optimization_barrier((x, inverse))[0] for x in (half, lower, upper, core))
     lower_half, upper_half = half_swap(lower), half_swap(upper)
     pieces = [
@@ -263,7 +267,7 @@
     def piece_shape(*lead):
         return shape((*lead, blocks, BLOCK, width), BF16)
 
-    inputs = (wide, inverse, self_logits, label_cols, weight_parts, tall, feat_parts)
+    inputs = (wide, inverse, self_logits, label_cols, weight_parts, feat_parts)
     outputs = (
         piece_shape(2), piece_shape(4), piece_shape(2), piece_shape(4),
         shape((rows, width), F32), shape((width, classes), F32), shape((width, classes), F32),
@@ -271,8 +275,8 @@
     keep_near, keep_rest, send_near, send_rest, direct, mine, passed = call(
         layer_body,
         outputs,
-        (*pieces, me.reshape(1), block_source, *inputs),
-        [ANY] * 12 + [SMEM] * 2 + [ANY] * 7,
+        (*pieces, block_source, *inputs),
+        [ANY] * 19,
         [ANY] * 7,
         scratch=[
             pltpu.VMEM((12 * blocks, BLOCK, width), BF16),
@@ -280,8 +284,9 @@
             pltpu.VMEM((rows, width), F32),
             pltpu.VMEM((12 * blocks, BLOCK, width), F32),
             pltpu.SMEM((blocks, slots), jnp.int32),
+            pltpu.SemaphoreType.DMA(()),
             pltpu.SemaphoreType.DMA((12,)),
-            pltpu.SemaphoreType.DMA((7,)),
+            pltpu.SemaphoreType.DMA((6,)),
             pltpu.SemaphoreType.DMA((15,)),
         ],
         flops=40 * rows * width * classes,
@@ -292,61 +297,64 @@
         return a.astype(F32) + b.astype(F32)
 
     lines, cols = lax.axis_size("row"), lax.axis_size("col")
-    group = lines * reps // 2
-    place = lax.axis_index("row").astype(jnp.int32) * (reps // 2) + me // 2
-
-    def to_group(x, d):
-        pairs = [(g * 2 + c, (g ^ d) * 2 + c) for g in range(group) for c in range(2)]
-        return lax.ppermute(x, ("row", "rep"), pairs)
+    line = lax.axis_index("row").astype(jnp.int32).reshape(1)
 
     def split(parts):
-        chunk = shape((parts[0].shape[0] // group, classes), F32)
+        chunk = shape((parts[0].shape[0] // lines, classes), F32)
         return call(
             split_body,
-            (chunk,) * group,
-            (place.reshape(1), *parts),
+            (chunk,) * lines,
+            (line, *parts),
             [SMEM] + [VMEM] * len(parts),
-            [VMEM] * group,
+            [VMEM] * lines,
             vmem=4,
         )
 
     def join(chunk):
-        parts = [chunk] + [to_group(chunk, d) for d in range(1, group)]
+        parts = [chunk] + [swap(chunk, "row", d) for d in range(1, lines)]
         (out,) = call(
             join_body,
-            (shape((chunk.shape[0] * group, classes), F32),),
-            (place.reshape(1), *parts),
-            [SMEM] + [VMEM] * group,
+            (shape((chunk.shape[0] * lines, classes), F32),),
+            (line, *parts),
+            [SMEM] + [VMEM] * lines,
             [VMEM],
             vmem=4,
         )
         return out
 
-    near = [both(keep_near[k], got_near[k]).astype(BF16) for k in range(2)]
-    near, got = lax.optimization_barrier((near, got))
-    half_near = [half_swap(x) for x in near]
+    def together(*values):
+        return lax.optimization_barrier(values)
+
+    near, got = together(both(keep_near, got_near).astype(BF16), got)
+    half_near = half_swap(near)
     chunks = split((mine, got))
-    part = tree_sum([chunks[0]] + [to_group(c, d) for d, c in enumerate(chunks) if d])
+    part = tree_sum([chunks[0]] + [swap(c.astype(BF16), "row", d).astype(F32) for d, c in enumerate(chunks) if d])
     step = 1
     while step < cols:
         part = part + swap(part, "col", step)
         step *= 2
-    half_near, part, got_rest = lax.optimization_barrier((half_near, part, got_rest))
+    half_near, part, got_rest = together(half_near, part, got_rest)
 
     near = [both(keep_rest[1 + k], got_rest[1 + k]) + half_near[k].astype(F32) for k in range(2)]
     from_upper = down(near[0].astype(BF16))
     from_lower = up(near[1].astype(BF16))
+    part = part + half_swap(part)
+    whole = join(part)
     half_own = half_swap(both(keep_rest[0], got_rest[0]).astype(BF16))
-    whole = join(part)
     other = core_swap(whole)
     first = me % 2 == 0
     grad_self = jnp.where(first, whole, other)
     grad_neigh = jnp.where(first, other, whole)
 
-    own_terms = both(keep_rest[3], got_rest[3]) + half_own.astype(F32)
-    own_terms = own_terms + from_upper.astype(F32) + from_lower.astype(F32)
-    grad_features = direct + own_terms.reshape(rows, width)
-    return grad_self, grad_neigh, grad_features
+    (own_terms,) = call(
+        own_body,
+        (shape((blocks, BLOCK, width), F32),),
+        (direct.reshape(blocks, BLOCK, width), keep_rest, got_rest),
+        [VMEM] * 3,
+        [VMEM],
+    )
+    grad_features = own_terms + half_own.astype(F32) + both(from_upper, from_lower)
+    return grad_self, grad_neigh, grad_features.reshape(rows, width)
 
 
 def solution(mesh):

time: 82.4 us -> 78.3 us (0.950)
  starting transfers between devices: 27.7 us -> 23.1 us
  other arithmetic: 6.88 us -> 5.48 us
  waiting for transfers between devices: 31.1 us -> 32.3 us
    ppermute x6 -> x0, starting transfers between devices: 7.71 us -> none  [to_group(): return lax.ppermute(x, ('row', 'rep'), pairs)]
    ppermute x6 -> x0, waiting for transfers between devices: 7.25 us -> none  [to_group(): return lax.ppermute(x, ('row', 'rep'), pairs)]
    ppermute x18 -> x20, waiting for transfers between devices: 18.5 us -> 22.9 us  [swap(): lax.ppermute(x, axis, [(i, i ^ d) for i in range(lax.axis_size(axis))])]
    ppermute x18 -> x20, starting transfers between devices: 11 us -> 14.4 us  [swap(): lax.ppermute(x, axis, [(i, i ^ d) for i in range(lax.axis_size(axis))])]
    ppermute x2, waiting for transfers between devices: 5.36 us -> 7.4 us  [up(): return lax.ppermute(x, 'col', [(i, (i + 1) % cols) for i in range(cols)])]
    ppermute x2, waiting for transfers between devices: 0.01 us -> 2 us  [down(): return lax.ppermute(x, 'col', [((i + 1) % cols, i) for i in range(cols)])]
    pallas_call x4 -> x5, Pallas kernels: 13.9 us -> 14.5 us  [call(): pl.pallas_call(body, out_shape=out_shape, in_specs=in_specs, out_specs=ou...]
  transfers between devices with their start and end apart: 28 -> 24, of which waited for: 14 -> 13; matrix products, arithmetic and copies ran while one was open for 5% -> 5% of each run, Pallas kernels for 7% -> 10%
where the time goes in v3:
time: 78.3 us; the launch traced here: 77.9 us
  waiting for transfers between devices  32.3 us (41%)
  starting transfers between devices  23.1 us (30%)
  Pallas kernels  14.5 us (19%)
  other arithmetic  5.48 us (7%)
  local copies, waits for them, and re-layouts  1.6 us (2%)
  between operations  0.91 us (1%)
    ppermute x20, waiting for transfers between devices, swap(): lax.ppermute(x, axis, [(i, i ^ d) for i in range(lax.axis_size(axis))])  22.9 us
    pallas_call x5, Pallas kernels, call(): pl.pallas_call(body, out_shape=out_shape, in_specs=in_specs, out_specs=ou...  14.5 us
    ppermute x20, starting transfers between devices, swap(): lax.ppermute(x, axis, [(i, i ^ d) for i in range(lax.axis_size(axis))])  14.4 us
    ppermute x2, starting transfers between devices, down(): return lax.ppermute(x, 'col', [((i + 1) % cols, i) for i in range(cols)])  8.62 us
    ppermute x2, waiting for transfers between devices, up(): return lax.ppermute(x, 'col', [(i, (i + 1) % cols) for i in range(cols)])  7.4 us
    ppermute x2, waiting for transfers between devices, down(): return lax.ppermute(x, 'col', [((i + 1) % cols, i) for i in range(cols)])  2 us
    add x1, other arithmetic, on_device(): own_terms + half_own.astype(F32) + both(from_upper, from_lower)  1.94 us
    unnamed x30, local copies, waits for them, and re-layouts  1.6 us
  transfers between devices with their start and end apart: 24, of which 13 were waited for; matrix products, arithmetic and copies ran while one was open for 5% of the time, Pallas kernels for 10%

profile of v3, /device:TPU:0, one launch (start us, length us, event | category | flops | bytes accessed | tf_op | source)
XLA Modules:
  0.0 77.9 jit_solution(3017468451118301705)
XLA Ops:
  1.7 5.1 %collective-permute-start.7 = (bf16[8,64,256]{2,1,0:T(8,128)(2,1)S(1)}, bf16[8,64,256]{2,1,0:T(8,128)(2,1)S(1)}, u32[]{:S(2)}, u32[]{:S(2)}) collective-permute-start(bf16[8,64,256]{2,1,0:T(8,128)(2,1)S(1)} %bitcast.11), channel_id=1, source_target_pairs={{4,0},{8,4},{12,8},{0,12},{5,1},{9,5},{13,9},{1,13},{6,2},{10,6},{... | collective-permute-start | bytes 786440 | tf_op jit(solution)/shard_map/ppermute | solution.py:230
  6.8 1.5 %collective-permute-start.1 = (bf16[8,64,256]{2,1,0:T(8,128)(2,1)S(1)}, bf16[8,64,256]{2,1,0:T(8,128)(2,1)S(1)}, u32[]{:S(2)}, u32[]{:S(2)}) collective-permute-start(bf16[8,64,256]{2,1,0:T(8,128)(2,1)S(1)} %bitcast.13), channel_id=1, source_target_pairs={{0,2},{1,3},{2,0},{3,1},{4,6},{5,7},{6,4},{7,5},{8,10},{9,11},{10,... | collective-permute-start | bytes 786440 | tf_op jit(solution)/shard_map/ppermute | solution.py:216
  8.3 4.8 %shard_map.85 = (bf16[8,64,512]{2,1,0:T(8,128)(2,1)}, f32[8,64,128]{2,1,0:T(8,128)}, f32[512,256]{1,0:T(8,128)}, bf16[512,128]{1,0:T(8,128)(2,1)}, bf16[2,256,51...) custom-call(s32[8,8,64,64]{3,2,1,0:T(8,128)} %edge_hbm.1, f32[512,256]{1,0:T(8,128)} %feat_hbm.1, f32[256,256]{1,0:T(8,128)} %self_hbm.1, ...), custom_call_target="tpu_custom_call" | custom-call | flops 201326592 | bytes 4851712 | tf_op jit(solution)/shard_map/pallas_call | solution.py:25
  13.5 1.5 %collective-permute-start.9 = (bf16[8,64,256]{2,1,0:T(8,128)(2,1)S(1)}, bf16[8,64,256]{2,1,0:T(8,128)(2,1)S(1)}, u32[]{:S(2)}, u32[]{:S(2)}) collective-permute-start(bf16[8,64,256]{2,1,0:T(8,128)(2,1)S(1)} %collective-permute-done.7.refs_8_), channel_id=1, source_target_pairs={{0,2},{1,3},{2,0},{3,1},{4,6},{5,7},{6,4},{7,5},{8,10},{9,11},{10,... | collective-permute-start | bytes 786440 | tf_op jit(solution)/shard_map/ppermute | solution.py:216
  15.1 3.9 %collective-permute-done.3.refs_4_ = bf16[8,64,256]{2,1,0:T(8,128)(2,1)S(1)} collective-permute-done((bf16[8,64,256]{2,1,0:T(8,128)(2,1)S(1)}, bf16[8,64,256]{2,1,0:T(8,128)(2,1)S(1)}, u32[]{:S(2)}, u32[]{:S(2)}) %collective-permute-start.3) | collective-permute-done | bytes 262176 | tf_op jit(solution)/shard_map/ppermute | solution.py:226
  18.9 1.5 %collective-permute-start.5 = (bf16[8,64,256]{2,1,0:T(8,128)(2,1)S(1)}, bf16[8,64,256]{2,1,0:T(8,128)(2,1)S(1)}, u32[]{:S(2)}, u32[]{:S(2)}) collective-permute-start(bf16[8,64,256]{2,1,0:T(8,128)(2,1)S(1)} %collective-permute-done.3.refs_4_), channel_id=1, source_target_pairs={{0,2},{1,3},{2,0},{3,1},{4,6},{5,7},{6,4},{7,5},{8,10},{9,11},{10,... | collective-permute-start | bytes 786440 | tf_op jit(solution)/shard_map/ppermute | solution.py:216
  21.0 1.6 %collective-permute-done.9.refs_10_ = bf16[8,64,256]{2,1,0:T(8,128)(2,1)S(1)} collective-permute-done((bf16[8,64,256]{2,1,0:T(8,128)(2,1)S(1)}, bf16[8,64,256]{2,1,0:T(8,128)(2,1)S(1)}, u32[]{:S(2)}, u32[]{:S(2)}) %collective-permute-start.9) | collective-permute-done | bytes 262176 | tf_op jit(solution)/shard_map/ppermute | solution.py:216
  22.7 4.8 %collective-permute-done.5.refs_6_ = bf16[8,64,256]{2,1,0:T(8,128)(2,1)S(1)} collective-permute-done((bf16[8,64,256]{2,1,0:T(8,128)(2,1)S(1)}, bf16[8,64,256]{2,1,0:T(8,128)(2,1)S(1)}, u32[]{:S(2)}, u32[]{:S(2)}) %collective-permute-start.5) | collective-permute-done | bytes 262176 | tf_op jit(solution)/shard_map/ppermute | solution.py:216
  27.6 1.5 %collective-permute-done.6.refs_7_ = bf16[8,64,256]{2,1,0:T(8,128)(2,1)S(1)} collective-permute-done((bf16[8,64,256]{2,1,0:T(8,128)(2,1)S(1)}, bf16[8,64,256]{2,1,0:T(8,128)(2,1)S(1)}, u32[]{:S(2)}, u32[]{:S(2)}) %collective-permute-start.6) | collective-permute-done | bytes 262176 | tf_op jit(solution)/shard_map/ppermute | solution.py:216
  29.8 7.1 %shard_map.86 = (bf16[2,8,64,256]{3,2,1,0:T(8,128)(2,1)}, bf16[4,8,64,256]{3,2,1,0:T(8,128)(2,1)}, bf16[2,8,64,256]{3,2,1,0:T(8,128)(2,1)}, bf16[4,8,64,256]{3,2...) custom-call(bf16[8,64,256]{2,1,0:T(8,128)(2,1)} %bitcast.15, ...), custom_call_target="tpu_custom_call" | custom-call | flops 1342177280 | bytes 10092800 | tf_op jit(solution)/shard_map/pallas_call | solution.py:25
  37.6 1.5 %collective-permute-done.11 = bf16[2,8,64,256]{3,2,1,0:T(8,128)(2,1)S(1)} collective-permute-done((bf16[2,8,64,256]{3,2,1,0:T(8,128)(2,1)}, bf16[2,8,64,256]{3,2,1,0:T(8,128)(2,1)S(1)}, u32[]{:S(2)}, u32[]{:S(2)}) %collective-permute-start.11) | collective-permute-done | bytes 524320 | tf_op jit(solution)/shard_map/ppermute | solution.py:216
  39.1 1.2 %add_convert_fusion = bf16[2,8,64,256]{3,2,1,0:T(8,128)(2,1)S(1)} fusion(bf16[2,8,64,256]{3,2,1,0:T(8,128)(2,1)S(1)} %collective-permute-done.11, bf16[2,8,64,256]{3,2,1,0:T(8,128)(2,1)} %get-tuple-element.37), kind=kLoop, calls=%fused_computation | loop fusion | flops 1048576 | bytes 1572864 | tf_op jit(solution)/shard_map/convert_element_type | solution.py:328
  42.0 1.6 %collective-permute-start.14 = (bf16[128,256]{1,0:T(8,128)(2,1)S(1)}, bf16[128,256]{1,0:T(8,128)(2,1)S(1)}, u32[]{:S(2)}, u32[]{:S(2)}) collective-permute-start(bf16[128,256]{1,0:T(8,128)(2,1)S(1)} %convert_element_type.81), channel_id=1, source_target_pairs={{0,16},{16,0},{1,17},{17,1},{2,18},{18,2},{3,19},{19,3},{4,20},{20... | collective-permute-start | bytes 196616 | tf_op jit(solution)/shard_map/ppermute | solution.py:216
  44.1 2.3 %collective-permute-done.14 = bf16[128,256]{1,0:T(8,128)(2,1)S(1)} collective-permute-done((bf16[128,256]{1,0:T(8,128)(2,1)S(1)}, bf16[128,256]{1,0:T(8,128)(2,1)S(1)}, u32[]{:S(2)}, u32[]{:S(2)}) %collective-permute-start.14) | collective-permute-done | bytes 65568 | tf_op jit(solution)/shard_map/ppermute | solution.py:216
  46.6 4.7 %collective-permute-done.15 = f32[128,256]{1,0:T(8,128)S(1)} collective-permute-done((f32[128,256]{1,0:T(8,128)S(1)}, f32[128,256]{1,0:T(8,128)S(1)}, u32[]{:S(2)}, u32[]{:S(2)}) %collective-permute-start.15) | collective-permute-done | bytes 131104 | tf_op jit(solution)/shard_map/ppermute | solution.py:216
  51.4 2.4 %collective-permute-start.16 = (f32[128,256]{1,0:T(8,128)S(1)}, f32[128,256]{1,0:T(8,128)S(1)}, u32[]{:S(2)}, u32[]{:S(2)}) collective-permute-start(f32[128,256]{1,0:T(8,128)S(1)} %add.51), channel_id=1, source_target_pairs={{0,8},{4,12},{8,0},{12,4},{1,9},{5,13},{9,1},{13,5},{2,10},{6,14},... | collective-permute-start | bytes 393224 | tf_op jit(solution)/shard_map/ppermute | solution.py:216
  53.8 4.9 %collective-permute-done.16 = f32[128,256]{1,0:T(8,128)S(1)} collective-permute-done((f32[128,256]{1,0:T(8,128)S(1)}, f32[128,256]{1,0:T(8,128)S(1)}, u32[]{:S(2)}, u32[]{:S(2)}) %collective-permute-start.16) | collective-permute-done | bytes 131104 | tf_op jit(solution)/shard_map/ppermute | solution.py:216
  59.7 1.6 %collective-permute-start.21 = (bf16[8,64,256]{2,1,0:T(8,128)(2,1)S(1)}, bf16[8,64,256]{2,1,0:T(8,128)(2,1)S(1)}, u32[]{:S(2)}, u32[]{:S(2)}) collective-permute-start(bf16[8,64,256]{2,1,0:T(8,128)(2,1)S(1)} %get-tuple-element.53), channel_id=1, source_target_pairs={{0,2},{1,3},{2,0},{3,1},{4,6},{5,7},{6,4},{7,5},{8,10},{9,11},{10,... | collective-permute-start | bytes 786440 | tf_op jit(solution)/shard_map/ppermute | solution.py:216
  61.3 3.5 %collective-permute-start.22 = (bf16[8,64,256]{2,1,0:T(8,128)(2,1)S(1)}, bf16[8,64,256]{2,1,0:T(8,128)(2,1)S(1)}, u32[]{:S(2)}, u32[]{:S(2)}) collective-permute-start(bf16[8,64,256]{2,1,0:T(8,128)(2,1)S(1)} %get-tuple-element.51), channel_id=1, source_target_pairs={{4,0},{8,4},{12,8},{0,12},{5,1},{9,5},{13,9},{1,13},{6,2},{10,6},{... | collective-permute-start | bytes 786440 | tf_op jit(solution)/shard_map/ppermute | solution.py:230
  64.9 1.6 %collective-permute-start.19 = (f32[128,256]{1,0:T(8,128)S(1)}, f32[128,256]{1,0:T(8,128)S(1)}, u32[]{:S(2)}, u32[]{:S(2)}) collective-permute-start(f32[128,256]{1,0:T(8,128)S(1)} %add.53.refs_0_), channel_id=1, source_target_pairs={{0,16},{16,0},{1,17},{17,1},{2,18},{18,2},{3,19},{19,3},{4,20},{20... | collective-permute-start | bytes 393224 | tf_op jit(solution)/shard_map/ppermute | solution.py:216
  66.4 2.6 %shard_map.89 = f32[8,64,256]{2,1,0:T(8,128)} custom-call(f32[8,64,256]{2,1,0:T(8,128)} %bitcast.17, bf16[4,8,64,256]{3,2,1,0:T(8,128)(2,1)} %get-tuple-element.48.keep_ref, bf16[4,8,64,256]{3,2,1,0:T(8,128)(2,1)} %copy-done.2), custom_call_target="tpu_custom_call" | custom-call | bytes 3145728 | tf_op jit(solution)/shard_map/pallas_call | solution.py:25
  70.0 1.6 %collective-permute-done.22 = bf16[8,64,256]{2,1,0:T(8,128)(2,1)S(1)} collective-permute-done((bf16[8,64,256]{2,1,0:T(8,128)(2,1)S(1)}, bf16[8,64,256]{2,1,0:T(8,128)(2,1)S(1)}, u32[]{:S(2)}, u32[]{:S(2)}) %collective-permute-start.22) | collective-permute-done | bytes 262176 | tf_op jit(solution)/shard_map/ppermute | solution.py:230
  71.6 3.6 %collective-permute-done.23 = bf16[8,64,256]{2,1,0:T(8,128)(2,1)S(1)} collective-permute-done((bf16[8,64,256]{2,1,0:T(8,128)(2,1)S(1)}, bf16[8,64,256]{2,1,0:T(8,128)(2,1)S(1)}, u32[]{:S(2)}, u32[]{:S(2)}) %collective-permute-start.23) | collective-permute-done | bytes 262176 | tf_op jit(solution)/shard_map/ppermute | solution.py:226
  75.2 1.9 %add_add_fusion = f32[8,64,256]{2,1,0:T(8,128)} fusion(bf16[8,64,256]{2,1,0:T(8,128)(2,1)S(1)} %collective-permute-done.23, bf16[8,64,256]{2,1,0:T(8,128)(2,1)S(1)} %collective-permute-done.22, f32[8,64,256]{2,1,0:T(8,128)} %shard_map.89, bf16[8,64,256]{2,1,0:T(8,128)(2,1)S(1)} %collective-permute-done.21), kind=kLoop, calls=%fused_computation.1 | loop fusion | flops 786432 | bytes 1835008 | tf_op jit(solution)/shard_map/add | solution.py:356
  (69 shorter events, 8.8 us)
Async XLA Ops:
  1.7 11.8 %collective-permute-start.7 = (bf16[8,64,256]{2,1,0:T(8,128)(2,1)S(1)}, bf16[8,64,256]{2,1,0:T(8,128)(2,1)S(1)}, u32[]{:S(2)}, u32[]{:S(2)}) collective-permute-start(bf16[8,64,256]{2,1,0:T(8,128)(2,1)S(1)} %bitcast.11), channel_id=1, source_target_pairs={{4,0},{8,4},{12,8},{0,12},{5,1},{9,5},{13,9},{1,13},{6,2},{10,6},{... | collective-permute-start | bytes 786440 | tf_op jit(solution)/shard_map/ppermute | solution.py:230
  6.8 12.1 %collective-permute-start.3 = (bf16[8,64,256]{2,1,0:T(8,128)(2,1)S(1)}, bf16[8,64,256]{2,1,0:T(8,128)(2,1)S(1)}, u32[]{:S(2)}, u32[]{:S(2)}) collective-permute-start(bf16[8,64,256]{2,1,0:T(8,128)(2,1)S(1)} %bitcast.12), channel_id=1, source_target_pairs={{0,4},{4,8},{8,12},{12,0},{1,5},{5,9},{9,13},{13,1},{2,6},{6,10},{... | collective-permute-start | bytes 786440 | tf_op jit(solution)/shard_map/ppermute | solution.py:226
  6.8 13.6 %collective-permute-start.1 = (bf16[8,64,256]{2,1,0:T(8,128)(2,1)S(1)}, bf16[8,64,256]{2,1,0:T(8,128)(2,1)S(1)}, u32[]{:S(2)}, u32[]{:S(2)}) collective-permute-start(bf16[8,64,256]{2,1,0:T(8,128)(2,1)S(1)} %bitcast.13), channel_id=1, source_target_pairs={{0,2},{1,3},{2,0},{3,1},{4,6},{5,7},{6,4},{7,5},{8,10},{9,11},{10,... | collective-permute-start | bytes 786440 | tf_op jit(solution)/shard_map/ppermute | solution.py:216
  8.3 12.6 %collective-permute-start = (bf16[8,64,256]{2,1,0:T(8,128)(2,1)S(1)}, bf16[8,64,256]{2,1,0:T(8,128)(2,1)S(1)}, u32[]{:S(2)}, u32[]{:S(2)}) collective-permute-start(bf16[8,64,256]{2,1,0:T(8,128)(2,1)S(1)} %bitcast.14), channel_id=1, source_target_pairs={{0,1},{1,0},{2,3},{3,2},{4,5},{5,4},{6,7},{7,6},{8,9},{9,8},{10,11... | collective-permute-start | bytes 786440 | tf_op jit(solution)/shard_map/ppermute | solution.py:216
  13.5 9.1 %collective-permute-start.9 = (bf16[8,64,256]{2,1,0:T(8,128)(2,1)S(1)}, bf16[8,64,256]{2,1,0:T(8,128)(2,1)S(1)}, u32[]{:S(2)}, u32[]{:S(2)}) collective-permute-start(bf16[8,64,256]{2,1,0:T(8,128)(2,1)S(1)} %collective-permute-done.7.refs_8_), channel_id=1, source_target_pairs={{0,2},{1,3},{2,0},{3,1},{4,6},{5,7},{6,4},{7,5},{8,10},{9,11},{10,... | collective-permute-start | bytes 786440 | tf_op jit(solution)/shard_map/ppermute | solution.py:216
  18.9 8.6 %collective-permute-start.5 = (bf16[8,64,256]{2,1,0:T(8,128)(2,1)S(1)}, bf16[8,64,256]{2,1,0:T(8,128)(2,1)S(1)}, u32[]{:S(2)}, u32[]{:S(2)}) collective-permute-start(bf16[8,64,256]{2,1,0:T(8,128)(2,1)S(1)} %collective-permute-done.3.refs_4_), channel_id=1, source_target_pairs={{0,2},{1,3},{2,0},{3,1},{4,6},{5,7},{6,4},{7,5},{8,10},{9,11},{10,... | collective-permute-start | bytes 786440 | tf_op jit(solution)/shard_map/ppermute | solution.py:216
  20.4 7.1 %collective-permute-start.4 = (bf16[8,64,256]{2,1,0:T(8,128)(2,1)S(1)}, bf16[8,64,256]{2,1,0:T(8,128)(2,1)S(1)}, u32[]{:S(2)}, u32[]{:S(2)}) collective-permute-start(bf16[8,64,256]{2,1,0:T(8,128)(2,1)S(1)} %collective-permute-done.3.refs_4_), channel_id=1, source_target_pairs={{0,1},{1,0},{2,3},{3,2},{4,5},{5,4},{6,7},{7,6},{8,9},{9,8},{10,11... | collective-permute-start | bytes 786440 | tf_op jit(solution)/shard_map/ppermute | solution.py:216
  20.4 7.1 %collective-permute-start.8 = (bf16[8,64,256]{2,1,0:T(8,128)(2,1)S(1)}, bf16[8,64,256]{2,1,0:T(8,128)(2,1)S(1)}, u32[]{:S(2)}, u32[]{:S(2)}) collective-permute-start(bf16[8,64,256]{2,1,0:T(8,128)(2,1)S(1)} %collective-permute-done.7.refs_8_), channel_id=1, source_target_pairs={{0,1},{1,0},{2,3},{3,2},{4,5},{5,4},{6,7},{7,6},{8,9},{9,8},{10,11... | collective-permute-start | bytes 786440 | tf_op jit(solution)/shard_map/ppermute | solution.py:216
  20.9 6.6 %collective-permute-start.2 = (bf16[8,64,256]{2,1,0:T(8,128)(2,1)S(1)}, bf16[8,64,256]{2,1,0:T(8,128)(2,1)S(1)}, u32[]{:S(2)}, u32[]{:S(2)}) collective-permute-start(bf16[8,64,256]{2,1,0:T(8,128)(2,1)S(1)} %collective-permute-done.1.refs_2_), channel_id=1, source_target_pairs={{0,1},{1,0},{2,3},{3,2},{4,5},{5,4},{6,7},{7,6},{8,9},{9,8},{10,11... | collective-permute-start | bytes 786440 | tf_op jit(solution)/shard_map/ppermute | solution.py:216
  22.7 4.9 %collective-permute-start.10 = (bf16[8,64,256]{2,1,0:T(8,128)(2,1)S(1)}, bf16[8,64,256]{2,1,0:T(8,128)(2,1)S(1)}, u32[]{:S(2)}, u32[]{:S(2)}) collective-permute-start(bf16[8,64,256]{2,1,0:T(8,128)(2,1)S(1)} %collective-permute-done.9.refs_10_), channel_id=1, source_target_pairs={{0,1},{1,0},{2,3},{3,2},{4,5},{5,4},{6,7},{7,6},{8,9},{9,8},{10,11... | collective-permute-start | bytes 786440 | tf_op jit(solution)/shard_map/ppermute | solution.py:216
  27.5 1.5 %collective-permute-start.6 = (bf16[8,64,256]{2,1,0:T(8,128)(2,1)S(1)}, bf16[8,64,256]{2,1,0:T(8,128)(2,1)S(1)}, u32[]{:S(2)}, u32[]{:S(2)}) collective-permute-start(bf16[8,64,256]{2,1,0:T(8,128)(2,1)S(1)} %collective-permute-done.5.refs_6_), channel_id=1, source_target_pairs={{0,1},{1,0},{2,3},{3,2},{4,5},{5,4},{6,7},{7,6},{8,9},{9,8},{10,11... | collective-permute-start | bytes 786440 | tf_op jit(solution)/shard_map/ppermute | solution.py:216
  36.9 2.2 %collective-permute-start.11 = (bf16[2,8,64,256]{3,2,1,0:T(8,128)(2,1)}, bf16[2,8,64,256]{3,2,1,0:T(8,128)(2,1)S(1)}, u32[]{:S(2)}, u32[]{:S(2)}) collective-permute-start(bf16[2,8,64,256]{3,2,1,0:T(8,128)(2,1)} %get-tuple-element.38), channel_id=1, source_target_pairs={{0,1},{1,0},{2,3},{3,2},{4,5},{5,4},{6,7},{7,6},{8,9},{9,8},{10,11... | collective-permute-start | bytes 1572872 | tf_op jit(solution)/shard_map/ppermute | solution.py:216
  37.1 21.7 %collective-permute-start.17 = (bf16[4,8,64,256]{3,2,1,0:T(8,128)(2,1)}, bf16[4,8,64,256]{3,2,1,0:T(8,128)(2,1)S(1)}, u32[]{:S(2)}, u32[]{:S(2)}) collective-permute-start(bf16[4,8,64,256]{3,2,1,0:T(8,128)(2,1)} %get-tuple-element.45), channel_id=1, source_target_pairs={{0,1},{1,0},{2,3},{3,2},{4,5},{5,4},{6,7},{7,6},{8,9},{9,8},{10,11... | collective-permute-start | bytes 3145736 | tf_op jit(solution)/shard_map/ppermute | solution.py:216
  37.5 3.5 %collective-permute-start.12 = (f32[256,256]{1,0:T(8,128)}, f32[256,256]{1,0:T(8,128)S(1)}, u32[]{:S(2)}, u32[]{:S(2)}) collective-permute-start(f32[256,256]{1,0:T(8,128)} %get-tuple-element.39), channel_id=1, source_target_pairs={{0,1},{1,0},{2,3},{3,2},{4,5},{5,4},{6,7},{7,6},{8,9},{9,8},{10,11... | collective-permute-start | bytes 786440 | tf_op jit(solution)/shard_map/ppermute | solution.py:216
  42.0 4.3 %collective-permute-start.14 = (bf16[128,256]{1,0:T(8,128)(2,1)S(1)}, bf16[128,256]{1,0:T(8,128)(2,1)S(1)}, u32[]{:S(2)}, u32[]{:S(2)}) collective-permute-start(bf16[128,256]{1,0:T(8,128)(2,1)S(1)} %convert_element_type.81), channel_id=1, source_target_pairs={{0,16},{16,0},{1,17},{17,1},{2,18},{18,2},{3,19},{19,3},{4,20},{20... | collective-permute-start | bytes 196616 | tf_op jit(solution)/shard_map/ppermute | solution.py:216
  43.6 15.2 %collective-permute-start.13 = (bf16[2,8,64,256]{3,2,1,0:T(8,128)(2,1)S(1)}, bf16[2,8,64,256]{3,2,1,0:T(8,128)(2,1)S(1)}, u32[]{:S(2)}, u32[]{:S(2)}) collective-permute-start(bf16[2,8,64,256]{3,2,1,0:T(8,128)(2,1)S(1)} %add_convert_fusion), channel_id=1, source_target_pairs={{0,2},{1,3},{2,0},{3,1},{4,6},{5,7},{6,4},{7,5},{8,10},{9,11},{10,... | collective-permute-start | bytes 1572872 | tf_op jit(solution)/shard_map/ppermute | solution.py:216
  46.3 5.0 %collective-permute-start.15 = (f32[128,256]{1,0:T(8,128)S(1)}, f32[128,256]{1,0:T(8,128)S(1)}, u32[]{:S(2)}, u32[]{:S(2)}) collective-permute-start(f32[128,256]{1,0:T(8,128)S(1)} %convert_add_fusion), channel_id=1, source_target_pairs={{0,4},{4,0},{8,12},{12,8},{1,5},{5,1},{9,13},{13,9},{2,6},{6,2},{1... | collective-permute-start | bytes 393224 | tf_op jit(solution)/shard_map/ppermute | solution.py:216
  51.4 7.3 %collective-permute-start.16 = (f32[128,256]{1,0:T(8,128)S(1)}, f32[128,256]{1,0:T(8,128)S(1)}, u32[]{:S(2)}, u32[]{:S(2)}) collective-permute-start(f32[128,256]{1,0:T(8,128)S(1)} %add.51), channel_id=1, source_target_pairs={{0,8},{4,12},{8,0},{12,4},{1,9},{5,13},{9,1},{13,5},{2,10},{6,14},... | collective-permute-start | bytes 393224 | tf_op jit(solution)/shard_map/ppermute | solution.py:216
  58.8 6.1 %collective-permute-start.18 = (f32[128,256]{1,0:T(8,128)S(1)}, f32[128,256]{1,0:T(8,128)S(1)}, u32[]{:S(2)}, u32[]{:S(2)}) collective-permute-start(f32[128,256]{1,0:T(8,128)S(1)} %add.52), channel_id=1, source_target_pairs={{0,2},{1,3},{2,0},{3,1},{4,6},{5,7},{6,4},{7,5},{8,10},{9,11},{10,... | collective-permute-start | bytes 393224 | tf_op jit(solution)/shard_map/ppermute | solution.py:216
  59.7 10.3 %collective-permute-start.21 = (bf16[8,64,256]{2,1,0:T(8,128)(2,1)S(1)}, bf16[8,64,256]{2,1,0:T(8,128)(2,1)S(1)}, u32[]{:S(2)}, u32[]{:S(2)}) collective-permute-start(bf16[8,64,256]{2,1,0:T(8,128)(2,1)S(1)} %get-tuple-element.53), channel_id=1, source_target_pairs={{0,2},{1,3},{2,0},{3,1},{4,6},{5,7},{6,4},{7,5},{8,10},{9,11},{10,... | collective-permute-start | bytes 786440 | tf_op jit(solution)/shard_map/ppermute | solution.py:216
  61.3 10.3 %collective-permute-start.22 = (bf16[8,64,256]{2,1,0:T(8,128)(2,1)S(1)}, bf16[8,64,256]{2,1,0:T(8,128)(2,1)S(1)}, u32[]{:S(2)}, u32[]{:S(2)}) collective-permute-start(bf16[8,64,256]{2,1,0:T(8,128)(2,1)S(1)} %get-tuple-element.51), channel_id=1, source_target_pairs={{4,0},{8,4},{12,8},{0,12},{5,1},{9,5},{13,9},{1,13},{6,2},{10,6},{... | collective-permute-start | bytes 786440 | tf_op jit(solution)/shard_map/ppermute | solution.py:230
  64.9 10.3 %collective-permute-start.23 = (bf16[8,64,256]{2,1,0:T(8,128)(2,1)S(1)}, bf16[8,64,256]{2,1,0:T(8,128)(2,1)S(1)}, u32[]{:S(2)}, u32[]{:S(2)}) collective-permute-start(bf16[8,64,256]{2,1,0:T(8,128)(2,1)S(1)} %get-tuple-element.52), channel_id=1, source_target_pairs={{0,4},{4,8},{8,12},{12,0},{1,5},{5,9},{9,13},{13,1},{2,6},{6,10},{... | collective-permute-start | bytes 786440 | tf_op jit(solution)/shard_map/ppermute | solution.py:226
  64.9 5.0 %collective-permute-start.19 = (f32[128,256]{1,0:T(8,128)S(1)}, f32[128,256]{1,0:T(8,128)S(1)}, u32[]{:S(2)}, u32[]{:S(2)}) collective-permute-start(f32[128,256]{1,0:T(8,128)S(1)} %add.53.refs_0_), channel_id=1, source_target_pairs={{0,16},{16,0},{1,17},{17,1},{2,18},{18,2},{3,19},{19,3},{4,20},{20... | collective-permute-start | bytes 393224 | tf_op jit(solution)/shard_map/ppermute | solution.py:216
  70.0 7.2 %collective-permute-start.20 = (f32[256,256]{1,0:T(8,128)S(1)}, f32[256,256]{1,0:T(8,128)S(1)}, u32[]{:S(2)}, u32[]{:S(2)}) collective-permute-start(f32[256,256]{1,0:T(8,128)S(1)} %shard_map.88), channel_id=1, source_target_pairs={{0,1},{1,0},{2,3},{3,2},{4,5},{5,4},{6,7},{7,6},{8,9},{9,8},{10,11... | collective-permute-start | bytes 786440 | tf_op jit(solution)/shard_map/ppermute | solution.py:216
  (15 other events, 115.9 us)

commit v4 on v3

v4 whole, which is shorter than its diff:
```python
import functools

import jax
import jax.numpy as jnp
from jax import lax
from jax.experimental import pallas as pl
from jax.experimental.pallas import tpu as pltpu
from jax.sharding import PartitionSpec as P

BLOCK = 64
F32 = jnp.float32
BF16 = jnp.bfloat16
VMEM = pl.BlockSpec(memory_space=pltpu.VMEM)
SMEM = pl.BlockSpec(memory_space=pltpu.SMEM)
ANY = pl.BlockSpec(memory_space=pl.ANY)
ROWS_BOTH = ((0,), (0,))


def shape(dims, dtype):
    return jax.ShapeDtypeStruct(dims, dtype)


def call(body, out_shape, operands, in_specs, out_specs, scratch=(), flops=0, vmem=60):
    moved = sum(x.size * x.dtype.itemsize for x in list(operands) + list(out_shape)) if flops else 0
    return pl.pallas_call(
        body,
        out_shape=out_shape,
        in_specs=in_specs,
        out_specs=out_specs,
        scratch_shapes=scratch,
        compiler_params=pltpu.CompilerParams(vmem_limit_bytes=vmem << 20),
        cost_estimate=pl.CostEstimate(flops=flops, bytes_accessed=moved, transcendentals=0),
    )(*operands)


def dot(a, b, contract=((1,), (0,))):
    return lax.dot_general(a, b, (contract, ((), ())), preferred_element_type=F32)


def halves(x):
    high = x.astype(BF16)
    return high, (x - high.astype(F32)).astype(BF16)


def dot3(a, b, contract=((1,), (0,))):
    return dot(a[0], b[0], contract) + (dot(a[0], b[1], contract) + dot(a[1], b[0], contract))


def wider(x):
    return jnp.concatenate([x, x], axis=-1)


def prepare_body(
    edge_hbm, feat_hbm, self_hbm, neigh_hbm, label_ref, low_ref, full_ref,
    edge_ref, feat_ref, self_ref, neigh_ref, sems,
):
    blocks, slots = edge_ref.shape[:2]
    tiles = [pltpu.make_async_copy(edge_hbm.at[b], edge_ref.at[b], sems.at[b]) for b in range(blocks)]
    dense = [
        pltpu.make_async_copy(source, target, sems.at[blocks + i])
        for i, (source, target) in enumerate(
            ((feat_hbm, feat_ref), (self_hbm, self_ref), (neigh_hbm, neigh_ref))
        )
    ]
    for c in tiles + dense:
        c.start()
    rows, width = feat_ref.shape
    classes = self_ref.shape[1]
    lines = label_ref.shape[0]
    columns = jnp.concatenate([label_ref[...].astype(F32), jnp.zeros((8 - lines % 8, 128), F32)], axis=0).T
    for r in range(lines):
        full_ref[r * 128 : (r + 1) * 128, classes + 128 :] = jnp.broadcast_to(columns[:, r : r + 1], (128, 128))
    for b in range(blocks):
        tiles[b].wait()
        wide = jnp.concatenate([edge_ref[b, s].astype(F32) for s in range(slots)], axis=1)
        low_ref[b * BLOCK : (b + 1) * BLOCK] = wide.astype(BF16)
        inverse = 1.0 / jnp.sum(wide, axis=1, keepdims=True)
        full_ref[b * BLOCK : (b + 1) * BLOCK, classes : classes + 128] = jnp.broadcast_to(inverse, (BLOCK, 128))
    for c in dense:
        c.wait()
    feat, own, neigh = feat_ref[...], self_ref[...], neigh_ref[...]
    full_ref[:, :classes] = dot3(halves(feat), halves(own))
    for k, x in enumerate(halves(feat.T)):
        low_ref[rows + k * width : rows + (k + 1) * width] = x
    for k, x in enumerate((neigh, neigh.T, own.T)):
        start = rows + (2 + k) * width
        low_ref[start : start + width] = jnp.concatenate(halves(x), axis=1)


def layer_body(*refs):
    pieces, (source_hbm, low_ref, full_ref), refs = refs[:12], refs[12:15], refs[15:]
    *made, direct_ref, mine_ref, passed_ref, table, mean, terms, source_ref, source_sem, piece_sems = refs
    sources = pltpu.make_async_copy(source_hbm, source_ref, source_sem)
    sources.start()
    per = pieces[0].shape[0]
    copies = [
        pltpu.make_async_copy(piece, table.at[pl.ds(i * per, per)], piece_sems.at[i])
        for i, piece in enumerate(pieces)
    ]
    for c in copies:
        c.start()
    rows, width = mean.shape
    classes = direct_ref.shape[1]
    blocks, slots = source_ref.shape
    me = lax.axis_index("rep")

    def named(b, s):
        return source_ref[b, s] ^ (me * blocks)

    terms[...] = jnp.zeros_like(terms)
    for c in [sources] + copies:
        c.wait()
    inverse = wider(full_ref[:, classes : classes + 128])
    for b in range(blocks):
        own = slice(b * BLOCK, (b + 1) * BLOCK)
        gathered = jnp.concatenate([table[named(b, s)] for s in range(slots)], axis=0)
        mean[own] = dot(low_ref[own], gathered) * inverse[own]

    def pair(k):
        x = low_ref[rows + (2 + k) * width : rows + (3 + k) * width]
        return x[:, :classes], x[:, classes:]

    neigh, neigh_t, own_t = [pair(k) for k in range(3)]
    mean_parts = halves(mean[...])
    logits = full_ref[:, :classes] + dot3(mean_parts, neigh)
    labels = lax.broadcasted_iota(jnp.int32, logits.shape, 1).astype(F32)
    target = jnp.where(labels == wider(full_ref[:, classes + 128 :]), 1.0, 0.0)
    residual = halves(1.0 / (1.0 + jnp.exp(-logits)) - target)
    spread = (dot3(residual, neigh_t) * inverse).astype(BF16)
    direct_ref[...] = dot3(residual, own_t)
    for b in range(blocks):
        own = slice(b * BLOCK, (b + 1) * BLOCK)
        contrib = dot(low_ref[own], spread[own], ROWS_BOTH)
        for s in range(slots):
            at = named(b, s)
            terms[at] = terms[at] + contrib[s * BLOCK : (s + 1) * BLOCK]

    for core in range(2):
        for place in range(6):
            rel = 2 + core if place < 3 else core
            region = (1, 2, 0)[place % 3]
            which, at = (2 * core, place) if place < 2 else (2 * core + 1, place - 2)
            made[which][at] = terms[pl.ds((region * 4 + rel) * per, per)].astype(BF16)

    self_part = dot3((low_ref[rows : rows + width], low_ref[rows + width : rows + 2 * width]), residual)
    neigh_part = dot3(mean_parts, residual, ROWS_BOTH)
    first = me % 2 == 0
    mine_ref[...] = jnp.where(first, self_part, neigh_part)
    passed_ref[...] = jnp.where(first, neigh_part, self_part)


def own_body(direct_ref, keep_ref, got_ref, half_ref, out_ref):
    both = keep_ref[3].astype(F32) + got_ref[3].astype(F32)
    out_ref[...] = direct_ref[...] + (both + half_ref[...].astype(F32))


def split_body(place_ref, *refs):
    outs = [r for r in refs if r.shape != refs[0].shape]
    total = tree_sum(r[...] for r in refs[: len(refs) - len(outs)])
    chunks = total.reshape(len(outs), *outs[0].shape)
    if len(outs) == 1:
        outs[0][...] = chunks[0]
        return
    for d, out in enumerate(outs):
        for c in range(len(outs)):

            @pl.when(place_ref[0] ^ d == c)
            def _():
                out[...] = chunks[c]


def add_body(a_ref, b_ref, sum_ref):
    sum_ref[...] = (a_ref[...].astype(F32) + b_ref[...].astype(F32)).astype(sum_ref.dtype)


def join_body(place_ref, *refs):
    out = refs[-1]
    rows = refs[0].shape[0]
    for d, chunk in enumerate(refs[:-1]):
        for c in range(len(refs) - 1):

            @pl.when(place_ref[0] ^ d == c)
            def _():
                out[c * rows : (c + 1) * rows] = chunk[...]


def tree_sum(values):
    values = list(values)
    while len(values) > 1:
        values = [sum(values[i + 1 : i + 2], values[i]) for i in range(0, len(values), 2)]
    return values[0]


def on_device(features, self_weight, neigh_weight, block_source, edge_weights, labels):
    rows, width = features.shape
    blocks, slots = block_source.shape
    classes = self_weight.shape[1]
    reps = lax.axis_size("rep")
    assert reps == 4
    me = lax.axis_index("rep").astype(jnp.int32)

    def swap(x, axis, d):
        return lax.ppermute(x, axis, [(i, i ^ d) for i in range(lax.axis_size(axis))])

    def core_swap(x):
        return swap(x, "rep", 1)

    def half_swap(x):
        return swap(x, "rep", 2)

    def up(x):
        cols = lax.axis_size("col")
        return lax.ppermute(x, "col", [(i, (i + 1) % cols) for i in range(cols)])

    def down(x):
        cols = lax.axis_size("col")
        return lax.ppermute(x, "col", [((i + 1) % cols, i) for i in range(cols)])

    own = features.astype(BF16).reshape(blocks, BLOCK, width)
    half, lower, upper, core = half_swap(own), up(own), down(own), core_swap(own)

    wide_cols = slots * BLOCK
    assert wide_cols == rows == 2 * width and classes == width
    low, full = call(
        prepare_body,
        (shape((2 * rows + 3 * width, wide_cols), BF16), shape((rows, classes + 256), F32)),
        (edge_weights, features, self_weight, neigh_weight, labels.reshape(rows // 128, 128)),
        [ANY] * 4 + [VMEM],
        [VMEM] * 2,
        scratch=[
            pltpu.VMEM(edge_weights.shape, jnp.int32),
            pltpu.VMEM(features.shape, F32),
            pltpu.VMEM(self_weight.shape, F32),
            pltpu.VMEM(neigh_weight.shape, F32),
            pltpu.SemaphoreType.DMA((blocks + 3,)),
        ],
        flops=6 * rows * width * classes,
        vmem=50,
    )
    half, lower, upper, core = (lax.optimization_barrier((x, full))[0] for x in (half, lower, upper, core))
    lower_half, upper_half = half_swap(lower), half_swap(upper)
    pieces = [
        own, core, half, core_swap(half),
        lower, core_swap(lower), lower_half, core_swap(lower_half),
        upper, core_swap(upper), upper_half, core_swap(upper_half),
    ]

    def piece_shape(*lead):
        return shape((*lead, blocks, BLOCK, width), BF16)

    weights = shape((width, classes), F32)
    keep_near, keep_rest, send_near, send_rest, direct, mine, passed = call(
        layer_body,
        (
            piece_shape(2), piece_shape(4), piece_shape(2), piece_shape(4),
            shape((rows, width), F32), weights, weights,
        ),
        (*pieces, block_source, low, full),
        [ANY] * 13 + [VMEM] * 2,
        [VMEM] * 7,
        scratch=[
            pltpu.VMEM((12 * blocks, BLOCK, width), BF16),
            pltpu.VMEM((rows, width), F32),
            pltpu.VMEM((12 * blocks, BLOCK, width), F32),
            pltpu.SMEM((blocks, slots), jnp.int32),
            pltpu.SemaphoreType.DMA(()),
            pltpu.SemaphoreType.DMA((12,)),
        ],
        flops=40 * rows * width * classes,
        vmem=24,
    )
    got_near, got_rest, got = core_swap(send_near), core_swap(send_rest), core_swap(passed)

    def both(a, b):
        return a.astype(F32) + b.astype(F32)

    lines, cols = lax.axis_size("row"), lax.axis_size("col")
    line = lax.axis_index("row").astype(jnp.int32).reshape(1)

    def split(parts):
        chunk = shape((parts[0].shape[0] // lines, classes), F32)
        return call(
            split_body,
            (chunk,) * lines,
            (line, *parts),
            [SMEM] + [VMEM] * len(parts),
            [VMEM] * lines,
            vmem=4,
        )

    def join(chunk):
        parts = [chunk] + [swap(chunk, "row", d) for d in range(1, lines)]
        (out,) = call(
            join_body,
            (shape((chunk.shape[0] * lines, classes), F32),),
            (line, *parts),
            [SMEM] + [VMEM] * lines,
            [VMEM],
            vmem=4,
        )
        return out

    def add(a, b, dtype=F32):
        (out,) = call(add_body, (shape(a.shape, dtype),), (a, b), [VMEM] * 2, [VMEM], vmem=4)
        return out

    def together(*values):
        return lax.optimization_barrier(values)

    near, got = together(both(keep_near, got_near).astype(BF16), got)
    half_near = half_swap(near)
    chunks = split((mine, got))
    part = chunks[0]
    for d in range(1, lines):
        part = add(part, swap(chunks[d].astype(BF16), "row", d), F32)
    step = 1
    while step < cols:
        part = add(part, swap(part, "col", step), BF16 if step == 1 else F32)
        step *= 2
    half_near, part, got_rest = together(half_near, part, got_rest)

    near = [both(keep_rest[1 + k], got_rest[1 + k]) + half_near[k].astype(F32) for k in range(2)]
    from_upper = down(near[0].astype(BF16))
    from_lower = up(near[1].astype(BF16))
    part = add(part, half_swap(part))
    whole = join(part)
    half_own = half_swap(both(keep_rest[0], got_rest[0]).astype(BF16))
    other = core_swap(whole)
    first = me % 2 == 0
    grad_self = jnp.where(first, whole, other)
    grad_neigh = jnp.where(first, other, whole)

    (own_terms,) = call(
        own_body,
        (shape((blocks, BLOCK, width), F32),),
        (direct.reshape(blocks, BLOCK, width), keep_rest, got_rest, half_own),
        [VMEM] * 4,
        [VMEM],
    )
    grad_features = own_terms + both(from_upper, from_lower)
    return grad_self, grad_neigh, grad_features.reshape(rows, width)


def solution(mesh):
    split = ("row", "col", "rep")
    return jax.shard_map(
        on_device,
        mesh=mesh,
        in_specs=(P(split, None), P(), P(), P(split, None), P(split, None, None, None), P(split)),
        out_specs=(P(), P(), P(split, None)),
        check_vma=False,
    )
```

time: 78.3 us -> 73.4 us (0.937)
  Pallas kernels: 14.5 us -> 9.43 us
  local copies, waits for them, and re-layouts: 1.6 us -> 4.34 us
  waiting for transfers between devices: 32.3 us -> 30.5 us
  starting transfers between devices: 23.1 us -> 22.3 us
    pallas_call x5 -> x9, Pallas kernels: 14.5 us -> 9.43 us  [call(): pl.pallas_call(body, out_shape=out_shape, in_specs=in_specs, out_specs=ou...]
    unnamed x30 -> x16, local copies, waits for them, and re-layouts: 1.6 us -> 4.34 us
    ppermute x20, waiting for transfers between devices: 22.9 us -> 25.5 us  [swap(): lax.ppermute(x, axis, [(i, i ^ d) for i in range(lax.axis_size(axis))])]
    ppermute x2, waiting for transfers between devices: 7.4 us -> 5.03 us  [up(): return lax.ppermute(x, 'col', [(i, (i + 1) % cols) for i in range(cols)])]
    ppermute x2, waiting for transfers between devices: 2 us -> 0.01 us  [down(): return lax.ppermute(x, 'col', [((i + 1) % cols, i) for i in range(cols)])]
    ppermute x20, starting transfers between devices: 14.4 us -> 13.2 us  [swap(): lax.ppermute(x, axis, [(i, i ^ d) for i in range(lax.axis_size(axis))])]
    convert_element_type x1, other arithmetic: 0.38 us -> 1.61 us  [on_device(): from_upper = down(near[0].astype(BF16))]
    convert_element_type x1, other arithmetic: 1.19 us -> 0.16 us  [on_device(): near, got = together(both(keep_near, got_near).astype(BF16), got)]
  transfers between devices with their start and end apart: 24 -> 24, of which waited for: 13 -> 12; matrix products, arithmetic and copies ran while one was open for 5% -> 3% of each run, Pallas kernels for 10% -> 8%
where the time goes in v4:
time: 73.4 us; the launch traced here: 73 us
  waiting for transfers between devices  30.5 us (42%)
  starting transfers between devices  22.3 us (30%)
  Pallas kernels  9.43 us (13%)
  other arithmetic  5.58 us (8%)
  local copies, waits for them, and re-layouts  4.34 us (6%)
  between operations  0.83 us (1%)
    ppermute x20, waiting for transfers between devices, swap(): lax.ppermute(x, axis, [(i, i ^ d) for i in range(lax.axis_size(axis))])  25.5 us
    ppermute x20, starting transfers between devices, swap(): lax.ppermute(x, axis, [(i, i ^ d) for i in range(lax.axis_size(axis))])  13.2 us
    pallas_call x9, Pallas kernels, call(): pl.pallas_call(body, out_shape=out_shape, in_specs=in_specs, out_specs=ou...  9.43 us
    ppermute x2, starting transfers between devices, down(): return lax.ppermute(x, 'col', [((i + 1) % cols, i) for i in range(cols)])  9.07 us
    ppermute x2, waiting for transfers between devices, up(): return lax.ppermute(x, 'col', [(i, (i + 1) % cols) for i in range(cols)])  5.03 us
    unnamed x16, local copies, waits for them, and re-layouts  4.34 us
    add x1, other arithmetic, on_device(): grad_features = own_terms + both(from_upper, from_lower)  1.91 us
    convert_element_type x1, other arithmetic, on_device(): from_upper = down(near[0].astype(BF16))  1.61 us
  transfers between devices with their start and end apart: 24, of which 12 were waited for; matrix products, arithmetic and copies ran while one was open for 3% of the time, Pallas kernels for 8%

profile of v4, /device:TPU:0, one launch (start us, length us, event | category | flops | bytes accessed | tf_op | source)
XLA Modules:
  0.0 73.0 jit_solution(334399868226681524)
XLA Ops:
  0.6 1.1 %convert_element_type.71 = bf16[512,256]{1,0:T(8,128)(2,1)S(1)} convert(f32[512,256]{1,0:T(8,128)} %feat_hbm.1) | non-fusion elementwise | flops 131072 | bytes 786432 | tf_op jit(solution)/shard_map/convert_element_type | solution.py:219
  1.7 5.1 %collective-permute-start.7 = (bf16[8,64,256]{2,1,0:T(8,128)(2,1)S(1)}, bf16[8,64,256]{2,1,0:T(8,128)(2,1)S(1)}, u32[]{:S(2)}, u32[]{:S(2)}) collective-permute-start(bf16[8,64,256]{2,1,0:T(8,128)(2,1)S(1)} %bitcast.11), channel_id=1, source_target_pairs={{4,0},{8,4},{12,8},{0,12},{5,1},{9,5},{13,9},{1,13},{6,2},{10,6},{... | collective-permute-start | bytes 786440 | tf_op jit(solution)/shard_map/ppermute | solution.py:217
  6.8 1.5 %collective-permute-start.1 = (bf16[8,64,256]{2,1,0:T(8,128)(2,1)S(1)}, bf16[8,64,256]{2,1,0:T(8,128)(2,1)S(1)}, u32[]{:S(2)}, u32[]{:S(2)}) collective-permute-start(bf16[8,64,256]{2,1,0:T(8,128)(2,1)S(1)} %bitcast.13), channel_id=1, source_target_pairs={{0,2},{1,3},{2,0},{3,1},{4,6},{5,7},{6,4},{7,5},{8,10},{9,11},{10,... | collective-permute-start | bytes 786440 | tf_op jit(solution)/shard_map/ppermute | solution.py:203
  12.0 2.9 %shard_map.85 = (bf16[1792,512]{1,0:T(8,128)(2,1)S(1)}, f32[512,512]{1,0:T(8,128)S(1)}) custom-call(s32[8,8,64,64]{3,2,1,0:T(8,128)} %edge_hbm.1, f32[512,256]{1,0:T(8,128)S(1)} %copy-done.1, f32[256,256]{1,0:T(8,128)S(1)} %copy-done.3, f32[256,256]{1,0:T(8,128)S(1)} %copy-done.4, s32[4,128]{1,0:T(4,128)S(1)} %bitcast.17), custom_call_target="tpu_custom_call" | custom-call | flops 201326592 | bytes 4982784 | tf_op jit(solution)/shard_map/pallas_call | solution.py:25
  15.5 3.4 %collective-permute-done.3.refs_4_ = bf16[8,64,256]{2,1,0:T(8,128)(2,1)S(1)} collective-permute-done((bf16[8,64,256]{2,1,0:T(8,128)(2,1)S(1)}, bf16[8,64,256]{2,1,0:T(8,128)(2,1)S(1)}, u32[]{:S(2)}, u32[]{:S(2)}) %collective-permute-start.3) | collective-permute-done | bytes 262176 | tf_op jit(solution)/shard_map/ppermute | solution.py:213
  18.9 1.5 %collective-permute-start.5 = (bf16[8,64,256]{2,1,0:T(8,128)(2,1)S(1)}, bf16[8,64,256]{2,1,0:T(8,128)(2,1)S(1)}, u32[]{:S(2)}, u32[]{:S(2)}) collective-permute-start(bf16[8,64,256]{2,1,0:T(8,128)(2,1)S(1)} %collective-permute-done.3.refs_4_), channel_id=1, source_target_pairs={{0,2},{1,3},{2,0},{3,1},{4,6},{5,7},{6,4},{7,5},{8,10},{9,11},{10,... | collective-permute-start | bytes 786440 | tf_op jit(solution)/shard_map/ppermute | solution.py:203
  21.0 3.1 %collective-permute-done.9.refs_10_ = bf16[8,64,256]{2,1,0:T(8,128)(2,1)S(1)} collective-permute-done((bf16[8,64,256]{2,1,0:T(8,128)(2,1)S(1)}, bf16[8,64,256]{2,1,0:T(8,128)(2,1)S(1)}, u32[]{:S(2)}, u32[]{:S(2)}) %collective-permute-start.9) | collective-permute-done | bytes 262176 | tf_op jit(solution)/shard_map/ppermute | solution.py:203
  24.1 5.2 %collective-permute-done.5.refs_6_ = bf16[8,64,256]{2,1,0:T(8,128)(2,1)S(1)} collective-permute-done((bf16[8,64,256]{2,1,0:T(8,128)(2,1)S(1)}, bf16[8,64,256]{2,1,0:T(8,128)(2,1)S(1)}, u32[]{:S(2)}, u32[]{:S(2)}) %collective-permute-start.5) | collective-permute-done | bytes 262176 | tf_op jit(solution)/shard_map/ppermute | solution.py:203
  29.4 1.5 %collective-permute-done.6.refs_7_ = bf16[8,64,256]{2,1,0:T(8,128)(2,1)S(1)} collective-permute-done((bf16[8,64,256]{2,1,0:T(8,128)(2,1)S(1)}, bf16[8,64,256]{2,1,0:T(8,128)(2,1)S(1)}, u32[]{:S(2)}, u32[]{:S(2)}) %collective-permute-start.6) | collective-permute-done | bytes 262176 | tf_op jit(solution)/shard_map/ppermute | solution.py:203
  30.9 3.7 %shard_map.86 = (bf16[2,8,64,256]{3,2,1,0:T(8,128)(2,1)S(1)}, bf16[4,8,64,256]{3,2,1,0:T(8,128)(2,1)S(1)}, bf16[2,8,64,256]{3,2,1,0:T(8,128)(2,1)S(1)}, bf16[4,8...) custom-call(bf16[8,64,256]{2,1,0:T(8,128)(2,1)S(1)} %bitcast.15, ...), custom_call_target="tpu_custom_call" | custom-call | flops 1342177280 | bytes 10223872 | tf_op jit(solution)/shard_map/pallas_call | solution.py:25
  35.3 1.3 %collective-permute-done.11 = bf16[2,8,64,256]{3,2,1,0:T(8,128)(2,1)S(1)} collective-permute-done((bf16[2,8,64,256]{3,2,1,0:T(8,128)(2,1)S(1)}, bf16[2,8,64,256]{3,2,1,0:T(8,128)(2,1)S(1)}, u32[]{:S(2)}, u32[]{:S(2)}) %collective-permute-start.11) | collective-permute-done | bytes 524320 | tf_op jit(solution)/shard_map/ppermute | solution.py:203
  37.9 1.6 %collective-permute-start.14 = (bf16[128,256]{1,0:T(8,128)(2,1)S(1)}, bf16[128,256]{1,0:T(8,128)(2,1)S(1)}, u32[]{:S(2)}, u32[]{:S(2)}) collective-permute-start(bf16[128,256]{1,0:T(8,128)(2,1)S(1)} %convert_element_type.75), channel_id=1, source_target_pairs={{0,16},{16,0},{1,17},{17,1},{2,18},{18,2},{3,19},{19,3},{4,20},{20... | collective-permute-start | bytes 196616 | tf_op jit(solution)/shard_map/ppermute | solution.py:203
  39.5 2.8 %collective-permute-done.14.b_ref = bf16[128,256]{1,0:T(8,128)(2,1)S(1)} collective-permute-done((bf16[128,256]{1,0:T(8,128)(2,1)S(1)}, bf16[128,256]{1,0:T(8,128)(2,1)S(1)}, u32[]{:S(2)}, u32[]{:S(2)}) %collective-permute-start.14) | collective-permute-done | bytes 65568 | tf_op jit(solution)/shard_map/ppermute | solution.py:203
  42.3 5.0 %collective-permute-done.15.b_ref = f32[128,256]{1,0:T(8,128)S(1)} collective-permute-done((f32[128,256]{1,0:T(8,128)S(1)}, f32[128,256]{1,0:T(8,128)S(1)}, u32[]{:S(2)}, u32[]{:S(2)}) %collective-permute-start.15) | collective-permute-done | bytes 131104 | tf_op jit(solution)/shard_map/ppermute | solution.py:203
  47.3 2.4 %collective-permute-start.16 = (bf16[128,256]{1,0:T(8,128)(2,1)S(1)}, bf16[128,256]{1,0:T(8,128)(2,1)S(1)}, u32[]{:S(2)}, u32[]{:S(2)}) collective-permute-start(bf16[128,256]{1,0:T(8,128)(2,1)S(1)} %shard_map.89.a_ref), channel_id=1, source_target_pairs={{0,8},{4,12},{8,0},{12,4},{1,9},{5,13},{9,1},{13,5},{2,10},{6,14},... | collective-permute-start | bytes 196616 | tf_op jit(solution)/shard_map/ppermute | solution.py:203
  49.7 2.8 %collective-permute-done.16.b_ref = bf16[128,256]{1,0:T(8,128)(2,1)S(1)} collective-permute-done((bf16[128,256]{1,0:T(8,128)(2,1)S(1)}, bf16[128,256]{1,0:T(8,128)(2,1)S(1)}, u32[]{:S(2)}, u32[]{:S(2)}) %collective-permute-start.16) | collective-permute-done | bytes 65568 | tf_op jit(solution)/shard_map/ppermute | solution.py:203
  52.6 1.6 %fusion.1 = (bf16[8,64,256]{2,1,0:T(8,128)(2,1)S(1)}, bf16[8,64,256]{2,1,0:T(8,128)(2,1)S(1)}, bf16[8,64,256]{2,1,0:T(8,128)(2,1)S(1)}) fusion(bf16[2,8,64,256]{3,2,1,0:T(8,128)(2,1)} %collective-permute-done.13, bf16[4,8,64,256]{3,2,1,0:T(8,128)(2,1)} %collective-permute-done.17.got_ref, bf16[4,8,64,256]{3,2,1,0:T(8,128)(2,1)S(1)} %get-tuple-element.40.keep_ref), kind=kLoop, calls=%fused_computation.6 | loop fusion | flops 2097152 | bytes 2883584 | tf_op jit(solution)/shard_map/convert_element_type | solution.py:323
  54.2 1.6 %collective-permute-start.21 = (bf16[8,64,256]{2,1,0:T(8,128)(2,1)S(1)}, bf16[8,64,256]{2,1,0:T(8,128)(2,1)S(1)}, u32[]{:S(2)}, u32[]{:S(2)}) collective-permute-start(bf16[8,64,256]{2,1,0:T(8,128)(2,1)S(1)} %get-tuple-element.45), channel_id=1, source_target_pairs={{0,2},{1,3},{2,0},{3,1},{4,6},{5,7},{6,4},{7,5},{8,10},{9,11},{10,... | collective-permute-start | bytes 786440 | tf_op jit(solution)/shard_map/ppermute | solution.py:203
  56.3 4.0 %collective-permute-start.22 = (bf16[8,64,256]{2,1,0:T(8,128)(2,1)S(1)}, bf16[8,64,256]{2,1,0:T(8,128)(2,1)S(1)}, u32[]{:S(2)}, u32[]{:S(2)}) collective-permute-start(bf16[8,64,256]{2,1,0:T(8,128)(2,1)S(1)} %get-tuple-element.43), channel_id=1, source_target_pairs={{4,0},{8,4},{12,8},{0,12},{5,1},{9,5},{13,9},{1,13},{6,2},{10,6},{... | collective-permute-start | bytes 786440 | tf_op jit(solution)/shard_map/ppermute | solution.py:217
  60.3 3.1 %collective-permute-done.18.b_ref = f32[128,256]{1,0:T(8,128)S(1)} collective-permute-done((f32[128,256]{1,0:T(8,128)S(1)}, f32[128,256]{1,0:T(8,128)S(1)}, u32[]{:S(2)}, u32[]{:S(2)}) %collective-permute-start.18) | collective-permute-done | bytes 131104 | tf_op jit(solution)/shard_map/ppermute | solution.py:203
  63.4 1.6 %collective-permute-start.19 = (f32[128,256]{1,0:T(8,128)S(1)}, f32[128,256]{1,0:T(8,128)S(1)}, u32[]{:S(2)}, u32[]{:S(2)}) collective-permute-start(f32[128,256]{1,0:T(8,128)S(1)} %shard_map.91.refs_0_), channel_id=1, source_target_pairs={{0,16},{16,0},{1,17},{17,1},{2,18},{18,2},{3,19},{19,3},{4,20},{20... | collective-permute-start | bytes 393224 | tf_op jit(solution)/shard_map/ppermute | solution.py:203
  65.7 2.6 %shard_map.93 = f32[8,64,256]{2,1,0:T(8,128)} custom-call(f32[8,64,256]{2,1,0:T(8,128)} %bitcast.16, bf16[4,8,64,256]{3,2,1,0:T(8,128)(2,1)} %copy-done, bf16[4,8,64,256]{3,2,1,0:T(8,128)(2,1)} %collective-permute-done.17.got_ref, bf16[8,64,256]{2,1,0:T(8,128)(2,1)} %copy-done.7), custom_call_target="tpu_custom_call" | custom-call | tf_op jit(solution)/shard_map/pallas_call | solution.py:25
  68.6 1.6 %collective-permute-done.23 = bf16[8,64,256]{2,1,0:T(8,128)(2,1)S(1)} collective-permute-done((bf16[8,64,256]{2,1,0:T(8,128)(2,1)S(1)}, bf16[8,64,256]{2,1,0:T(8,128)(2,1)S(1)}, u32[]{:S(2)}, u32[]{:S(2)}) %collective-permute-start.23) | collective-permute-done | bytes 262176 | tf_op jit(solution)/shard_map/ppermute | solution.py:213
  70.2 1.9 %add_add_fusion = f32[8,64,256]{2,1,0:T(8,128)} fusion(f32[8,64,256]{2,1,0:T(8,128)} %shard_map.93, bf16[8,64,256]{2,1,0:T(8,128)(2,1)S(1)} %collective-permute-done.23, bf16[8,64,256]{2,1,0:T(8,128)(2,1)S(1)} %collective-permute-done.22), kind=kLoop, calls=%fused_computation.1 | loop fusion | flops 524288 | bytes 1572864 | tf_op jit(solution)/shard_map/add | solution.py:340
  (55 shorter events, 9.2 us)
Async XLA Ops:
  1.7 13.2 %collective-permute-start.7 = (bf16[8,64,256]{2,1,0:T(8,128)(2,1)S(1)}, bf16[8,64,256]{2,1,0:T(8,128)(2,1)S(1)}, u32[]{:S(2)}, u32[]{:S(2)}) collective-permute-start(bf16[8,64,256]{2,1,0:T(8,128)(2,1)S(1)} %bitcast.11), channel_id=1, source_target_pairs={{4,0},{8,4},{12,8},{0,12},{5,1},{9,5},{13,9},{1,13},{6,2},{10,6},{... | collective-permute-start | bytes 786440 | tf_op jit(solution)/shard_map/ppermute | solution.py:217
  6.8 12.1 %collective-permute-start.3 = (bf16[8,64,256]{2,1,0:T(8,128)(2,1)S(1)}, bf16[8,64,256]{2,1,0:T(8,128)(2,1)S(1)}, u32[]{:S(2)}, u32[]{:S(2)}) collective-permute-start(bf16[8,64,256]{2,1,0:T(8,128)(2,1)S(1)} %bitcast.12), channel_id=1, source_target_pairs={{0,4},{4,8},{8,12},{12,0},{1,5},{5,9},{9,13},{13,1},{2,6},{6,10},{... | collective-permute-start | bytes 786440 | tf_op jit(solution)/shard_map/ppermute | solution.py:213
  6.8 13.6 %collective-permute-start.1 = (bf16[8,64,256]{2,1,0:T(8,128)(2,1)S(1)}, bf16[8,64,256]{2,1,0:T(8,128)(2,1)S(1)}, u32[]{:S(2)}, u32[]{:S(2)}) collective-permute-start(bf16[8,64,256]{2,1,0:T(8,128)(2,1)S(1)} %bitcast.13), channel_id=1, source_target_pairs={{0,2},{1,3},{2,0},{3,1},{4,6},{5,7},{6,4},{7,5},{8,10},{9,11},{10,... | collective-permute-start | bytes 786440 | tf_op jit(solution)/shard_map/ppermute | solution.py:203
  8.3 12.6 %collective-permute-start = (bf16[8,64,256]{2,1,0:T(8,128)(2,1)S(1)}, bf16[8,64,256]{2,1,0:T(8,128)(2,1)S(1)}, u32[]{:S(2)}, u32[]{:S(2)}) collective-permute-start(bf16[8,64,256]{2,1,0:T(8,128)(2,1)S(1)} %bitcast.14), channel_id=1, source_target_pairs={{0,1},{1,0},{2,3},{3,2},{4,5},{5,4},{6,7},{7,6},{8,9},{9,8},{10,11... | collective-permute-start | bytes 786440 | tf_op jit(solution)/shard_map/ppermute | solution.py:203
  14.9 9.2 %collective-permute-start.9 = (bf16[8,64,256]{2,1,0:T(8,128)(2,1)S(1)}, bf16[8,64,256]{2,1,0:T(8,128)(2,1)S(1)}, u32[]{:S(2)}, u32[]{:S(2)}) collective-permute-start(bf16[8,64,256]{2,1,0:T(8,128)(2,1)S(1)} %collective-permute-done.7.refs_8_), channel_id=1, source_target_pairs={{0,2},{1,3},{2,0},{3,1},{4,6},{5,7},{6,4},{7,5},{8,10},{9,11},{10,... | collective-permute-start | bytes 786440 | tf_op jit(solution)/shard_map/ppermute | solution.py:203
  18.9 10.4 %collective-permute-start.5 = (bf16[8,64,256]{2,1,0:T(8,128)(2,1)S(1)}, bf16[8,64,256]{2,1,0:T(8,128)(2,1)S(1)}, u32[]{:S(2)}, u32[]{:S(2)}) collective-permute-start(bf16[8,64,256]{2,1,0:T(8,128)(2,1)S(1)} %collective-permute-done.3.refs_4_), channel_id=1, source_target_pairs={{0,2},{1,3},{2,0},{3,1},{4,6},{5,7},{6,4},{7,5},{8,10},{9,11},{10,... | collective-permute-start | bytes 786440 | tf_op jit(solution)/shard_map/ppermute | solution.py:203
  20.4 8.9 %collective-permute-start.4 = (bf16[8,64,256]{2,1,0:T(8,128)(2,1)S(1)}, bf16[8,64,256]{2,1,0:T(8,128)(2,1)S(1)}, u32[]{:S(2)}, u32[]{:S(2)}) collective-permute-start(bf16[8,64,256]{2,1,0:T(8,128)(2,1)S(1)} %collective-permute-done.3.refs_4_), channel_id=1, source_target_pairs={{0,1},{1,0},{2,3},{3,2},{4,5},{5,4},{6,7},{7,6},{8,9},{9,8},{10,11... | collective-permute-start | bytes 786440 | tf_op jit(solution)/shard_map/ppermute | solution.py:203
  20.4 8.9 %collective-permute-start.8 = (bf16[8,64,256]{2,1,0:T(8,128)(2,1)S(1)}, bf16[8,64,256]{2,1,0:T(8,128)(2,1)S(1)}, u32[]{:S(2)}, u32[]{:S(2)}) collective-permute-start(bf16[8,64,256]{2,1,0:T(8,128)(2,1)S(1)} %collective-permute-done.7.refs_8_), channel_id=1, source_target_pairs={{0,1},{1,0},{2,3},{3,2},{4,5},{5,4},{6,7},{7,6},{8,9},{9,8},{10,11... | collective-permute-start | bytes 786440 | tf_op jit(solution)/shard_map/ppermute | solution.py:203
  20.9 8.4 %collective-permute-start.2 = (bf16[8,64,256]{2,1,0:T(8,128)(2,1)S(1)}, bf16[8,64,256]{2,1,0:T(8,128)(2,1)S(1)}, u32[]{:S(2)}, u32[]{:S(2)}) collective-permute-start(bf16[8,64,256]{2,1,0:T(8,128)(2,1)S(1)} %collective-permute-done.1.refs_2_), channel_id=1, source_target_pairs={{0,1},{1,0},{2,3},{3,2},{4,5},{5,4},{6,7},{7,6},{8,9},{9,8},{10,11... | collective-permute-start | bytes 786440 | tf_op jit(solution)/shard_map/ppermute | solution.py:203
  24.1 5.3 %collective-permute-start.10 = (bf16[8,64,256]{2,1,0:T(8,128)(2,1)S(1)}, bf16[8,64,256]{2,1,0:T(8,128)(2,1)S(1)}, u32[]{:S(2)}, u32[]{:S(2)}) collective-permute-start(bf16[8,64,256]{2,1,0:T(8,128)(2,1)S(1)} %collective-permute-done.9.refs_10_), channel_id=1, source_target_pairs={{0,1},{1,0},{2,3},{3,2},{4,5},{5,4},{6,7},{7,6},{8,9},{9,8},{10,11... | collective-permute-start | bytes 786440 | tf_op jit(solution)/shard_map/ppermute | solution.py:203
  29.3 1.5 %collective-permute-start.6 = (bf16[8,64,256]{2,1,0:T(8,128)(2,1)S(1)}, bf16[8,64,256]{2,1,0:T(8,128)(2,1)S(1)}, u32[]{:S(2)}, u32[]{:S(2)}) collective-permute-start(bf16[8,64,256]{2,1,0:T(8,128)(2,1)S(1)} %collective-permute-done.5.refs_6_), channel_id=1, source_target_pairs={{0,1},{1,0},{2,3},{3,2},{4,5},{5,4},{6,7},{7,6},{8,9},{9,8},{10,11... | collective-permute-start | bytes 786440 | tf_op jit(solution)/shard_map/ppermute | solution.py:203
  34.6 2.0 %collective-permute-start.11 = (bf16[2,8,64,256]{3,2,1,0:T(8,128)(2,1)S(1)}, bf16[2,8,64,256]{3,2,1,0:T(8,128)(2,1)S(1)}, u32[]{:S(2)}, u32[]{:S(2)}) collective-permute-start(bf16[2,8,64,256]{3,2,1,0:T(8,128)(2,1)S(1)} %get-tuple-element.30), channel_id=1, source_target_pairs={{0,1},{1,0},{2,3},{3,2},{4,5},{5,4},{6,7},{7,6},{8,9},{9,8},{10,11... | collective-permute-start | bytes 1572872 | tf_op jit(solution)/shard_map/ppermute | solution.py:203
  34.8 17.8 %collective-permute-start.17 = (bf16[4,8,64,256]{3,2,1,0:T(8,128)(2,1)S(1)}, bf16[4,8,64,256]{3,2,1,0:T(8,128)(2,1)}, u32[]{:S(2)}, u32[]{:S(2)}) collective-permute-start(bf16[4,8,64,256]{3,2,1,0:T(8,128)(2,1)S(1)} %get-tuple-element.37), channel_id=1, source_target_pairs={{0,1},{1,0},{2,3},{3,2},{4,5},{5,4},{6,7},{7,6},{8,9},{9,8},{10,11... | collective-permute-start | bytes 3145736 | tf_op jit(solution)/shard_map/ppermute | solution.py:203
  35.2 2.1 %collective-permute-start.12 = (f32[256,256]{1,0:T(8,128)S(1)}, f32[256,256]{1,0:T(8,128)S(1)}, u32[]{:S(2)}, u32[]{:S(2)}) collective-permute-start(f32[256,256]{1,0:T(8,128)S(1)} %get-tuple-element.31), channel_id=1, source_target_pairs={{0,1},{1,0},{2,3},{3,2},{4,5},{5,4},{6,7},{7,6},{8,9},{9,8},{10,11... | collective-permute-start | bytes 786440 | tf_op jit(solution)/shard_map/ppermute | solution.py:203
  37.3 15.2 %collective-permute-start.13 = (bf16[2,8,64,256]{3,2,1,0:T(8,128)(2,1)S(1)}, bf16[2,8,64,256]{3,2,1,0:T(8,128)(2,1)}, u32[]{:S(2)}, u32[]{:S(2)}) collective-permute-start(bf16[2,8,64,256]{3,2,1,0:T(8,128)(2,1)S(1)} %add_convert_fusion), channel_id=1, source_target_pairs={{0,2},{1,3},{2,0},{3,1},{4,6},{5,7},{6,4},{7,5},{8,10},{9,11},{10,... | collective-permute-start | bytes 1572872 | tf_op jit(solution)/shard_map/ppermute | solution.py:203
  37.9 4.3 %collective-permute-start.14 = (bf16[128,256]{1,0:T(8,128)(2,1)S(1)}, bf16[128,256]{1,0:T(8,128)(2,1)S(1)}, u32[]{:S(2)}, u32[]{:S(2)}) collective-permute-start(bf16[128,256]{1,0:T(8,128)(2,1)S(1)} %convert_element_type.75), channel_id=1, source_target_pairs={{0,16},{16,0},{1,17},{17,1},{2,18},{18,2},{3,19},{19,3},{4,20},{20... | collective-permute-start | bytes 196616 | tf_op jit(solution)/shard_map/ppermute | solution.py:203
  42.2 5.0 %collective-permute-start.15 = (f32[128,256]{1,0:T(8,128)S(1)}, f32[128,256]{1,0:T(8,128)S(1)}, u32[]{:S(2)}, u32[]{:S(2)}) collective-permute-start(f32[128,256]{1,0:T(8,128)S(1)} %shard_map.88.a_ref), channel_id=1, source_target_pairs={{0,4},{4,0},{8,12},{12,8},{1,5},{5,1},{9,13},{13,9},{2,6},{6,2},{1... | collective-permute-start | bytes 393224 | tf_op jit(solution)/shard_map/ppermute | solution.py:203
  47.3 5.2 %collective-permute-start.16 = (bf16[128,256]{1,0:T(8,128)(2,1)S(1)}, bf16[128,256]{1,0:T(8,128)(2,1)S(1)}, u32[]{:S(2)}, u32[]{:S(2)}) collective-permute-start(bf16[128,256]{1,0:T(8,128)(2,1)S(1)} %shard_map.89.a_ref), channel_id=1, source_target_pairs={{0,8},{4,12},{8,0},{12,4},{1,9},{5,13},{9,1},{13,5},{2,10},{6,14},... | collective-permute-start | bytes 196616 | tf_op jit(solution)/shard_map/ppermute | solution.py:203
  54.2 10.8 %collective-permute-start.21 = (bf16[8,64,256]{2,1,0:T(8,128)(2,1)S(1)}, bf16[8,64,256]{2,1,0:T(8,128)(2,1)S(1)}, u32[]{:S(2)}, u32[]{:S(2)}) collective-permute-start(bf16[8,64,256]{2,1,0:T(8,128)(2,1)S(1)} %get-tuple-element.45), channel_id=1, source_target_pairs={{0,2},{1,3},{2,0},{3,1},{4,6},{5,7},{6,4},{7,5},{8,10},{9,11},{10,... | collective-permute-start | bytes 786440 | tf_op jit(solution)/shard_map/ppermute | solution.py:203
  55.8 7.6 %collective-permute-start.18 = (f32[128,256]{1,0:T(8,128)S(1)}, f32[128,256]{1,0:T(8,128)S(1)}, u32[]{:S(2)}, u32[]{:S(2)}) collective-permute-start(f32[128,256]{1,0:T(8,128)S(1)} %shard_map.90.a_ref), channel_id=1, source_target_pairs={{0,2},{1,3},{2,0},{3,1},{4,6},{5,7},{6,4},{7,5},{8,10},{9,11},{10,... | collective-permute-start | bytes 393224 | tf_op jit(solution)/shard_map/ppermute | solution.py:203
  56.3 12.3 %collective-permute-start.22 = (bf16[8,64,256]{2,1,0:T(8,128)(2,1)S(1)}, bf16[8,64,256]{2,1,0:T(8,128)(2,1)S(1)}, u32[]{:S(2)}, u32[]{:S(2)}) collective-permute-start(bf16[8,64,256]{2,1,0:T(8,128)(2,1)S(1)} %get-tuple-element.43), channel_id=1, source_target_pairs={{4,0},{8,4},{12,8},{0,12},{5,1},{9,5},{13,9},{1,13},{6,2},{10,6},{... | collective-permute-start | bytes 786440 | tf_op jit(solution)/shard_map/ppermute | solution.py:217
  60.3 10.0 %collective-permute-start.23 = (bf16[8,64,256]{2,1,0:T(8,128)(2,1)S(1)}, bf16[8,64,256]{2,1,0:T(8,128)(2,1)S(1)}, u32[]{:S(2)}, u32[]{:S(2)}) collective-permute-start(bf16[8,64,256]{2,1,0:T(8,128)(2,1)S(1)} %get-tuple-element.44), channel_id=1, source_target_pairs={{0,4},{4,8},{8,12},{12,0},{1,5},{5,9},{9,13},{13,1},{2,6},{6,10},{... | collective-permute-start | bytes 786440 | tf_op jit(solution)/shard_map/ppermute | solution.py:213
  63.4 5.0 %collective-permute-start.19 = (f32[128,256]{1,0:T(8,128)S(1)}, f32[128,256]{1,0:T(8,128)S(1)}, u32[]{:S(2)}, u32[]{:S(2)}) collective-permute-start(f32[128,256]{1,0:T(8,128)S(1)} %shard_map.91.refs_0_), channel_id=1, source_target_pairs={{0,16},{16,0},{1,17},{17,1},{2,18},{18,2},{3,19},{19,3},{4,20},{20... | collective-permute-start | bytes 393224 | tf_op jit(solution)/shard_map/ppermute | solution.py:203
  68.5 3.6 %collective-permute-start.20 = (f32[256,256]{1,0:T(8,128)S(1)}, f32[256,256]{1,0:T(8,128)S(1)}, u32[]{:S(2)}, u32[]{:S(2)}) collective-permute-start(f32[256,256]{1,0:T(8,128)S(1)} %shard_map.92), channel_id=1, source_target_pairs={{0,1},{1,0},{2,3},{3,2},{4,5},{5,4},{6,7},{7,6},{8,9},{9,8},{10,11... | collective-permute-start | bytes 786440 | tf_op jit(solution)/shard_map/ppermute | solution.py:203
  (8 other events, 56.3 us)

commit v5 on v4

--- a/solution.py
+++ b/solution.py
@@ -149,11 +149,6 @@
     passed_ref[...] = jnp.where(first, neigh_part, self_part)
 
 
-def own_body(direct_ref, keep_ref, got_ref, half_ref, out_ref):
-    both = keep_ref[3].astype(F32) + got_ref[3].astype(F32)
-    out_ref[...] = direct_ref[...] + (both + half_ref[...].astype(F32))
-
-
 def split_body(place_ref, *refs):
     outs = [r for r in refs if r.shape != refs[0].shape]
     total = tree_sum(r[...] for r in refs[: len(refs) - len(outs)])
@@ -330,13 +325,8 @@
     grad_self = jnp.where(first, whole, other)
     grad_neigh = jnp.where(first, other, whole)
 
-    (own_terms,) = call(
-        own_body,
-        (shape((blocks, BLOCK, width), F32),),
-        (direct.reshape(blocks, BLOCK, width), keep_rest, got_rest, half_own),
-        [VMEM] * 4,
-        [VMEM],
-    )
+    own_terms = direct.reshape(blocks, BLOCK, width) + both(keep_rest[3], got_rest[3]) + half_own.astype(F32)
+    own_terms, from_upper = together(own_terms, from_upper)
     grad_features = own_terms + both(from_upper, from_lower)
     return grad_self, grad_neigh, grad_features.reshape(rows, width)
 

time: 73.4 us -> 72.5 us (0.988)
  Pallas kernels: 9.43 us -> 6.78 us
  waiting for transfers between devices: 30.5 us -> 32.2 us
  other arithmetic: 5.58 us -> 6.4 us
    pallas_call x9 -> x8, Pallas kernels: 9.43 us -> 6.78 us  [call(): pl.pallas_call(body, out_shape=out_shape, in_specs=in_specs, out_specs=ou...]
    ppermute x20, waiting for transfers between devices: 25.5 us -> 27.2 us  [swap(): lax.ppermute(x, axis, [(i, i ^ d) for i in range(lax.axis_size(axis))])]
    add x0 -> x1, other arithmetic: none -> 1.06 us  [on_device(): direct.reshape(blocks, BLOCK, width) + both(keep_rest[3], got_rest[3])]
    add x1, other arithmetic: 1.91 us -> 0.87 us  [on_device(): grad_features = own_terms + both(from_upper, from_lower)]
    convert_element_type x1, other arithmetic: 0.16 us -> 0.96 us  [on_device(): near, got = together(both(keep_near, got_near).astype(BF16), got)]
    unnamed x16 -> x10, local copies, waits for them, and re-layouts: 4.34 us -> 3.63 us
  transfers between devices with their start and end apart: 24 -> 24, of which waited for: 12 -> 12; matrix products, arithmetic and copies ran while one was open for 3% -> 4% of each run, Pallas kernels for 8% -> 4%
where the time goes in v5:
time: 72.5 us; the launch traced here: 72.1 us
  waiting for transfers between devices  32.2 us (44%)
  starting transfers between devices  22.3 us (31%)
  Pallas kernels  6.78 us (9%)
  other arithmetic  6.4 us (9%)
  local copies, waits for them, and re-layouts  3.63 us (5%)
  between operations  0.79 us (1%)
    ppermute x20, waiting for transfers between devices, swap(): lax.ppermute(x, axis, [(i, i ^ d) for i in range(lax.axis_size(axis))])  27.2 us
    ppermute x20, starting transfers between devices, swap(): lax.ppermute(x, axis, [(i, i ^ d) for i in range(lax.axis_size(axis))])  13.2 us
    ppermute x2, starting transfers between devices, down(): return lax.ppermute(x, 'col', [((i + 1) % cols, i) for i in range(cols)])  9.07 us
    pallas_call x8, Pallas kernels, call(): pl.pallas_call(body, out_shape=out_shape, in_specs=in_specs, out_specs=ou...  6.78 us
    ppermute x2, waiting for transfers between devices, up(): return lax.ppermute(x, 'col', [(i, (i + 1) % cols) for i in range(cols)])  4.84 us
    unnamed x10, local copies, waits for them, and re-layouts  3.63 us
    convert_element_type x1, other arithmetic, on_device(): from_lower = up(near[1].astype(BF16))  1.61 us
  transfers between devices with their start and end apart: 24, of which 12 were waited for; matrix products, arithmetic and copies ran while one was open for 4% of the time, Pallas kernels for 4%

profile of v5, /device:TPU:0, one launch (start us, length us, event | category | flops | bytes accessed | tf_op | source)
XLA Modules:
  0.0 72.1 jit_solution(17419024032687637077)
XLA Ops:
  0.6 1.1 %convert_element_type.82 = bf16[512,256]{1,0:T(8,128)(2,1)S(1)} convert(f32[512,256]{1,0:T(8,128)} %feat_hbm.1) | non-fusion elementwise | flops 131072 | bytes 786432 | tf_op jit(solution)/shard_map/convert_element_type | solution.py:214
  1.7 5.1 %collective-permute-start.7 = (bf16[8,64,256]{2,1,0:T(8,128)(2,1)S(1)}, bf16[8,64,256]{2,1,0:T(8,128)(2,1)S(1)}, u32[]{:S(2)}, u32[]{:S(2)}) collective-permute-start(bf16[8,64,256]{2,1,0:T(8,128)(2,1)S(1)} %bitcast.15), channel_id=1, source_target_pairs={{4,0},{8,4},{12,8},{0,12},{5,1},{9,5},{13,9},{1,13},{6,2},{10,6},{... | collective-permute-start | bytes 786440 | tf_op jit(solution)/shard_map/ppermute | solution.py:212
  6.8 1.5 %collective-permute-start.1 = (bf16[8,64,256]{2,1,0:T(8,128)(2,1)S(1)}, bf16[8,64,256]{2,1,0:T(8,128)(2,1)S(1)}, u32[]{:S(2)}, u32[]{:S(2)}) collective-permute-start(bf16[8,64,256]{2,1,0:T(8,128)(2,1)S(1)} %bitcast.17), channel_id=1, source_target_pairs={{0,2},{1,3},{2,0},{3,1},{4,6},{5,7},{6,4},{7,5},{8,10},{9,11},{10,... | collective-permute-start | bytes 786440 | tf_op jit(solution)/shard_map/ppermute | solution.py:198
  12.0 2.9 %shard_map.85 = (bf16[1792,512]{1,0:T(8,128)(2,1)S(1)}, f32[512,512]{1,0:T(8,128)S(1)}) custom-call(s32[8,8,64,64]{3,2,1,0:T(8,128)} %edge_hbm.1, f32[512,256]{1,0:T(8,128)S(1)} %copy-done, f32[256,256]{1,0:T(8,128)S(1)} %copy-done.1, f32[256,256]{1,0:T(8,128)S(1)} %copy-done.2, s32[4,128]{1,0:T(4,128)S(1)} %bitcast.21), custom_call_target="tpu_custom_call" | custom-call | flops 201326592 | bytes 4982784 | tf_op jit(solution)/shard_map/pallas_call | solution.py:25
  15.5 3.4 %collective-permute-done.3.refs_4_ = bf16[8,64,256]{2,1,0:T(8,128)(2,1)S(1)} collective-permute-done((bf16[8,64,256]{2,1,0:T(8,128)(2,1)S(1)}, bf16[8,64,256]{2,1,0:T(8,128)(2,1)S(1)}, u32[]{:S(2)}, u32[]{:S(2)}) %collective-permute-start.3) | collective-permute-done | bytes 262176 | tf_op jit(solution)/shard_map/ppermute | solution.py:208
  18.9 1.5 %collective-permute-start.5 = (bf16[8,64,256]{2,1,0:T(8,128)(2,1)S(1)}, bf16[8,64,256]{2,1,0:T(8,128)(2,1)S(1)}, u32[]{:S(2)}, u32[]{:S(2)}) collective-permute-start(bf16[8,64,256]{2,1,0:T(8,128)(2,1)S(1)} %collective-permute-done.3.refs_4_), channel_id=1, source_target_pairs={{0,2},{1,3},{2,0},{3,1},{4,6},{5,7},{6,4},{7,5},{8,10},{9,11},{10,... | collective-permute-start | bytes 786440 | tf_op jit(solution)/shard_map/ppermute | solution.py:198
  21.0 3.1 %collective-permute-done.9.refs_10_ = bf16[8,64,256]{2,1,0:T(8,128)(2,1)S(1)} collective-permute-done((bf16[8,64,256]{2,1,0:T(8,128)(2,1)S(1)}, bf16[8,64,256]{2,1,0:T(8,128)(2,1)S(1)}, u32[]{:S(2)}, u32[]{:S(2)}) %collective-permute-start.9) | collective-permute-done | bytes 262176 | tf_op jit(solution)/shard_map/ppermute | solution.py:198
  24.1 5.2 %collective-permute-done.5.refs_6_ = bf16[8,64,256]{2,1,0:T(8,128)(2,1)S(1)} collective-permute-done((bf16[8,64,256]{2,1,0:T(8,128)(2,1)S(1)}, bf16[8,64,256]{2,1,0:T(8,128)(2,1)S(1)}, u32[]{:S(2)}, u32[]{:S(2)}) %collective-permute-start.5) | collective-permute-done | bytes 262176 | tf_op jit(solution)/shard_map/ppermute | solution.py:198
  29.4 1.5 %collective-permute-done.6.refs_7_ = bf16[8,64,256]{2,1,0:T(8,128)(2,1)S(1)} collective-permute-done((bf16[8,64,256]{2,1,0:T(8,128)(2,1)S(1)}, bf16[8,64,256]{2,1,0:T(8,128)(2,1)S(1)}, u32[]{:S(2)}, u32[]{:S(2)}) %collective-permute-start.6) | collective-permute-done | bytes 262176 | tf_op jit(solution)/shard_map/ppermute | solution.py:198
  30.9 3.7 %shard_map.86 = (bf16[2,8,64,256]{3,2,1,0:T(8,128)(2,1)S(1)}, bf16[4,8,64,256]{3,2,1,0:T(8,128)(2,1)S(1)}, bf16[2,8,64,256]{3,2,1,0:T(8,128)(2,1)S(1)}, bf16[4,8...) custom-call(bf16[8,64,256]{2,1,0:T(8,128)(2,1)S(1)} %bitcast.19, ...), custom_call_target="tpu_custom_call" | custom-call | flops 1342177280 | bytes 10223872 | tf_op jit(solution)/shard_map/pallas_call | solution.py:25
  35.3 1.3 %collective-permute-done.11 = bf16[2,8,64,256]{3,2,1,0:T(8,128)(2,1)S(1)} collective-permute-done((bf16[2,8,64,256]{3,2,1,0:T(8,128)(2,1)S(1)}, bf16[2,8,64,256]{3,2,1,0:T(8,128)(2,1)S(1)}, u32[]{:S(2)}, u32[]{:S(2)}) %collective-permute-start.11) | collective-permute-done | bytes 524320 | tf_op jit(solution)/shard_map/ppermute | solution.py:198
  38.1 1.6 %collective-permute-start.14 = (bf16[128,256]{1,0:T(8,128)(2,1)S(1)}, bf16[128,256]{1,0:T(8,128)(2,1)S(1)}, u32[]{:S(2)}, u32[]{:S(2)}) collective-permute-start(bf16[128,256]{1,0:T(8,128)(2,1)S(1)} %convert_element_type.86), channel_id=1, source_target_pairs={{0,16},{16,0},{1,17},{17,1},{2,18},{18,2},{3,19},{19,3},{4,20},{20... | collective-permute-start | bytes 196616 | tf_op jit(solution)/shard_map/ppermute | solution.py:198
  39.6 2.8 %collective-permute-done.14.b_ref = bf16[128,256]{1,0:T(8,128)(2,1)S(1)} collective-permute-done((bf16[128,256]{1,0:T(8,128)(2,1)S(1)}, bf16[128,256]{1,0:T(8,128)(2,1)S(1)}, u32[]{:S(2)}, u32[]{:S(2)}) %collective-permute-start.14) | collective-permute-done | bytes 65568 | tf_op jit(solution)/shard_map/ppermute | solution.py:198
  42.5 5.0 %collective-permute-done.15.b_ref = f32[128,256]{1,0:T(8,128)S(1)} collective-permute-done((f32[128,256]{1,0:T(8,128)S(1)}, f32[128,256]{1,0:T(8,128)S(1)}, u32[]{:S(2)}, u32[]{:S(2)}) %collective-permute-start.15) | collective-permute-done | bytes 131104 | tf_op jit(solution)/shard_map/ppermute | solution.py:198
  47.5 2.4 %collective-permute-start.16 = (bf16[128,256]{1,0:T(8,128)(2,1)S(1)}, bf16[128,256]{1,0:T(8,128)(2,1)S(1)}, u32[]{:S(2)}, u32[]{:S(2)}) collective-permute-start(bf16[128,256]{1,0:T(8,128)(2,1)S(1)} %shard_map.89.a_ref), channel_id=1, source_target_pairs={{0,8},{4,12},{8,0},{12,4},{1,9},{5,13},{9,1},{13,5},{2,10},{6,14},... | collective-permute-start | bytes 196616 | tf_op jit(solution)/shard_map/ppermute | solution.py:198
  49.9 2.8 %collective-permute-done.16.b_ref = bf16[128,256]{1,0:T(8,128)(2,1)S(1)} collective-permute-done((bf16[128,256]{1,0:T(8,128)(2,1)S(1)}, bf16[128,256]{1,0:T(8,128)(2,1)S(1)}, u32[]{:S(2)}, u32[]{:S(2)}) %collective-permute-start.16) | collective-permute-done | bytes 65568 | tf_op jit(solution)/shard_map/ppermute | solution.py:198
  52.8 1.6 %fusion.3 = (bf16[8,64,256]{2,1,0:T(8,128)(2,1)S(1)}, bf16[8,64,256]{2,1,0:T(8,128)(2,1)S(1)}, bf16[8,64,256]{2,1,0:T(8,128)(2,1)S(1)}) fusion(bf16[2,8,64,256]{3,2,1,0:T(8,128)(2,1)} %collective-permute-done.13, bf16[4,8,64,256]{3,2,1,0:T(8,128)(2,1)} %collective-permute-done.17, bf16[4,8,64,256]{3,2,1,0:T(8,128)(2,1)S(1)} %get-tuple-element.42), kind=kLoop, calls=%fused_computation.9 | loop fusion | flops 2097152 | bytes 2883584 | tf_op jit(solution)/shard_map/convert_element_type | solution.py:319
  54.4 1.6 %collective-permute-start.21 = (bf16[8,64,256]{2,1,0:T(8,128)(2,1)S(1)}, bf16[8,64,256]{2,1,0:T(8,128)(2,1)S(1)}, u32[]{:S(2)}, u32[]{:S(2)}) collective-permute-start(bf16[8,64,256]{2,1,0:T(8,128)(2,1)S(1)} %get-tuple-element.49), channel_id=1, source_target_pairs={{0,2},{1,3},{2,0},{3,1},{4,6},{5,7},{6,4},{7,5},{8,10},{9,11},{10,... | collective-permute-start | bytes 786440 | tf_op jit(solution)/shard_map/ppermute | solution.py:198
  56.5 4.0 %collective-permute-start.22 = (bf16[8,64,256]{2,1,0:T(8,128)(2,1)S(1)}, bf16[8,64,256]{2,1,0:T(8,128)(2,1)S(1)}, u32[]{:S(2)}, u32[]{:S(2)}) collective-permute-start(bf16[8,64,256]{2,1,0:T(8,128)(2,1)S(1)} %get-tuple-element.48), channel_id=1, source_target_pairs={{4,0},{8,4},{12,8},{0,12},{5,1},{9,5},{13,9},{1,13},{6,2},{10,6},{... | collective-permute-start | bytes 786440 | tf_op jit(solution)/shard_map/ppermute | solution.py:212
  60.4 3.4 %collective-permute-done.18.b_ref = f32[128,256]{1,0:T(8,128)S(1)} collective-permute-done((f32[128,256]{1,0:T(8,128)S(1)}, f32[128,256]{1,0:T(8,128)S(1)}, u32[]{:S(2)}, u32[]{:S(2)}) %collective-permute-start.18) | collective-permute-done | bytes 131104 | tf_op jit(solution)/shard_map/ppermute | solution.py:198
  63.8 1.6 %collective-permute-start.19 = (f32[128,256]{1,0:T(8,128)S(1)}, f32[128,256]{1,0:T(8,128)S(1)}, u32[]{:S(2)}, u32[]{:S(2)}) collective-permute-start(f32[128,256]{1,0:T(8,128)S(1)} %shard_map.91.refs_0_), channel_id=1, source_target_pairs={{0,16},{16,0},{1,17},{17,1},{2,18},{18,2},{3,19},{19,3},{4,20},{20... | collective-permute-start | bytes 393224 | tf_op jit(solution)/shard_map/ppermute | solution.py:198
  65.4 1.1 %fusion = f32[8,64,256]{2,1,0:T(8,128)S(1)} fusion(f32[8,64,256]{2,1,0:T(8,128)S(1)} %bitcast.20, bf16[8,64,256]{2,1,0:T(8,128)(2,1)S(1)} %collective-permute-done.21, bf16[4,8,64,256]{3,2,1,0:T(8,128)(2,1)} %collective-permute-done.17, bf16[4,8,64,256]{3,2,1,0:T(8,128)(2,1)S(1)} %get-tuple-element.42), kind=kLoop, calls=%fused_computation.2 | loop fusion | flops 786432 | bytes 1835008 | tf_op jit(solution)/shard_map/add | solution.py:328
  66.6 2.2 %collective-permute-done.19.refs_1_ = f32[128,256]{1,0:T(8,128)S(1)} collective-permute-done((f32[128,256]{1,0:T(8,128)S(1)}, f32[128,256]{1,0:T(8,128)S(1)}, u32[]{:S(2)}, u32[]{:S(2)}) %collective-permute-start.19) | collective-permute-done | bytes 131104 | tf_op jit(solution)/shard_map/ppermute | solution.py:198
  69.0 1.4 %collective-permute-done.23 = bf16[8,64,256]{2,1,0:T(8,128)(2,1)S(1)} collective-permute-done((bf16[8,64,256]{2,1,0:T(8,128)(2,1)S(1)}, bf16[8,64,256]{2,1,0:T(8,128)(2,1)S(1)}, u32[]{:S(2)}, u32[]{:S(2)}) %collective-permute-start.23) | collective-permute-done | bytes 262176 | tf_op jit(solution)/shard_map/ppermute | solution.py:208
  (49 shorter events, 9.7 us)
Async XLA Ops:
  1.7 13.2 %collective-permute-start.7 = (bf16[8,64,256]{2,1,0:T(8,128)(2,1)S(1)}, bf16[8,64,256]{2,1,0:T(8,128)(2,1)S(1)}, u32[]{:S(2)}, u32[]{:S(2)}) collective-permute-start(bf16[8,64,256]{2,1,0:T(8,128)(2,1)S(1)} %bitcast.15), channel_id=1, source_target_pairs={{4,0},{8,4},{12,8},{0,12},{5,1},{9,5},{13,9},{1,13},{6,2},{10,6},{... | collective-permute-start | bytes 786440 | tf_op jit(solution)/shard_map/ppermute | solution.py:212
  6.8 12.1 %collective-permute-start.3 = (bf16[8,64,256]{2,1,0:T(8,128)(2,1)S(1)}, bf16[8,64,256]{2,1,0:T(8,128)(2,1)S(1)}, u32[]{:S(2)}, u32[]{:S(2)}) collective-permute-start(bf16[8,64,256]{2,1,0:T(8,128)(2,1)S(1)} %bitcast.16), channel_id=1, source_target_pairs={{0,4},{4,8},{8,12},{12,0},{1,5},{5,9},{9,13},{13,1},{2,6},{6,10},{... | collective-permute-start | bytes 786440 | tf_op jit(solution)/shard_map/ppermute | solution.py:208
  6.8 13.6 %collective-permute-start.1 = (bf16[8,64,256]{2,1,0:T(8,128)(2,1)S(1)}, bf16[8,64,256]{2,1,0:T(8,128)(2,1)S(1)}, u32[]{:S(2)}, u32[]{:S(2)}) collective-permute-start(bf16[8,64,256]{2,1,0:T(8,128)(2,1)S(1)} %bitcast.17), channel_id=1, source_target_pairs={{0,2},{1,3},{2,0},{3,1},{4,6},{5,7},{6,4},{7,5},{8,10},{9,11},{10,... | collective-permute-start | bytes 786440 | tf_op jit(solution)/shard_map/ppermute | solution.py:198
  8.3 12.6 %collective-permute-start = (bf16[8,64,256]{2,1,0:T(8,128)(2,1)S(1)}, bf16[8,64,256]{2,1,0:T(8,128)(2,1)S(1)}, u32[]{:S(2)}, u32[]{:S(2)}) collective-permute-start(bf16[8,64,256]{2,1,0:T(8,128)(2,1)S(1)} %bitcast.18), channel_id=1, source_target_pairs={{0,1},{1,0},{2,3},{3,2},{4,5},{5,4},{6,7},{7,6},{8,9},{9,8},{10,11... | collective-permute-start | bytes 786440 | tf_op jit(solution)/shard_map/ppermute | solution.py:198
  14.9 9.2 %collective-permute-start.9 = (bf16[8,64,256]{2,1,0:T(8,128)(2,1)S(1)}, bf16[8,64,256]{2,1,0:T(8,128)(2,1)S(1)}, u32[]{:S(2)}, u32[]{:S(2)}) collective-permute-start(bf16[8,64,256]{2,1,0:T(8,128)(2,1)S(1)} %collective-permute-done.7.refs_8_), channel_id=1, source_target_pairs={{0,2},{1,3},{2,0},{3,1},{4,6},{5,7},{6,4},{7,5},{8,10},{9,11},{10,... | collective-permute-start | bytes 786440 | tf_op jit(solution)/shard_map/ppermute | solution.py:198
  18.9 10.4 %collective-permute-start.5 = (bf16[8,64,256]{2,1,0:T(8,128)(2,1)S(1)}, bf16[8,64,256]{2,1,0:T(8,128)(2,1)S(1)}, u32[]{:S(2)}, u32[]{:S(2)}) collective-permute-start(bf16[8,64,256]{2,1,0:T(8,128)(2,1)S(1)} %collective-permute-done.3.refs_4_), channel_id=1, source_target_pairs={{0,2},{1,3},{2,0},{3,1},{4,6},{5,7},{6,4},{7,5},{8,10},{9,11},{10,... | collective-permute-start | bytes 786440 | tf_op jit(solution)/shard_map/ppermute | solution.py:198
  20.4 8.9 %collective-permute-start.4 = (bf16[8,64,256]{2,1,0:T(8,128)(2,1)S(1)}, bf16[8,64,256]{2,1,0:T(8,128)(2,1)S(1)}, u32[]{:S(2)}, u32[]{:S(2)}) collective-permute-start(bf16[8,64,256]{2,1,0:T(8,128)(2,1)S(1)} %collective-permute-done.3.refs_4_), channel_id=1, source_target_pairs={{0,1},{1,0},{2,3},{3,2},{4,5},{5,4},{6,7},{7,6},{8,9},{9,8},{10,11... | collective-permute-start | bytes 786440 | tf_op jit(solution)/shard_map/ppermute | solution.py:198
  20.4 8.9 %collective-permute-start.8 = (bf16[8,64,256]{2,1,0:T(8,128)(2,1)S(1)}, bf16[8,64,256]{2,1,0:T(8,128)(2,1)S(1)}, u32[]{:S(2)}, u32[]{:S(2)}) collective-permute-start(bf16[8,64,256]{2,1,0:T(8,128)(2,1)S(1)} %collective-permute-done.7.refs_8_), channel_id=1, source_target_pairs={{0,1},{1,0},{2,3},{3,2},{4,5},{5,4},{6,7},{7,6},{8,9},{9,8},{10,11... | collective-permute-start | bytes 786440 | tf_op jit(solution)/shard_map/ppermute | solution.py:198
  20.9 8.4 %collective-permute-start.2 = (bf16[8,64,256]{2,1,0:T(8,128)(2,1)S(1)}, bf16[8,64,256]{2,1,0:T(8,128)(2,1)S(1)}, u32[]{:S(2)}, u32[]{:S(2)}) collective-permute-start(bf16[8,64,256]{2,1,0:T(8,128)(2,1)S(1)} %collective-permute-done.1.refs_2_), channel_id=1, source_target_pairs={{0,1},{1,0},{2,3},{3,2},{4,5},{5,4},{6,7},{7,6},{8,9},{9,8},{10,11... | collective-permute-start | bytes 786440 | tf_op jit(solution)/shard_map/ppermute | solution.py:198
  24.1 5.3 %collective-permute-start.10 = (bf16[8,64,256]{2,1,0:T(8,128)(2,1)S(1)}, bf16[8,64,256]{2,1,0:T(8,128)(2,1)S(1)}, u32[]{:S(2)}, u32[]{:S(2)}) collective-permute-start(bf16[8,64,256]{2,1,0:T(8,128)(2,1)S(1)} %collective-permute-done.9.refs_10_), channel_id=1, source_target_pairs={{0,1},{1,0},{2,3},{3,2},{4,5},{5,4},{6,7},{7,6},{8,9},{9,8},{10,11... | collective-permute-start | bytes 786440 | tf_op jit(solution)/shard_map/ppermute | solution.py:198
  29.3 1.5 %collective-permute-start.6 = (bf16[8,64,256]{2,1,0:T(8,128)(2,1)S(1)}, bf16[8,64,256]{2,1,0:T(8,128)(2,1)S(1)}, u32[]{:S(2)}, u32[]{:S(2)}) collective-permute-start(bf16[8,64,256]{2,1,0:T(8,128)(2,1)S(1)} %collective-permute-done.5.refs_6_), channel_id=1, source_target_pairs={{0,1},{1,0},{2,3},{3,2},{4,5},{5,4},{6,7},{7,6},{8,9},{9,8},{10,11... | collective-permute-start | bytes 786440 | tf_op jit(solution)/shard_map/ppermute | solution.py:198
  34.6 2.0 %collective-permute-start.11 = (bf16[2,8,64,256]{3,2,1,0:T(8,128)(2,1)S(1)}, bf16[2,8,64,256]{3,2,1,0:T(8,128)(2,1)S(1)}, u32[]{:S(2)}, u32[]{:S(2)}) collective-permute-start(bf16[2,8,64,256]{3,2,1,0:T(8,128)(2,1)S(1)} %get-tuple-element.32), channel_id=1, source_target_pairs={{0,1},{1,0},{2,3},{3,2},{4,5},{5,4},{6,7},{7,6},{8,9},{9,8},{10,11... | collective-permute-start | bytes 1572872 | tf_op jit(solution)/shard_map/ppermute | solution.py:198
  34.8 18.0 %collective-permute-start.17 = (bf16[4,8,64,256]{3,2,1,0:T(8,128)(2,1)S(1)}, bf16[4,8,64,256]{3,2,1,0:T(8,128)(2,1)}, u32[]{:S(2)}, u32[]{:S(2)}) collective-permute-start(bf16[4,8,64,256]{3,2,1,0:T(8,128)(2,1)S(1)} %get-tuple-element.39), channel_id=1, source_target_pairs={{0,1},{1,0},{2,3},{3,2},{4,5},{5,4},{6,7},{7,6},{8,9},{9,8},{10,11... | collective-permute-start | bytes 3145736 | tf_op jit(solution)/shard_map/ppermute | solution.py:198
  35.1 2.4 %collective-permute-start.12 = (f32[256,256]{1,0:T(8,128)S(1)}, f32[256,256]{1,0:T(8,128)S(1)}, u32[]{:S(2)}, u32[]{:S(2)}) collective-permute-start(f32[256,256]{1,0:T(8,128)S(1)} %get-tuple-element.33), channel_id=1, source_target_pairs={{0,1},{1,0},{2,3},{3,2},{4,5},{5,4},{6,7},{7,6},{8,9},{9,8},{10,11... | collective-permute-start | bytes 786440 | tf_op jit(solution)/shard_map/ppermute | solution.py:198
  37.5 15.2 %collective-permute-start.13 = (bf16[2,8,64,256]{3,2,1,0:T(8,128)(2,1)}, bf16[2,8,64,256]{3,2,1,0:T(8,128)(2,1)}, u32[]{:S(2)}, u32[]{:S(2)}) collective-permute-start(bf16[2,8,64,256]{3,2,1,0:T(8,128)(2,1)} %add_convert_fusion), channel_id=1, source_target_pairs={{0,2},{1,3},{2,0},{3,1},{4,6},{5,7},{6,4},{7,5},{8,10},{9,11},{10,... | collective-permute-start | bytes 1572872 | tf_op jit(solution)/shard_map/ppermute | solution.py:198
  38.1 4.3 %collective-permute-start.14 = (bf16[128,256]{1,0:T(8,128)(2,1)S(1)}, bf16[128,256]{1,0:T(8,128)(2,1)S(1)}, u32[]{:S(2)}, u32[]{:S(2)}) collective-permute-start(bf16[128,256]{1,0:T(8,128)(2,1)S(1)} %convert_element_type.86), channel_id=1, source_target_pairs={{0,16},{16,0},{1,17},{17,1},{2,18},{18,2},{3,19},{19,3},{4,20},{20... | collective-permute-start | bytes 196616 | tf_op jit(solution)/shard_map/ppermute | solution.py:198
  42.4 5.0 %collective-permute-start.15 = (f32[128,256]{1,0:T(8,128)S(1)}, f32[128,256]{1,0:T(8,128)S(1)}, u32[]{:S(2)}, u32[]{:S(2)}) collective-permute-start(f32[128,256]{1,0:T(8,128)S(1)} %shard_map.88.a_ref), channel_id=1, source_target_pairs={{0,4},{4,0},{8,12},{12,8},{1,5},{5,1},{9,13},{13,9},{2,6},{6,2},{1... | collective-permute-start | bytes 393224 | tf_op jit(solution)/shard_map/ppermute | solution.py:198
  47.5 5.2 %collective-permute-start.16 = (bf16[128,256]{1,0:T(8,128)(2,1)S(1)}, bf16[128,256]{1,0:T(8,128)(2,1)S(1)}, u32[]{:S(2)}, u32[]{:S(2)}) collective-permute-start(bf16[128,256]{1,0:T(8,128)(2,1)S(1)} %shard_map.89.a_ref), channel_id=1, source_target_pairs={{0,8},{4,12},{8,0},{12,4},{1,9},{5,13},{9,1},{13,5},{2,10},{6,14},... | collective-permute-start | bytes 196616 | tf_op jit(solution)/shard_map/ppermute | solution.py:198
  54.4 11.0 %collective-permute-start.21 = (bf16[8,64,256]{2,1,0:T(8,128)(2,1)S(1)}, bf16[8,64,256]{2,1,0:T(8,128)(2,1)S(1)}, u32[]{:S(2)}, u32[]{:S(2)}) collective-permute-start(bf16[8,64,256]{2,1,0:T(8,128)(2,1)S(1)} %get-tuple-element.49), channel_id=1, source_target_pairs={{0,2},{1,3},{2,0},{3,1},{4,6},{5,7},{6,4},{7,5},{8,10},{9,11},{10,... | collective-permute-start | bytes 786440 | tf_op jit(solution)/shard_map/ppermute | solution.py:198
  56.0 7.8 %collective-permute-start.18 = (f32[128,256]{1,0:T(8,128)S(1)}, f32[128,256]{1,0:T(8,128)S(1)}, u32[]{:S(2)}, u32[]{:S(2)}) collective-permute-start(f32[128,256]{1,0:T(8,128)S(1)} %shard_map.90.a_ref), channel_id=1, source_target_pairs={{0,2},{1,3},{2,0},{3,1},{4,6},{5,7},{6,4},{7,5},{8,10},{9,11},{10,... | collective-permute-start | bytes 393224 | tf_op jit(solution)/shard_map/ppermute | solution.py:198
  56.5 10.2 %collective-permute-start.22 = (bf16[8,64,256]{2,1,0:T(8,128)(2,1)S(1)}, bf16[8,64,256]{2,1,0:T(8,128)(2,1)S(1)}, u32[]{:S(2)}, u32[]{:S(2)}) collective-permute-start(bf16[8,64,256]{2,1,0:T(8,128)(2,1)S(1)} %get-tuple-element.48), channel_id=1, source_target_pairs={{4,0},{8,4},{12,8},{0,12},{5,1},{9,5},{13,9},{1,13},{6,2},{10,6},{... | collective-permute-start | bytes 786440 | tf_op jit(solution)/shard_map/ppermute | solution.py:212
  60.4 10.0 %collective-permute-start.23 = (bf16[8,64,256]{2,1,0:T(8,128)(2,1)S(1)}, bf16[8,64,256]{2,1,0:T(8,128)(2,1)S(1)}, u32[]{:S(2)}, u32[]{:S(2)}) collective-permute-start(bf16[8,64,256]{2,1,0:T(8,128)(2,1)S(1)} %get-tuple-element.47), channel_id=1, source_target_pairs={{0,4},{4,8},{8,12},{12,0},{1,5},{5,9},{9,13},{13,1},{2,6},{6,10},{... | collective-permute-start | bytes 786440 | tf_op jit(solution)/shard_map/ppermute | solution.py:208
  63.8 5.0 %collective-permute-start.19 = (f32[128,256]{1,0:T(8,128)S(1)}, f32[128,256]{1,0:T(8,128)S(1)}, u32[]{:S(2)}, u32[]{:S(2)}) collective-permute-start(f32[128,256]{1,0:T(8,128)S(1)} %shard_map.91.refs_0_), channel_id=1, source_target_pairs={{0,16},{16,0},{1,17},{17,1},{2,18},{18,2},{3,19},{19,3},{4,20},{20... | collective-permute-start | bytes 393224 | tf_op jit(solution)/shard_map/ppermute | solution.py:198
  68.9 2.4 %collective-permute-start.20 = (f32[256,256]{1,0:T(8,128)S(1)}, f32[256,256]{1,0:T(8,128)S(1)}, u32[]{:S(2)}, u32[]{:S(2)}) collective-permute-start(f32[256,256]{1,0:T(8,128)S(1)} %shard_map.92), channel_id=1, source_target_pairs={{0,1},{1,0},{2,3},{3,2},{4,5},{5,4},{6,7},{7,6},{8,9},{9,8},{10,11... | collective-permute-start | bytes 786440 | tf_op jit(solution)/shard_map/ppermute | solution.py:198
  (5 other events, 33.9 us)

commit v6 on v5

--- a/solution.py
+++ b/solution.py
@@ -232,7 +232,7 @@
         flops=6 * rows * width * classes,
         vmem=50,
     )
-    half, lower, upper, core = (lax.optimization_barrier((x, full))[0] for x in (half, lower, upper, core))
+    half, lower, core = (lax.optimization_barrier((x, full))[0] for x in (half, lower, core))
     lower_half, upper_half = half_swap(lower), half_swap(upper)
     pieces = [
         own, core, half, core_swap(half),

time: 72.5 us -> 71.9 us (level)
  starting transfers between devices: 22.3 us -> 19.7 us
  waiting for transfers between devices: 32.2 us -> 34.2 us
    ppermute x2, waiting for transfers between devices: 4.84 us -> 0.01 us  [up(): return lax.ppermute(x, 'col', [(i, (i + 1) % cols) for i in range(cols)])]
    ppermute x20, waiting for transfers between devices: 27.2 us -> 31.8 us  [swap(): lax.ppermute(x, axis, [(i, i ^ d) for i in range(lax.axis_size(axis))])]
    ppermute x2, starting transfers between devices: 9.07 us -> 4.57 us  [down(): return lax.ppermute(x, 'col', [((i + 1) % cols, i) for i in range(cols)])]
    ppermute x2, starting transfers between devices: 0.01 us -> 3.08 us  [up(): return lax.ppermute(x, 'col', [(i, (i + 1) % cols) for i in range(cols)])]
    ppermute x2, waiting for transfers between devices: 0.21 us -> 2.42 us  [down(): return lax.ppermute(x, 'col', [((i + 1) % cols, i) for i in range(cols)])]
    ppermute x20, starting transfers between devices: 13.2 us -> 12.1 us  [swap(): lax.ppermute(x, axis, [(i, i ^ d) for i in range(lax.axis_size(axis))])]
  transfers between devices with their start and end apart: 24 -> 24, of which waited for: 12 -> 11; matrix products, arithmetic and copies ran while one was open for 4% -> 4% of each run, Pallas kernels for 4% -> 4%
where the time goes in v6:
time: 71.9 us; the launch traced here: 71.5 us
  waiting for transfers between devices  34.2 us (48%)
  starting transfers between devices  19.7 us (27%)
  Pallas kernels  6.78 us (9%)
  other arithmetic  6.41 us (9%)
  local copies, waits for them, and re-layouts  3.63 us (5%)
  between operations  0.8 us (1%)
    ppermute x20, waiting for transfers between devices, swap(): lax.ppermute(x, axis, [(i, i ^ d) for i in range(lax.axis_size(axis))])  31.8 us
    ppermute x20, starting transfers between devices, swap(): lax.ppermute(x, axis, [(i, i ^ d) for i in range(lax.axis_size(axis))])  12.1 us
    pallas_call x8, Pallas kernels, call(): pl.pallas_call(body, out_shape=out_shape, in_specs=in_specs, out_specs=ou...  6.78 us
    ppermute x2, starting transfers between devices, down(): return lax.ppermute(x, 'col', [((i + 1) % cols, i) for i in range(cols)])  4.57 us
    unnamed x10, local copies, waits for them, and re-layouts  3.63 us
    ppermute x2, starting transfers between devices, up(): return lax.ppermute(x, 'col', [(i, (i + 1) % cols) for i in range(cols)])  3.08 us
    ppermute x2, waiting for transfers between devices, down(): return lax.ppermute(x, 'col', [((i + 1) % cols, i) for i in range(cols)])  2.42 us
    convert_element_type x1, other arithmetic, on_device(): from_lower = up(near[1].astype(BF16))  1.61 us
  transfers between devices with their start and end apart: 24, of which 11 were waited for; matrix products, arithmetic and copies ran while one was open for 4% of the time, Pallas kernels for 4%

profile of v6, /device:TPU:0, one launch (start us, length us, event | category | flops | bytes accessed | tf_op | source)
XLA Modules:
  0.0 71.5 jit_solution(10397056763449361246)
XLA Ops:
  0.6 1.1 %convert_element_type.82 = bf16[512,256]{1,0:T(8,128)(2,1)S(1)} convert(f32[512,256]{1,0:T(8,128)} %feat_hbm.1) | non-fusion elementwise | flops 131072 | bytes 786432 | tf_op jit(solution)/shard_map/convert_element_type | solution.py:214
  1.7 3.1 %collective-permute-start.3 = (bf16[8,64,256]{2,1,0:T(8,128)(2,1)S(1)}, bf16[8,64,256]{2,1,0:T(8,128)(2,1)S(1)}, u32[]{:S(2)}, u32[]{:S(2)}) collective-permute-start(bf16[8,64,256]{2,1,0:T(8,128)(2,1)S(1)} %bitcast.15), channel_id=1, source_target_pairs={{0,4},{4,8},{8,12},{12,0},{1,5},{5,9},{9,13},{13,1},{2,6},{6,10},{... | collective-permute-start | bytes 786440 | tf_op jit(solution)/shard_map/ppermute | solution.py:208
  4.8 2.1 %collective-permute-start.7 = (bf16[8,64,256]{2,1,0:T(8,128)(2,1)S(1)}, bf16[8,64,256]{2,1,0:T(8,128)(2,1)S(1)}, u32[]{:S(2)}, u32[]{:S(2)}) collective-permute-start(bf16[8,64,256]{2,1,0:T(8,128)(2,1)S(1)} %bitcast.16), channel_id=1, source_target_pairs={{4,0},{8,4},{12,8},{0,12},{5,1},{9,5},{13,9},{1,13},{6,2},{10,6},{... | collective-permute-start | bytes 786440 | tf_op jit(solution)/shard_map/ppermute | solution.py:212
  6.9 1.7 %collective-permute-start.1 = (bf16[8,64,256]{2,1,0:T(8,128)(2,1)S(1)}, bf16[8,64,256]{2,1,0:T(8,128)(2,1)S(1)}, u32[]{:S(2)}, u32[]{:S(2)}) collective-permute-start(bf16[8,64,256]{2,1,0:T(8,128)(2,1)S(1)} %bitcast.17), channel_id=1, source_target_pairs={{0,2},{1,3},{2,0},{3,1},{4,6},{5,7},{6,4},{7,5},{8,10},{9,11},{10,... | collective-permute-start | bytes 786440 | tf_op jit(solution)/shard_map/ppermute | solution.py:198
  12.2 2.9 %shard_map.85 = (bf16[1792,512]{1,0:T(8,128)(2,1)S(1)}, f32[512,512]{1,0:T(8,128)S(1)}) custom-call(s32[8,8,64,64]{3,2,1,0:T(8,128)} %edge_hbm.1, f32[512,256]{1,0:T(8,128)S(1)} %copy-done, f32[256,256]{1,0:T(8,128)S(1)} %copy-done.1, f32[256,256]{1,0:T(8,128)S(1)} %copy-done.2, s32[4,128]{1,0:T(4,128)S(1)} %bitcast.21), custom_call_target="tpu_custom_call" | custom-call | flops 201326592 | bytes 4982784 | tf_op jit(solution)/shard_map/pallas_call | solution.py:25
  15.8 2.4 %collective-permute-done.7.refs_8_ = bf16[8,64,256]{2,1,0:T(8,128)(2,1)S(1)} collective-permute-done((bf16[8,64,256]{2,1,0:T(8,128)(2,1)S(1)}, bf16[8,64,256]{2,1,0:T(8,128)(2,1)S(1)}, u32[]{:S(2)}, u32[]{:S(2)}) %collective-permute-start.7) | collective-permute-done | bytes 262176 | tf_op jit(solution)/shard_map/ppermute | solution.py:212
  18.2 1.5 %collective-permute-start.9 = (bf16[8,64,256]{2,1,0:T(8,128)(2,1)S(1)}, bf16[8,64,256]{2,1,0:T(8,128)(2,1)S(1)}, u32[]{:S(2)}, u32[]{:S(2)}) collective-permute-start(bf16[8,64,256]{2,1,0:T(8,128)(2,1)S(1)} %collective-permute-done.7.refs_8_), channel_id=1, source_target_pairs={{0,2},{1,3},{2,0},{3,1},{4,6},{5,7},{6,4},{7,5},{8,10},{9,11},{10,... | collective-permute-start | bytes 786440 | tf_op jit(solution)/shard_map/ppermute | solution.py:198
  20.3 4.0 %collective-permute-done.5.refs_6_ = bf16[8,64,256]{2,1,0:T(8,128)(2,1)S(1)} collective-permute-done((bf16[8,64,256]{2,1,0:T(8,128)(2,1)S(1)}, bf16[8,64,256]{2,1,0:T(8,128)(2,1)S(1)}, u32[]{:S(2)}, u32[]{:S(2)}) %collective-permute-start.5) | collective-permute-done | bytes 262176 | tf_op jit(solution)/shard_map/ppermute | solution.py:198
  24.3 5.2 %collective-permute-done.9.refs_10_ = bf16[8,64,256]{2,1,0:T(8,128)(2,1)S(1)} collective-permute-done((bf16[8,64,256]{2,1,0:T(8,128)(2,1)S(1)}, bf16[8,64,256]{2,1,0:T(8,128)(2,1)S(1)}, u32[]{:S(2)}, u32[]{:S(2)}) %collective-permute-start.9) | collective-permute-done | bytes 262176 | tf_op jit(solution)/shard_map/ppermute | solution.py:198
  29.6 1.5 %collective-permute-done.10.refs_11_ = bf16[8,64,256]{2,1,0:T(8,128)(2,1)S(1)} collective-permute-done((bf16[8,64,256]{2,1,0:T(8,128)(2,1)S(1)}, bf16[8,64,256]{2,1,0:T(8,128)(2,1)S(1)}, u32[]{:S(2)}, u32[]{:S(2)}) %collective-permute-start.10) | collective-permute-done | bytes 262176 | tf_op jit(solution)/shard_map/ppermute | solution.py:198
  31.1 3.7 %shard_map.86 = (bf16[2,8,64,256]{3,2,1,0:T(8,128)(2,1)S(1)}, bf16[4,8,64,256]{3,2,1,0:T(8,128)(2,1)S(1)}, bf16[2,8,64,256]{3,2,1,0:T(8,128)(2,1)S(1)}, bf16[4,8...) custom-call(bf16[8,64,256]{2,1,0:T(8,128)(2,1)S(1)} %bitcast.19, ...), custom_call_target="tpu_custom_call" | custom-call | flops 1342177280 | bytes 10223872 | tf_op jit(solution)/shard_map/pallas_call | solution.py:25
  35.5 1.3 %collective-permute-done.11 = bf16[2,8,64,256]{3,2,1,0:T(8,128)(2,1)S(1)} collective-permute-done((bf16[2,8,64,256]{3,2,1,0:T(8,128)(2,1)S(1)}, bf16[2,8,64,256]{3,2,1,0:T(8,128)(2,1)S(1)}, u32[]{:S(2)}, u32[]{:S(2)}) %collective-permute-start.11) | collective-permute-done | bytes 524320 | tf_op jit(solution)/shard_map/ppermute | solution.py:198
  38.2 1.7 %collective-permute-start.14 = (bf16[128,256]{1,0:T(8,128)(2,1)S(1)}, bf16[128,256]{1,0:T(8,128)(2,1)S(1)}, u32[]{:S(2)}, u32[]{:S(2)}) collective-permute-start(bf16[128,256]{1,0:T(8,128)(2,1)S(1)} %convert_element_type.86), channel_id=1, source_target_pairs={{0,16},{16,0},{1,17},{17,1},{2,18},{18,2},{3,19},{19,3},{4,20},{20... | collective-permute-start | bytes 196616 | tf_op jit(solution)/shard_map/ppermute | solution.py:198
  39.9 2.6 %collective-permute-done.14.b_ref = bf16[128,256]{1,0:T(8,128)(2,1)S(1)} collective-permute-done((bf16[128,256]{1,0:T(8,128)(2,1)S(1)}, bf16[128,256]{1,0:T(8,128)(2,1)S(1)}, u32[]{:S(2)}, u32[]{:S(2)}) %collective-permute-start.14) | collective-permute-done | bytes 65568 | tf_op jit(solution)/shard_map/ppermute | solution.py:198
  42.6 5.0 %collective-permute-done.15.b_ref = f32[128,256]{1,0:T(8,128)S(1)} collective-permute-done((f32[128,256]{1,0:T(8,128)S(1)}, f32[128,256]{1,0:T(8,128)S(1)}, u32[]{:S(2)}, u32[]{:S(2)}) %collective-permute-start.15) | collective-permute-done | bytes 131104 | tf_op jit(solution)/shard_map/ppermute | solution.py:198
  47.6 1.1 %collective-permute-start.16 = (bf16[128,256]{1,0:T(8,128)(2,1)S(1)}, bf16[128,256]{1,0:T(8,128)(2,1)S(1)}, u32[]{:S(2)}, u32[]{:S(2)}) collective-permute-start(bf16[128,256]{1,0:T(8,128)(2,1)S(1)} %shard_map.89.a_ref), channel_id=1, source_target_pairs={{0,8},{4,12},{8,0},{12,4},{1,9},{5,13},{9,1},{13,5},{2,10},{6,14},... | collective-permute-start | bytes 196616 | tf_op jit(solution)/shard_map/ppermute | solution.py:198
  48.6 4.3 %collective-permute-done.16.b_ref = bf16[128,256]{1,0:T(8,128)(2,1)S(1)} collective-permute-done((bf16[128,256]{1,0:T(8,128)(2,1)S(1)}, bf16[128,256]{1,0:T(8,128)(2,1)S(1)}, u32[]{:S(2)}, u32[]{:S(2)}) %collective-permute-start.16) | collective-permute-done | bytes 65568 | tf_op jit(solution)/shard_map/ppermute | solution.py:198
  53.0 1.6 %fusion.3 = (bf16[8,64,256]{2,1,0:T(8,128)(2,1)S(1)}, bf16[8,64,256]{2,1,0:T(8,128)(2,1)S(1)}, bf16[8,64,256]{2,1,0:T(8,128)(2,1)S(1)}) fusion(bf16[2,8,64,256]{3,2,1,0:T(8,128)(2,1)} %collective-permute-done.13, bf16[4,8,64,256]{3,2,1,0:T(8,128)(2,1)} %collective-permute-done.17, bf16[4,8,64,256]{3,2,1,0:T(8,128)(2,1)S(1)} %get-tuple-element.40), kind=kLoop, calls=%fused_computation.9 | loop fusion | flops 2097152 | bytes 2883584 | tf_op jit(solution)/shard_map/convert_element_type | solution.py:319
  54.6 1.7 %collective-permute-start.21 = (bf16[8,64,256]{2,1,0:T(8,128)(2,1)S(1)}, bf16[8,64,256]{2,1,0:T(8,128)(2,1)S(1)}, u32[]{:S(2)}, u32[]{:S(2)}) collective-permute-start(bf16[8,64,256]{2,1,0:T(8,128)(2,1)S(1)} %get-tuple-element.47), channel_id=1, source_target_pairs={{0,2},{1,3},{2,0},{3,1},{4,6},{5,7},{6,4},{7,5},{8,10},{9,11},{10,... | collective-permute-start | bytes 786440 | tf_op jit(solution)/shard_map/ppermute | solution.py:198
  56.7 2.5 %collective-permute-start.22 = (bf16[8,64,256]{2,1,0:T(8,128)(2,1)S(1)}, bf16[8,64,256]{2,1,0:T(8,128)(2,1)S(1)}, u32[]{:S(2)}, u32[]{:S(2)}) collective-permute-start(bf16[8,64,256]{2,1,0:T(8,128)(2,1)S(1)} %get-tuple-element.46), channel_id=1, source_target_pairs={{4,0},{8,4},{12,8},{0,12},{5,1},{9,5},{13,9},{1,13},{6,2},{10,6},{... | collective-permute-start | bytes 786440 | tf_op jit(solution)/shard_map/ppermute | solution.py:212
  59.2 4.9 %collective-permute-done.18.b_ref = f32[128,256]{1,0:T(8,128)S(1)} collective-permute-done((f32[128,256]{1,0:T(8,128)S(1)}, f32[128,256]{1,0:T(8,128)S(1)}, u32[]{:S(2)}, u32[]{:S(2)}) %collective-permute-start.18) | collective-permute-done | bytes 131104 | tf_op jit(solution)/shard_map/ppermute | solution.py:198
  64.0 1.6 %collective-permute-start.19 = (f32[128,256]{1,0:T(8,128)S(1)}, f32[128,256]{1,0:T(8,128)S(1)}, u32[]{:S(2)}, u32[]{:S(2)}) collective-permute-start(f32[128,256]{1,0:T(8,128)S(1)} %shard_map.91.refs_0_), channel_id=1, source_target_pairs={{0,16},{16,0},{1,17},{17,1},{2,18},{18,2},{3,19},{19,3},{4,20},{20... | collective-permute-start | bytes 393224 | tf_op jit(solution)/shard_map/ppermute | solution.py:198
  65.6 1.1 %fusion = f32[8,64,256]{2,1,0:T(8,128)S(1)} fusion(f32[8,64,256]{2,1,0:T(8,128)S(1)} %bitcast.20, bf16[8,64,256]{2,1,0:T(8,128)(2,1)S(1)} %collective-permute-done.21, bf16[4,8,64,256]{3,2,1,0:T(8,128)(2,1)} %collective-permute-done.17, bf16[4,8,64,256]{3,2,1,0:T(8,128)(2,1)S(1)} %get-tuple-element.40), kind=kLoop, calls=%fused_computation.2 | loop fusion | flops 786432 | bytes 1835008 | tf_op jit(solution)/shard_map/add | solution.py:328
  66.7 2.4 %collective-permute-done.19.refs_1_ = f32[128,256]{1,0:T(8,128)S(1)} collective-permute-done((f32[128,256]{1,0:T(8,128)S(1)}, f32[128,256]{1,0:T(8,128)S(1)}, u32[]{:S(2)}, u32[]{:S(2)}) %collective-permute-start.19) | collective-permute-done | bytes 131104 | tf_op jit(solution)/shard_map/ppermute | solution.py:198
  (49 shorter events, 9.9 us)
Async XLA Ops:
  1.7 13.4 %collective-permute-start.3 = (bf16[8,64,256]{2,1,0:T(8,128)(2,1)S(1)}, bf16[8,64,256]{2,1,0:T(8,128)(2,1)S(1)}, u32[]{:S(2)}, u32[]{:S(2)}) collective-permute-start(bf16[8,64,256]{2,1,0:T(8,128)(2,1)S(1)} %bitcast.15), channel_id=1, source_target_pairs={{0,4},{4,8},{8,12},{12,0},{1,5},{5,9},{9,13},{13,1},{2,6},{6,10},{... | collective-permute-start | bytes 786440 | tf_op jit(solution)/shard_map/ppermute | solution.py:208
  4.8 13.4 %collective-permute-start.7 = (bf16[8,64,256]{2,1,0:T(8,128)(2,1)S(1)}, bf16[8,64,256]{2,1,0:T(8,128)(2,1)S(1)}, u32[]{:S(2)}, u32[]{:S(2)}) collective-permute-start(bf16[8,64,256]{2,1,0:T(8,128)(2,1)S(1)} %bitcast.16), channel_id=1, source_target_pairs={{4,0},{8,4},{12,8},{0,12},{5,1},{9,5},{13,9},{1,13},{6,2},{10,6},{... | collective-permute-start | bytes 786440 | tf_op jit(solution)/shard_map/ppermute | solution.py:212
  6.9 12.8 %collective-permute-start.1 = (bf16[8,64,256]{2,1,0:T(8,128)(2,1)S(1)}, bf16[8,64,256]{2,1,0:T(8,128)(2,1)S(1)}, u32[]{:S(2)}, u32[]{:S(2)}) collective-permute-start(bf16[8,64,256]{2,1,0:T(8,128)(2,1)S(1)} %bitcast.17), channel_id=1, source_target_pairs={{0,2},{1,3},{2,0},{3,1},{4,6},{5,7},{6,4},{7,5},{8,10},{9,11},{10,... | collective-permute-start | bytes 786440 | tf_op jit(solution)/shard_map/ppermute | solution.py:198
  8.6 11.7 %collective-permute-start = (bf16[8,64,256]{2,1,0:T(8,128)(2,1)S(1)}, bf16[8,64,256]{2,1,0:T(8,128)(2,1)S(1)}, u32[]{:S(2)}, u32[]{:S(2)}) collective-permute-start(bf16[8,64,256]{2,1,0:T(8,128)(2,1)S(1)} %bitcast.18), channel_id=1, source_target_pairs={{0,1},{1,0},{2,3},{3,2},{4,5},{5,4},{6,7},{7,6},{8,9},{9,8},{10,11... | collective-permute-start | bytes 786440 | tf_op jit(solution)/shard_map/ppermute | solution.py:198
  15.1 9.2 %collective-permute-start.5 = (bf16[8,64,256]{2,1,0:T(8,128)(2,1)S(1)}, bf16[8,64,256]{2,1,0:T(8,128)(2,1)S(1)}, u32[]{:S(2)}, u32[]{:S(2)}) collective-permute-start(bf16[8,64,256]{2,1,0:T(8,128)(2,1)S(1)} %collective-permute-done.3.refs_4_), channel_id=1, source_target_pairs={{0,2},{1,3},{2,0},{3,1},{4,6},{5,7},{6,4},{7,5},{8,10},{9,11},{10,... | collective-permute-start | bytes 786440 | tf_op jit(solution)/shard_map/ppermute | solution.py:198
  18.2 11.4 %collective-permute-start.9 = (bf16[8,64,256]{2,1,0:T(8,128)(2,1)S(1)}, bf16[8,64,256]{2,1,0:T(8,128)(2,1)S(1)}, u32[]{:S(2)}, u32[]{:S(2)}) collective-permute-start(bf16[8,64,256]{2,1,0:T(8,128)(2,1)S(1)} %collective-permute-done.7.refs_8_), channel_id=1, source_target_pairs={{0,2},{1,3},{2,0},{3,1},{4,6},{5,7},{6,4},{7,5},{8,10},{9,11},{10,... | collective-permute-start | bytes 786440 | tf_op jit(solution)/shard_map/ppermute | solution.py:198
  19.7 9.9 %collective-permute-start.4 = (bf16[8,64,256]{2,1,0:T(8,128)(2,1)S(1)}, bf16[8,64,256]{2,1,0:T(8,128)(2,1)S(1)}, u32[]{:S(2)}, u32[]{:S(2)}) collective-permute-start(bf16[8,64,256]{2,1,0:T(8,128)(2,1)S(1)} %collective-permute-done.3.refs_4_), channel_id=1, source_target_pairs={{0,1},{1,0},{2,3},{3,2},{4,5},{5,4},{6,7},{7,6},{8,9},{9,8},{10,11... | collective-permute-start | bytes 786440 | tf_op jit(solution)/shard_map/ppermute | solution.py:198
  19.7 9.9 %collective-permute-start.2 = (bf16[8,64,256]{2,1,0:T(8,128)(2,1)S(1)}, bf16[8,64,256]{2,1,0:T(8,128)(2,1)S(1)}, u32[]{:S(2)}, u32[]{:S(2)}) collective-permute-start(bf16[8,64,256]{2,1,0:T(8,128)(2,1)S(1)} %collective-permute-done.1.refs_2_), channel_id=1, source_target_pairs={{0,1},{1,0},{2,3},{3,2},{4,5},{5,4},{6,7},{7,6},{8,9},{9,8},{10,11... | collective-permute-start | bytes 786440 | tf_op jit(solution)/shard_map/ppermute | solution.py:198
  20.2 9.3 %collective-permute-start.8 = (bf16[8,64,256]{2,1,0:T(8,128)(2,1)S(1)}, bf16[8,64,256]{2,1,0:T(8,128)(2,1)S(1)}, u32[]{:S(2)}, u32[]{:S(2)}) collective-permute-start(bf16[8,64,256]{2,1,0:T(8,128)(2,1)S(1)} %collective-permute-done.7.refs_8_), channel_id=1, source_target_pairs={{0,1},{1,0},{2,3},{3,2},{4,5},{5,4},{6,7},{7,6},{8,9},{9,8},{10,11... | collective-permute-start | bytes 786440 | tf_op jit(solution)/shard_map/ppermute | solution.py:198
  24.3 5.3 %collective-permute-start.6 = (bf16[8,64,256]{2,1,0:T(8,128)(2,1)S(1)}, bf16[8,64,256]{2,1,0:T(8,128)(2,1)S(1)}, u32[]{:S(2)}, u32[]{:S(2)}) collective-permute-start(bf16[8,64,256]{2,1,0:T(8,128)(2,1)S(1)} %collective-permute-done.5.refs_6_), channel_id=1, source_target_pairs={{0,1},{1,0},{2,3},{3,2},{4,5},{5,4},{6,7},{7,6},{8,9},{9,8},{10,11... | collective-permute-start | bytes 786440 | tf_op jit(solution)/shard_map/ppermute | solution.py:198
  29.5 1.5 %collective-permute-start.10 = (bf16[8,64,256]{2,1,0:T(8,128)(2,1)S(1)}, bf16[8,64,256]{2,1,0:T(8,128)(2,1)S(1)}, u32[]{:S(2)}, u32[]{:S(2)}) collective-permute-start(bf16[8,64,256]{2,1,0:T(8,128)(2,1)S(1)} %collective-permute-done.9.refs_10_), channel_id=1, source_target_pairs={{0,1},{1,0},{2,3},{3,2},{4,5},{5,4},{6,7},{7,6},{8,9},{9,8},{10,11... | collective-permute-start | bytes 786440 | tf_op jit(solution)/shard_map/ppermute | solution.py:198
  34.8 2.0 %collective-permute-start.11 = (bf16[2,8,64,256]{3,2,1,0:T(8,128)(2,1)S(1)}, bf16[2,8,64,256]{3,2,1,0:T(8,128)(2,1)S(1)}, u32[]{:S(2)}, u32[]{:S(2)}) collective-permute-start(bf16[2,8,64,256]{3,2,1,0:T(8,128)(2,1)S(1)} %get-tuple-element.30), channel_id=1, source_target_pairs={{0,1},{1,0},{2,3},{3,2},{4,5},{5,4},{6,7},{7,6},{8,9},{9,8},{10,11... | collective-permute-start | bytes 1572872 | tf_op jit(solution)/shard_map/ppermute | solution.py:198
  35.0 18.0 %collective-permute-start.17 = (bf16[4,8,64,256]{3,2,1,0:T(8,128)(2,1)S(1)}, bf16[4,8,64,256]{3,2,1,0:T(8,128)(2,1)}, u32[]{:S(2)}, u32[]{:S(2)}) collective-permute-start(bf16[4,8,64,256]{3,2,1,0:T(8,128)(2,1)S(1)} %get-tuple-element.37), channel_id=1, source_target_pairs={{0,1},{1,0},{2,3},{3,2},{4,5},{5,4},{6,7},{7,6},{8,9},{9,8},{10,11... | collective-permute-start | bytes 3145736 | tf_op jit(solution)/shard_map/ppermute | solution.py:198
  35.4 2.4 %collective-permute-start.12 = (f32[256,256]{1,0:T(8,128)S(1)}, f32[256,256]{1,0:T(8,128)S(1)}, u32[]{:S(2)}, u32[]{:S(2)}) collective-permute-start(f32[256,256]{1,0:T(8,128)S(1)} %get-tuple-element.31), channel_id=1, source_target_pairs={{0,1},{1,0},{2,3},{3,2},{4,5},{5,4},{6,7},{7,6},{8,9},{9,8},{10,11... | collective-permute-start | bytes 786440 | tf_op jit(solution)/shard_map/ppermute | solution.py:198
  37.7 15.2 %collective-permute-start.13 = (bf16[2,8,64,256]{3,2,1,0:T(8,128)(2,1)}, bf16[2,8,64,256]{3,2,1,0:T(8,128)(2,1)}, u32[]{:S(2)}, u32[]{:S(2)}) collective-permute-start(bf16[2,8,64,256]{3,2,1,0:T(8,128)(2,1)} %add_convert_fusion), channel_id=1, source_target_pairs={{0,2},{1,3},{2,0},{3,1},{4,6},{5,7},{6,4},{7,5},{8,10},{9,11},{10,... | collective-permute-start | bytes 1572872 | tf_op jit(solution)/shard_map/ppermute | solution.py:198
  38.2 4.3 %collective-permute-start.14 = (bf16[128,256]{1,0:T(8,128)(2,1)S(1)}, bf16[128,256]{1,0:T(8,128)(2,1)S(1)}, u32[]{:S(2)}, u32[]{:S(2)}) collective-permute-start(bf16[128,256]{1,0:T(8,128)(2,1)S(1)} %convert_element_type.86), channel_id=1, source_target_pairs={{0,16},{16,0},{1,17},{17,1},{2,18},{18,2},{3,19},{19,3},{4,20},{20... | collective-permute-start | bytes 196616 | tf_op jit(solution)/shard_map/ppermute | solution.py:198
  42.5 5.0 %collective-permute-start.15 = (f32[128,256]{1,0:T(8,128)S(1)}, f32[128,256]{1,0:T(8,128)S(1)}, u32[]{:S(2)}, u32[]{:S(2)}) collective-permute-start(f32[128,256]{1,0:T(8,128)S(1)} %shard_map.88.a_ref), channel_id=1, source_target_pairs={{0,4},{4,0},{8,12},{12,8},{1,5},{5,1},{9,13},{13,9},{2,6},{6,2},{1... | collective-permute-start | bytes 393224 | tf_op jit(solution)/shard_map/ppermute | solution.py:198
  47.6 5.4 %collective-permute-start.16 = (bf16[128,256]{1,0:T(8,128)(2,1)S(1)}, bf16[128,256]{1,0:T(8,128)(2,1)S(1)}, u32[]{:S(2)}, u32[]{:S(2)}) collective-permute-start(bf16[128,256]{1,0:T(8,128)(2,1)S(1)} %shard_map.89.a_ref), channel_id=1, source_target_pairs={{0,8},{4,12},{8,0},{12,4},{1,9},{5,13},{9,1},{13,5},{2,10},{6,14},... | collective-permute-start | bytes 196616 | tf_op jit(solution)/shard_map/ppermute | solution.py:198
  54.6 11.0 %collective-permute-start.21 = (bf16[8,64,256]{2,1,0:T(8,128)(2,1)S(1)}, bf16[8,64,256]{2,1,0:T(8,128)(2,1)S(1)}, u32[]{:S(2)}, u32[]{:S(2)}) collective-permute-start(bf16[8,64,256]{2,1,0:T(8,128)(2,1)S(1)} %get-tuple-element.47), channel_id=1, source_target_pairs={{0,2},{1,3},{2,0},{3,1},{4,6},{5,7},{6,4},{7,5},{8,10},{9,11},{10,... | collective-permute-start | bytes 786440 | tf_op jit(solution)/shard_map/ppermute | solution.py:198
  56.3 7.7 %collective-permute-start.18 = (f32[128,256]{1,0:T(8,128)S(1)}, f32[128,256]{1,0:T(8,128)S(1)}, u32[]{:S(2)}, u32[]{:S(2)}) collective-permute-start(f32[128,256]{1,0:T(8,128)S(1)} %shard_map.90.a_ref), channel_id=1, source_target_pairs={{0,2},{1,3},{2,0},{3,1},{4,6},{5,7},{6,4},{7,5},{8,10},{9,11},{10,... | collective-permute-start | bytes 393224 | tf_op jit(solution)/shard_map/ppermute | solution.py:198
  56.7 10.0 %collective-permute-start.22 = (bf16[8,64,256]{2,1,0:T(8,128)(2,1)S(1)}, bf16[8,64,256]{2,1,0:T(8,128)(2,1)S(1)}, u32[]{:S(2)}, u32[]{:S(2)}) collective-permute-start(bf16[8,64,256]{2,1,0:T(8,128)(2,1)S(1)} %get-tuple-element.46), channel_id=1, source_target_pairs={{4,0},{8,4},{12,8},{0,12},{5,1},{9,5},{13,9},{1,13},{6,2},{10,6},{... | collective-permute-start | bytes 786440 | tf_op jit(solution)/shard_map/ppermute | solution.py:212
  59.2 10.0 %collective-permute-start.23 = (bf16[8,64,256]{2,1,0:T(8,128)(2,1)S(1)}, bf16[8,64,256]{2,1,0:T(8,128)(2,1)S(1)}, u32[]{:S(2)}, u32[]{:S(2)}) collective-permute-start(bf16[8,64,256]{2,1,0:T(8,128)(2,1)S(1)} %get-tuple-element.45), channel_id=1, source_target_pairs={{0,4},{4,8},{8,12},{12,0},{1,5},{5,9},{9,13},{13,1},{2,6},{6,10},{... | collective-permute-start | bytes 786440 | tf_op jit(solution)/shard_map/ppermute | solution.py:208
  64.0 5.0 %collective-permute-start.19 = (f32[128,256]{1,0:T(8,128)S(1)}, f32[128,256]{1,0:T(8,128)S(1)}, u32[]{:S(2)}, u32[]{:S(2)}) collective-permute-start(f32[128,256]{1,0:T(8,128)S(1)} %shard_map.91.refs_0_), channel_id=1, source_target_pairs={{0,16},{16,0},{1,17},{17,1},{2,18},{18,2},{3,19},{19,3},{4,20},{20... | collective-permute-start | bytes 393224 | tf_op jit(solution)/shard_map/ppermute | solution.py:198
  69.1 1.6 %collective-permute-start.20 = (f32[256,256]{1,0:T(8,128)S(1)}, f32[256,256]{1,0:T(8,128)S(1)}, u32[]{:S(2)}, u32[]{:S(2)}) collective-permute-start(f32[256,256]{1,0:T(8,128)S(1)} %shard_map.92), channel_id=1, source_target_pairs={{0,1},{1,0},{2,3},{3,2},{4,5},{5,4},{6,7},{7,6},{8,9},{9,8},{10,11... | collective-permute-start | bytes 786440 | tf_op jit(solution)/shard_map/ppermute | solution.py:198
  (5 other events, 34.1 us)
